TPU v7x, 128 devices: a whole 4x4x4 slice. The times are simulated.
128 devices in a mesh: src: 64 (over y, z_hi, x, core), hi: 2 (over z_lo).
Axes of the slice: x: 4, y: 4, z: 4 (z_hi: 2, z_lo: 2; z = z_hi * 2 + z_lo), core: 2. Of those that a mesh axis runs over, the one named last changes fastest.
Arguments:
- traces: bfloat16 [64, 64, 2, 64, 128], P(None, None, 'hi', 'src'), may hold values from -6 to 6
- observed: bfloat16 [64, 2, 64, 64, 128], P(None, 'hi', 'src'), may hold values from -6 to 6
- leaf_maps: bfloat16 [64, 2, 64, 64, 128], P(None, 'hi', 'src'), may hold values from -0.5 to 0.5
- level_maps: bfloat16 [13, 64, 2, 64, 64, 128], P(None, None, 'hi', 'src'), may hold values from -0.5 to 0.5
- final_maps: bfloat16 [2, 64, 64, 64, 128], P('hi', 'src'), may hold values from -0.75 to 0.75
Outputs:
- residual: bfloat16 [64, 2, 64, 64, 128], P(None, 'hi', 'src')
- gradient: bfloat16 [64, 64, 2, 64, 128], P(None, None, 'hi', 'src')
All inputs are finite; a program needn't handle non-finite values.
Results may differ from a plain program's by a relative error of at most 0.035.
Values may be sent and summed in bfloat16 or wider, within the bound.
No kernel may reach another device: no remote copies, remote signals or barrier semaphores. Data moves between devices by JAX's collectives and lax.ppermute only.
A program may use at most 128 MiB of HBM per device.

v0:
```python
import functools

import jax
import jax.numpy as jnp
from jax import lax
from jax.experimental import pallas as pl
from jax.experimental.pallas import tpu as pltpu
from jax.sharding import PartitionSpec as P

CHUNKS = 2
LANES = 128
BF = jnp.bfloat16
F32 = jnp.float32


def reverse_bits(value, bits):
    return int(format(value, f"0{bits}b")[::-1], 2)


def lane_block(shape, width):
    return lax.broadcasted_iota(jnp.int32, shape, len(shape) - 1) // width


def pick_lanes(product, rows, count, width):
    block = lane_block((rows, LANES), width)
    out = product[:rows]
    for b in range(1, count):
        out = jnp.where(block == b, product[b * rows:(b + 1) * rows], out)
    return out


def split_rows(pair):
    left = lane_block(pair.shape, LANES // 2) == 0
    zero = jnp.zeros(pair.shape, pair.dtype)
    return jnp.concatenate([jnp.where(left, pair, zero), jnp.where(left, zero, pair)], axis=0)


def halves_of(product, rows):
    first, second = product[:rows], product[rows:]
    left = lane_block((rows, LANES), LANES // 2) == 0
    low = jnp.where(left, first, pltpu.roll(second, LANES // 2, 1))
    high = jnp.where(left, pltpu.roll(first, LANES // 2, 1), second)
    return low, high


def is_high(level, src_bits):
    if level < src_bits:
        return (lax.axis_index("src") >> level & 1) == 1
    return (lax.axis_index("hi") >> (level - src_bits) & 1) == 1


def shear_x(device):
    return device ^ reverse_bits(device >> 4 & 3, 2) << 1


def shear_y(device):
    return device ^ reverse_bits(device >> 1 & 3, 2) << 4


def swap_ends(device):
    return device & 62 | device >> 6 | (device & 1) << 6


def first_hop(device):
    return shear_y(device)


def second_hop(device):
    return swap_ends(shear_y(shear_x(device)))


def dot(a, b):
    return jnp.dot(a, b, preferred_element_type=F32)


def dot_nt(a, b):
    return lax.dot_general(a, b, (((1,), (1,)), ((), ())), preferred_element_type=F32)


def leaf_kernel(chunk, traces, leaf, token, out, held, mats, sems, wide):
    vectors, boxes, points = held.shape
    lane_boxes = LANES // vectors
    rank = mats.shape[1]
    copies = [
        pltpu.make_async_copy(traces.at[pl.ds(chunk * vectors, vectors)], held, sems.at[0]),
        pltpu.make_async_copy(leaf, mats, sems.at[1]),
    ]
    for copy in copies:
        copy.start()
    copies[0].wait()
    wide[...] = held[...].astype(F32).reshape(wide.shape)
    copies[1].wait()
    for g in range(boxes // lane_boxes):
        rows = [
            wide[pl.ds(g * lane_boxes + b, vectors, stride=boxes), :] for b in range(lane_boxes)
        ]
        stacked = jnp.concatenate(rows, axis=0).astype(BF)
        group = mats[pl.ds(g * lane_boxes, lane_boxes)].reshape(lane_boxes * rank, points)
        out[g] = pick_lanes(dot_nt(group, stacked), rank, lane_boxes, vectors).astype(BF)


def forward_group(weights, stacked, lane_boxes, rank):
    mats = weights.reshape(lane_boxes * rank, LANES)
    return pick_lanes(dot(mats, stacked), rank, lane_boxes, LANES // lane_boxes).astype(BF)


def cross_step(own, other, mats, out, high, lane_boxes):
    groups, rank = own.shape[0], own.shape[1]
    for g in range(groups):
        mine, theirs = own[g], other[g]
        take = jnp.broadcast_to(high, mine.shape)
        lower = jnp.where(take, theirs, mine)
        upper = jnp.where(take, mine, theirs)
        stacked = jnp.concatenate([lower, upper], axis=0)
        weights = mats[pl.ds(g * lane_boxes, lane_boxes)]
        out[g] = forward_group(weights, stacked, lane_boxes, rank)


def cross_kernel(level, src_bits, lane_boxes, own, other, maps, *refs):
    mats = maps.at[level if maps.shape[0] > 1 else 0]
    cross_step(own, other, mats, refs[-1], is_high(level, src_bits), lane_boxes)


def local_forward(lane_boxes, maps, first, out, work):
    groups, rank = out.shape[0], out.shape[1]
    lane_bits = lane_boxes.bit_length() - 1
    box_bits = maps.shape[1].bit_length() - 1
    for bit in range(box_bits):
        mats = maps.at[first + bit]
        source = work.at[bit % 2]
        target = out if bit == box_bits - 1 else work.at[(bit + 1) % 2]
        if bit < lane_bits:
            shift = LANES // lane_boxes << bit
            for g in range(groups):
                value = source[g].astype(F32)
                is_set = (lane_block(value.shape, shift) & 1) == 1
                lower = jnp.where(is_set, pltpu.roll(value, shift, 1), value)
                upper = jnp.where(is_set, value, pltpu.roll(value, LANES - shift, 1))
                stacked = jnp.concatenate([lower, upper], axis=0).astype(BF)
                weights = mats[pl.ds(g * lane_boxes, lane_boxes)]
                target[g] = forward_group(weights, stacked, lane_boxes, rank)
        else:
            inner = 1 << bit - lane_bits
            for g0 in range(groups):
                if g0 & inner:
                    continue
                stacked = jnp.concatenate([source[g0], source[g0 + inner]], axis=0)
                for g in (g0, g0 + inner):
                    weights = mats[pl.ds(g * lane_boxes, lane_boxes)]
                    target[g] = forward_group(weights, stacked, lane_boxes, rank)


def target_kernel(chunk, coeffs, final, observed, token, *refs):
    residual, adjoint, held, sems, wide, result = refs[-6:]
    groups, rank = coeffs.shape[0], coeffs.shape[1]
    vectors, boxes, points = held.shape
    box_bits = boxes.bit_length() - 1
    lane_boxes = LANES // vectors
    own_rows = pl.ds(chunk * vectors, vectors)
    fetch = pltpu.make_async_copy(observed.at[own_rows], held, sems.at[0])
    fetch.start()
    fetch.wait()
    wide[...] = held[...].astype(F32).reshape(wide.shape)
    for g in range(groups):
        turned = jnp.transpose(coeffs[g].astype(F32)).astype(BF)
        for pair in range(lane_boxes // 2):
            kept, mats = [], []
            for b in (2 * pair, 2 * pair + 1):
                t = reverse_bits(g * lane_boxes + b, box_bits)
                mat = final[t]
                rows = pl.ds(t, vectors, stride=boxes)
                value = dot(turned[b * vectors:(b + 1) * vectors], mat) - wide[rows, :]
                result[rows, :] = value
                kept.append(value)
                mats.append(mat)
            rows = jnp.concatenate(kept, axis=0).astype(BF)
            product = dot_nt(rows, jnp.concatenate(mats, axis=0))
            adjoint[g * lane_boxes // 2 + pair] = pick_lanes(product, vectors, 2, rank).astype(BF)
    held[...] = result[...].reshape(held.shape).astype(BF)
    store = pltpu.make_async_copy(held, residual.at[own_rows], sems.at[1])
    store.start()
    store.wait()


def adjoint_cross_pair(value, mats, kept, sent, p, high):
    rows = value.shape[0]
    low, upper = halves_of(dot(split_rows(value), mats), rows)
    take = jnp.broadcast_to(high, low.shape)
    kept[p] = jnp.where(take, upper, low)
    sent[p] = jnp.where(take, low, upper).astype(BF)


def pair_rows(mats, p):
    rank = mats.shape[1]
    return mats[pl.ds(2 * p, 2)].reshape(2 * rank, LANES)


def local_forward_kernel(level, src_bits, lane_boxes, own, other, maps, token, coeffs, work):
    high = is_high(level, src_bits)
    cross_step(own, other, maps.at[level], work.at[0], high, lane_boxes)
    local_forward(lane_boxes, maps, level + 1, coeffs, work)


def local_adjoint_kernel(level, src_bits, adjoint, maps, token, kept, sent, work):
    pairs, vectors = work.shape[1], work.shape[2]
    box_bits = maps.shape[1].bit_length() - 1
    for step, bit in enumerate(reversed(range(box_bits))):
        mats = maps.at[level + 1 + bit]
        source = work.at[step % 2] if step else adjoint
        target = work.at[(step + 1) % 2]
        if bit == 0:
            for p in range(pairs):
                target[p] = dot(source[p], pair_rows(mats, p)).astype(BF)
        else:
            inner = 1 << bit - 1
            for p0 in range(pairs):
                if p0 & inner:
                    continue
                p1 = p0 + inner
                rows = jnp.concatenate([split_rows(source[p0]), split_rows(source[p1])], axis=1)
                stacked = jnp.concatenate([pair_rows(mats, p0), pair_rows(mats, p1)], axis=0)
                low, upper = halves_of(dot(rows, stacked), vectors)
                target[p0] = low.astype(BF)
                target[p1] = upper.astype(BF)
    source = work.at[box_bits % 2]
    high = is_high(level, src_bits)
    for p in range(pairs):
        adjoint_cross_pair(source[p], pair_rows(maps.at[level], p), kept, sent, p, high)


def adjoint_cross_kernel(level, src_bits, held_part, received, maps, *refs):
    kept, sent = refs[-2:]
    high = is_high(level, src_bits)
    for p in range(held_part.shape[0]):
        value = (held_part[p] + received[p].astype(F32)).astype(BF)
        adjoint_cross_pair(value, pair_rows(maps.at[level], p), kept, sent, p, high)


def gradient_kernel(chunk, held_part, received, leaf, *refs):
    gradient, held, sems, result = refs[-4:]
    pairs, vectors = held_part.shape[0], held_part.shape[1]
    boxes = leaf.shape[0]
    for p in range(pairs):
        value = (held_part[p] + received[p].astype(F32)).astype(BF)
        product = dot(split_rows(value), pair_rows(leaf, p))
        result[pl.ds(2 * p, vectors, stride=boxes), :] = product[:vectors]
        result[pl.ds(2 * p + 1, vectors, stride=boxes), :] = product[vectors:]
    held[...] = result[...].reshape(held.shape).astype(BF)
    store = pltpu.make_async_copy(
        held, gradient.at[pl.ds(chunk * vectors, vectors)], sems.at[0]
    )
    store.start()
    store.wait()


VMEM = pl.BlockSpec(memory_space=pltpu.VMEM)
ANY = pl.BlockSpec(memory_space=pl.ANY)
HBM = pl.BlockSpec(memory_space=pltpu.HBM)


def call(kernel, out_shape, in_specs, out_specs, scratch, flops, moved, limit, aliases=None):
    return pl.pallas_call(
        kernel,
        out_shape=out_shape,
        in_specs=in_specs,
        out_specs=out_specs,
        scratch_shapes=scratch,
        input_output_aliases=aliases or {},
        compiler_params=pltpu.CompilerParams(vmem_limit_bytes=limit << 20),
        cost_estimate=pl.CostEstimate(flops=flops, bytes_accessed=moved, transcendentals=0),
    )


def body(traces, observed, leaf_maps, level_maps, final_maps):
    total = traces.shape[0]
    boxes, points = traces.shape[1], traces.shape[4]
    rank = leaf_maps.shape[3]
    src_count, hi_count = lax.axis_size("src"), lax.axis_size("hi")
    src_bits = src_count.bit_length() - 1
    hi_bits = hi_count.bit_length() - 1
    device_bits = src_bits + hi_bits
    box_bits = boxes.bit_length() - 1
    vectors = total // CHUNKS
    lane_boxes = LANES // vectors
    groups, pairs = boxes // lane_boxes, boxes // 2

    leaf = leaf_maps.reshape(boxes, rank, points)
    final = final_maps.reshape(boxes, rank, points)
    levels = level_maps.reshape(level_maps.shape[0], boxes, rank, 2 * rank)
    samples = traces.reshape(total, boxes, points)
    wanted = observed.reshape(total, boxes, points)

    def shape(*dims, dtype=BF):
        return jax.ShapeDtypeStruct(dims, dtype)

    forward_shape = shape(groups, rank, LANES)
    pair_shape = shape(pairs, vectors, LANES)
    kept_shape = shape(pairs, vectors, LANES, dtype=F32)
    sample_shape = shape(vectors, boxes, points)
    full_shape = shape(total, boxes, points)
    wide = pltpu.VMEM((vectors * boxes, points), F32)
    held = pltpu.VMEM((vectors, boxes, points), BF)
    sems = pltpu.SemaphoreType.DMA((2,))
    flops = 2 * boxes * rank * 2 * rank * vectors
    moved = boxes * rank * 2 * rank * 2

    def exchange(array, level):
        if level < src_bits:
            axis, count, bit = "src", src_count, level
        else:
            axis, count, bit = "hi", hi_count, level - src_bits
        return lax.ppermute(array, axis, [(i, i ^ 1 << bit) for i in range(count)])

    def move(array, route):
        pairs_of = []
        for src in range(src_count):
            for hi in range(hi_count):
                there = route(hi * src_count + src)
                pairs_of.append(
                    (src * hi_count + hi, there % src_count * hi_count + there // src_count)
                )
        return lax.ppermute(array, ("src", "hi"), pairs_of)

    def reversal(array):
        return move(move(array, first_hop), second_hop)

    for device in range(src_count * hi_count):
        assert second_hop(first_hop(device)) == reverse_bits(device, device_bits)

    def leaf_call(chunk):
        kernel = functools.partial(leaf_kernel, chunk)
        scratch = [held, pltpu.VMEM((boxes, rank, points), BF), sems, wide]
        return call(kernel, forward_shape, [HBM, HBM, ANY], VMEM, scratch, flops, 2 * moved, 8)

    def target_call(chunk, *operands):
        kernel = functools.partial(target_kernel, chunk)
        specs = [VMEM, VMEM, HBM, ANY] + [HBM] * (len(operands) - 4)
        return call(
            kernel, (full_shape, pair_shape), specs, (HBM, VMEM), [held, sems, wide, wide],
            2 * flops, 4 * moved, 8, {4: 0} if len(operands) > 4 else None,
        )(*operands)

    def gradient_call(chunk, *operands):
        kernel = functools.partial(gradient_kernel, chunk)
        specs = [VMEM] * 3 + [HBM] * (len(operands) - 3)
        return call(
            kernel, full_shape, specs, HBM, [held, sems, wide],
            flops, 2 * moved, 8, {3: 0} if len(operands) > 3 else None,
        )(*operands)

    def cross_call(level, *operands):
        kernel = functools.partial(cross_kernel, level, src_bits, lane_boxes)
        specs = [VMEM] * 3 + [ANY] * (len(operands) - 3)
        return call(kernel, forward_shape, specs, VMEM, [], flops, moved, 4)(*operands)

    def adjoint_call(level, *operands):
        kernel = functools.partial(adjoint_cross_kernel, level, src_bits)
        specs = [VMEM] * 3 + [ANY] * (len(operands) - 3)
        return call(
            kernel, (kept_shape, pair_shape), specs, (VMEM, VMEM), [], flops, moved, 4
        )(*operands)

    def local_forward_call(*operands):
        kernel = functools.partial(local_forward_kernel, top, src_bits, lane_boxes)
        scratch = [pltpu.VMEM((2, groups, rank, LANES), BF)]
        return call(
            kernel, forward_shape, [VMEM] * 3 + [ANY], VMEM, scratch, 7 * flops, 7 * moved, 8
        )(*operands)

    def local_adjoint_call(*operands):
        kernel = functools.partial(local_adjoint_kernel, top, src_bits)
        scratch = [pltpu.VMEM((2, pairs, vectors, LANES), BF)]
        return call(
            kernel, (kept_shape, pair_shape), [VMEM] * 2 + [ANY], (VMEM, VMEM), scratch,
            7 * flops, 7 * moved, 8,
        )(*operands)

    top = device_bits - 1
    every = range(CHUNKS)
    coeffs, kept, sent = [None] * CHUNKS, [None] * CHUNKS, [None] * CHUNKS
    token = leaf
    for c in every:
        coeffs[c] = token = leaf_call(c)(samples, leaf, token)
    for level in range(top):
        maps = levels[level:level + 1] if level < 2 else levels
        for c in every:
            coeffs[c] = token = cross_call(
                level, coeffs[c], exchange(coeffs[c], level), maps, token
            )
    for c in every:
        coeffs[c] = token = local_forward_call(
            coeffs[c], exchange(coeffs[c], top), levels, token
        )
    residual = ()
    for c in every:
        *residual, sent[c] = target_call(c, reversal(coeffs[c]), final, wanted, token, *residual)
        token = sent[c]
    for c in every:
        kept[c], sent[c] = local_adjoint_call(reversal(sent[c]), levels, token)
        token = sent[c]
    for level in reversed(range(top)):
        for c in every:
            kept[c], sent[c] = adjoint_call(
                level, kept[c], exchange(sent[c], level + 1), levels, token
            )
            token = sent[c]
    residual = residual[0]
    gradient = ()
    for c in every:
        gradient = [gradient_call(c, kept[c], exchange(sent[c], 0), leaf, *gradient)]
    gradient = gradient[0]
    return (
        residual.reshape(total, 1, 1, boxes, points),
        gradient.reshape(total, boxes, 1, 1, points),
    )


def solution(mesh):
    placed = (
        P(None, None, "hi", "src", None),
        P(None, "hi", "src", None, None),
        P(None, "hi", "src", None, None),
        P(None, None, "hi", "src", None, None),
        P("hi", "src", None, None, None),
    )
    return jax.shard_map(
        body,
        mesh=mesh,
        in_specs=placed,
        out_specs=(P(None, "hi", "src", None, None), P(None, None, "hi", "src", None)),
        check_vma=False,
    )
```

profile of v0, /device:TPU:1, one launch (start us, length us, event | category | flops | bytes accessed | tf_op | source)
XLA Modules:
  0.0 204.5 jit_solution(3316128908458011751)
XLA Ops:
  11.3 5.4 %collective-permute-done.3.other = bf16[16,64,128]{2,1,0:T(8,128)(2,1)S(1)} collective-permute-done((bf16[16,64,128]{2,1,0:T(8,128)(2,1)S(1)}, bf16[16,64,128]{2,1,0:T(8,128)(2,1)S(1)}, u32[]{:S(2)}, u32[]{:S(2)}) %collective-permute-start.3) | collective-permute-done | bytes 262176 | tf_op jit(solution)/shard_map/ppermute | solution.py:312
  17.2 2.9 %collective-permute-start.5 = (bf16[16,64,128]{2,1,0:T(8,128)(2,1)S(1)}, bf16[16,64,128]{2,1,0:T(8,128)(2,1)S(1)}, u32[]{:S(2)}, u32[]{:S(2)}) collective-permute-start(bf16[16,64,128]{2,1,0:T(8,128)(2,1)S(1)} %shard_map.72.refs_0_.own), channel_id=1, source_target_pairs={{0,8},{2,10},{4,12},{6,14},{8,0},{10,2},{12,4},{14,6},{16,24},{18,... | collective-permute-start | bytes 786440 | tf_op jit(solution)/shard_map/ppermute | solution.py:312
  20.1 2.3 %collective-permute-done.2.other = bf16[16,64,128]{2,1,0:T(8,128)(2,1)S(1)} collective-permute-done((bf16[16,64,128]{2,1,0:T(8,128)(2,1)S(1)}, bf16[16,64,128]{2,1,0:T(8,128)(2,1)S(1)}, u32[]{:S(2)}, u32[]{:S(2)}) %collective-permute-start.2) | collective-permute-done | bytes 262176 | tf_op jit(solution)/shard_map/ppermute | solution.py:312
  22.8 2.9 %collective-permute-start.4 = (bf16[16,64,128]{2,1,0:T(8,128)(2,1)S(1)}, bf16[16,64,128]{2,1,0:T(8,128)(2,1)S(1)}, u32[]{:S(2)}, u32[]{:S(2)}) collective-permute-start(bf16[16,64,128]{2,1,0:T(8,128)(2,1)S(1)} %shard_map.73.refs_0_.own), channel_id=1, source_target_pairs={{0,8},{2,10},{4,12},{6,14},{8,0},{10,2},{12,4},{14,6},{16,24},{18,... | collective-permute-start | bytes 786440 | tf_op jit(solution)/shard_map/ppermute | solution.py:312
  25.7 4.5 %collective-permute-done.5.other = bf16[16,64,128]{2,1,0:T(8,128)(2,1)S(1)} collective-permute-done((bf16[16,64,128]{2,1,0:T(8,128)(2,1)S(1)}, bf16[16,64,128]{2,1,0:T(8,128)(2,1)S(1)}, u32[]{:S(2)}, u32[]{:S(2)}) %collective-permute-start.5) | collective-permute-done | bytes 262176 | tf_op jit(solution)/shard_map/ppermute | solution.py:312
  30.7 3.7 %collective-permute-start.7 = (bf16[16,64,128]{2,1,0:T(8,128)(2,1)S(1)}, bf16[16,64,128]{2,1,0:T(8,128)(2,1)S(1)}, u32[]{:S(2)}, u32[]{:S(2)}) collective-permute-start(bf16[16,64,128]{2,1,0:T(8,128)(2,1)S(1)} %shard_map.74.refs_0_.own), channel_id=1, source_target_pairs={{0,16},{2,18},{4,20},{6,22},{8,24},{10,26},{12,28},{14,30},{16,0},... | collective-permute-start | bytes 786440 | tf_op jit(solution)/shard_map/ppermute | solution.py:312
  36.3 3.7 %collective-permute-start.6 = (bf16[16,64,128]{2,1,0:T(8,128)(2,1)S(1)}, bf16[16,64,128]{2,1,0:T(8,128)(2,1)S(1)}, u32[]{:S(2)}, u32[]{:S(2)}) collective-permute-start(bf16[16,64,128]{2,1,0:T(8,128)(2,1)S(1)} %shard_map.75.refs_0_.own), channel_id=1, source_target_pairs={{0,16},{2,18},{4,20},{6,22},{8,24},{10,26},{12,28},{14,30},{16,0},... | collective-permute-start | bytes 786440 | tf_op jit(solution)/shard_map/ppermute | solution.py:312
  41.8 3.5 %collective-permute-done.6.other = bf16[16,64,128]{2,1,0:T(8,128)(2,1)S(1)} collective-permute-done((bf16[16,64,128]{2,1,0:T(8,128)(2,1)S(1)}, bf16[16,64,128]{2,1,0:T(8,128)(2,1)S(1)}, u32[]{:S(2)}, u32[]{:S(2)}) %collective-permute-start.6) | collective-permute-done | bytes 262176 | tf_op jit(solution)/shard_map/ppermute | solution.py:312
  47.5 2.7 %collective-permute-start.11 = (bf16[16,64,128]{2,1,0:T(8,128)(2,1)S(1)}, bf16[16,64,128]{2,1,0:T(8,128)(2,1)S(1)}, u32[]{:S(2)}, u32[]{:S(2)}) collective-permute-start(bf16[16,64,128]{2,1,0:T(8,128)(2,1)S(1)} %shard_map.78.refs_0_.own), channel_id=1, source_target_pairs={{0,64},{2,66},{4,68},{6,70},{8,72},{10,74},{12,76},{14,78},{16,80}... | collective-permute-start | bytes 786440 | tf_op jit(solution)/shard_map/ppermute | solution.py:312
  52.7 3.0 %collective-permute-start.10 = (bf16[16,64,128]{2,1,0:T(8,128)(2,1)S(1)}, bf16[16,64,128]{2,1,0:T(8,128)(2,1)S(1)}, u32[]{:S(2)}, u32[]{:S(2)}) collective-permute-start(bf16[16,64,128]{2,1,0:T(8,128)(2,1)S(1)} %shard_map.79.refs_0_.own), channel_id=1, source_target_pairs={{0,64},{2,66},{4,68},{6,70},{8,72},{10,74},{12,76},{14,78},{16,80}... | collective-permute-start | bytes 786440 | tf_op jit(solution)/shard_map/ppermute | solution.py:312
  55.7 4.6 %collective-permute-done.11.other = bf16[16,64,128]{2,1,0:T(8,128)(2,1)S(1)} collective-permute-done((bf16[16,64,128]{2,1,0:T(8,128)(2,1)S(1)}, bf16[16,64,128]{2,1,0:T(8,128)(2,1)S(1)}, u32[]{:S(2)}, u32[]{:S(2)}) %collective-permute-start.11) | collective-permute-done | bytes 262176 | tf_op jit(solution)/shard_map/ppermute | solution.py:312
  61.3 4.6 %collective-permute-done.10.other = bf16[16,64,128]{2,1,0:T(8,128)(2,1)S(1)} collective-permute-done((bf16[16,64,128]{2,1,0:T(8,128)(2,1)S(1)}, bf16[16,64,128]{2,1,0:T(8,128)(2,1)S(1)}, u32[]{:S(2)}, u32[]{:S(2)}) %collective-permute-start.10) | collective-permute-done | bytes 262176 | tf_op jit(solution)/shard_map/ppermute | solution.py:312
  67.2 2.1 %shard_map.82.token = bf16[16,64,128]{2,1,0:T(8,128)(2,1)S(1)} custom-call(bf16[16,64,128]{2,1,0:T(8,128)(2,1)S(1)} %shard_map.80.refs_0_.own, bf16[16,64,128]{2,1,0:T(8,128)(2,1)S(1)} %collective-permute-done.13.other, bf16[13,64,64,128]{3,2,1,0:T(8,128)(2,1)S(1)} %bitcast.25, bf16[16,64,128]{2,1,0:T(8,128)(2,1)S(1)} %shard_map.81.token.own), custom_call_target="tpu_custom_call" | custom-call | flops 234881024 | bytes 7340032 | tf_op jit(solution)/shard_map/pallas_call | solution.py:366
  70.0 5.0 %collective-permute-done.12.other = bf16[16,64,128]{2,1,0:T(8,128)(2,1)S(1)} collective-permute-done((bf16[16,64,128]{2,1,0:T(8,128)(2,1)S(1)}, bf16[16,64,128]{2,1,0:T(8,128)(2,1)S(1)}, u32[]{:S(2)}, u32[]{:S(2)}) %collective-permute-start.12) | collective-permute-done | bytes 262176 | tf_op jit(solution)/shard_map/ppermute | solution.py:312
  77.8 5.4 %collective-permute-start.17 = (bf16[16,64,128]{2,1,0:T(8,128)(2,1)S(1)}, bf16[16,64,128]{2,1,0:T(8,128)(2,1)S(1)}, u32[]{:S(2)}, u32[]{:S(2)}) collective-permute-start(bf16[16,64,128]{2,1,0:T(8,128)(2,1)S(1)} %collective-permute-done.16), channel_id=1, source_target_pairs={{0,0},{1,2},{2,1},{3,3},{4,68},{5,70},{6,69},{7,71},{8,40},{9,42},... | collective-permute-start | bytes 786440 | tf_op jit(solution)/shard_map/ppermute | solution.py:322
  87.2 3.5 %shard_map.84 = (bf16[64,64,128]{2,1,0:T(8,128)(2,1)}, bf16[32,32,128]{2,1,0:T(8,128)(2,1)S(1)}) custom-call(bf16[16,64,128]{2,1,0:T(8,128)(2,1)S(1)} %collective-permute-done.17.coeffs, bf16[64,64,128]{2,1,0:T(8,128)(2,1)S(1)} %bitcast.46, bf16[64,64,128]{2,1,0:T(8,128)(2,1)S(1)} %bitcast.48, bf16[16,64,128]{2,1,0:T(8,128)(2,1)S(1)} %shard_map.83.token), custom_call_target="tpu_custom_call" | custom-call | flops 67108864 | bytes 4194304 | tf_op jit(solution)/shard_map/pallas_call | solution.py:338
  91.5 3.5 %shard_map.85 = (bf16[64,64,128]{2,1,0:T(8,128)(2,1)}, bf16[32,32,128]{2,1,0:T(8,128)(2,1)S(1)}) custom-call(bf16[16,64,128]{2,1,0:T(8,128)(2,1)S(1)} %collective-permute-done.15.coeffs, bf16[64,64,128]{2,1,0:T(8,128)(2,1)S(1)} %bitcast.47, bf16[64,64,128]{2,1,0:T(8,128)(2,1)S(1)} %bitcast.49, ...), custom_call_target="tpu_custom_call", output_to_operand_aliasing={{0}: (4, {})} | custom-call | flops 67108864 | bytes 4194304 | tf_op jit(solution)/shard_map/pallas_call | solution.py:338
  95.7 3.6 %collective-permute-start.21 = (bf16[32,32,128]{2,1,0:T(8,128)(2,1)S(1)}, bf16[32,32,128]{2,1,0:T(8,128)(2,1)S(1)}, u32[]{:S(2)}, u32[]{:S(2)}) collective-permute-start(bf16[32,32,128]{2,1,0:T(8,128)(2,1)S(1)} %collective-permute-done.20), channel_id=1, source_target_pairs={{0,0},{1,2},{2,1},{3,3},{4,68},{5,70},{6,69},{7,71},{8,40},{9,42},... | collective-permute-start | bytes 786440 | tf_op jit(solution)/shard_map/ppermute | solution.py:322
  103.4 2.1 %shard_map.86 = (f32[32,32,128]{2,1,0:T(8,128)S(1)}, bf16[32,32,128]{2,1,0:T(8,128)(2,1)S(1)}) custom-call(bf16[32,32,128]{2,1,0:T(8,128)(2,1)S(1)} %collective-permute-done.21.adjoint, bf16[13,64,64,128]{3,2,1,0:T(8,128)(2,1)S(1)} %bitcast.27, bf16[32,32,128]{2,1,0:T(8,128)(2,1)S(1)} %get-tuple-element.37.token), custom_call_target="tpu_custom_call" | custom-call | flops 234881024 | bytes 7340032 | tf_op jit(solution)/shard_map/pallas_call | solution.py:373
  107.0 2.1 %shard_map.87 = (f32[32,32,128]{2,1,0:T(8,128)S(1)}, bf16[32,32,128]{2,1,0:T(8,128)(2,1)S(1)}) custom-call(bf16[32,32,128]{2,1,0:T(8,128)(2,1)S(1)} %collective-permute-done.19.adjoint, bf16[13,64,64,128]{3,2,1,0:T(8,128)(2,1)S(1)} %bitcast.28, bf16[32,32,128]{2,1,0:T(8,128)(2,1)S(1)} %get-tuple-element.38.token), custom_call_target="tpu_custom_call" | custom-call | flops 234881024 | bytes 7340032 | tf_op jit(solution)/shard_map/pallas_call | solution.py:373
  109.4 4.2 %collective-permute-done.23.received = bf16[32,32,128]{2,1,0:T(8,128)(2,1)S(1)} collective-permute-done((bf16[32,32,128]{2,1,0:T(8,128)(2,1)S(1)}, bf16[32,32,128]{2,1,0:T(8,128)(2,1)S(1)}, u32[]{:S(2)}, u32[]{:S(2)}) %collective-permute-start.23) | collective-permute-done | bytes 262176 | tf_op jit(solution)/shard_map/ppermute | solution.py:312
  114.1 32.1 %collective-permute-start.25 = (bf16[32,32,128]{2,1,0:T(8,128)(2,1)S(1)}, bf16[32,32,128]{2,1,0:T(8,128)(2,1)S(1)}, u32[]{:S(2)}, u32[]{:S(2)}) collective-permute-start(bf16[32,32,128]{2,1,0:T(8,128)(2,1)S(1)} %get-tuple-element.42.refs_0_), channel_id=1, source_target_pairs={{0,64},{2,66},{4,68},{6,70},{8,72},{10,74},{12,76},{14,78},{16,80}... | collective-permute-start | bytes 786440 | tf_op jit(solution)/shard_map/ppermute | solution.py:312
  146.7 3.8 %collective-permute-start.24 = (bf16[32,32,128]{2,1,0:T(8,128)(2,1)S(1)}, bf16[32,32,128]{2,1,0:T(8,128)(2,1)S(1)}, u32[]{:S(2)}, u32[]{:S(2)}) collective-permute-start(bf16[32,32,128]{2,1,0:T(8,128)(2,1)S(1)} %get-tuple-element.44.refs_0_), channel_id=1, source_target_pairs={{0,64},{2,66},{4,68},{6,70},{8,72},{10,74},{12,76},{14,78},{16,80}... | collective-permute-start | bytes 786440 | tf_op jit(solution)/shard_map/ppermute | solution.py:312
  152.6 4.3 %collective-permute-done.24.received = bf16[32,32,128]{2,1,0:T(8,128)(2,1)S(1)} collective-permute-done((bf16[32,32,128]{2,1,0:T(8,128)(2,1)S(1)}, bf16[32,32,128]{2,1,0:T(8,128)(2,1)S(1)}, u32[]{:S(2)}, u32[]{:S(2)}) %collective-permute-start.24) | collective-permute-done | bytes 262176 | tf_op jit(solution)/shard_map/ppermute | solution.py:312
  157.6 4.7 %collective-permute-done.27.received = bf16[32,32,128]{2,1,0:T(8,128)(2,1)S(1)} collective-permute-done((bf16[32,32,128]{2,1,0:T(8,128)(2,1)S(1)}, bf16[32,32,128]{2,1,0:T(8,128)(2,1)S(1)}, u32[]{:S(2)}, u32[]{:S(2)}) %collective-permute-start.27) | collective-permute-done | bytes 262176 | tf_op jit(solution)/shard_map/ppermute | solution.py:312
  164.2 3.4 %collective-permute-done.26.received = bf16[32,32,128]{2,1,0:T(8,128)(2,1)S(1)} collective-permute-done((bf16[32,32,128]{2,1,0:T(8,128)(2,1)S(1)}, bf16[32,32,128]{2,1,0:T(8,128)(2,1)S(1)}, u32[]{:S(2)}, u32[]{:S(2)}) %collective-permute-start.26) | collective-permute-done | bytes 262176 | tf_op jit(solution)/shard_map/ppermute | solution.py:312
  169.3 2.9 %collective-permute-done.29.received = bf16[32,32,128]{2,1,0:T(8,128)(2,1)S(1)} collective-permute-done((bf16[32,32,128]{2,1,0:T(8,128)(2,1)S(1)}, bf16[32,32,128]{2,1,0:T(8,128)(2,1)S(1)}, u32[]{:S(2)}, u32[]{:S(2)}) %collective-permute-start.29) | collective-permute-done | bytes 262176 | tf_op jit(solution)/shard_map/ppermute | solution.py:312
  172.7 4.0 %collective-permute-start.31 = (bf16[32,32,128]{2,1,0:T(8,128)(2,1)S(1)}, bf16[32,32,128]{2,1,0:T(8,128)(2,1)S(1)}, u32[]{:S(2)}, u32[]{:S(2)}) collective-permute-start(bf16[32,32,128]{2,1,0:T(8,128)(2,1)S(1)} %get-tuple-element.54.refs_0_), channel_id=1, source_target_pairs={{0,8},{2,10},{4,12},{6,14},{8,0},{10,2},{12,4},{14,6},{16,24},{18,... | collective-permute-start | bytes 786440 | tf_op jit(solution)/shard_map/ppermute | solution.py:312
  178.3 3.4 %collective-permute-start.30 = (bf16[32,32,128]{2,1,0:T(8,128)(2,1)S(1)}, bf16[32,32,128]{2,1,0:T(8,128)(2,1)S(1)}, u32[]{:S(2)}, u32[]{:S(2)}) collective-permute-start(bf16[32,32,128]{2,1,0:T(8,128)(2,1)S(1)} %get-tuple-element.56.refs_0_), channel_id=1, source_target_pairs={{0,8},{2,10},{4,12},{6,14},{8,0},{10,2},{12,4},{14,6},{16,24},{18,... | collective-permute-start | bytes 786440 | tf_op jit(solution)/shard_map/ppermute | solution.py:312
  183.8 5.0 %collective-permute-done.30.received = bf16[32,32,128]{2,1,0:T(8,128)(2,1)S(1)} collective-permute-done((bf16[32,32,128]{2,1,0:T(8,128)(2,1)S(1)}, bf16[32,32,128]{2,1,0:T(8,128)(2,1)S(1)}, u32[]{:S(2)}, u32[]{:S(2)}) %collective-permute-start.30) | collective-permute-done | bytes 262176 | tf_op jit(solution)/shard_map/ppermute | solution.py:312
  189.4 4.3 %collective-permute-done.33.received = bf16[32,32,128]{2,1,0:T(8,128)(2,1)S(1)} collective-permute-done((bf16[32,32,128]{2,1,0:T(8,128)(2,1)S(1)}, bf16[32,32,128]{2,1,0:T(8,128)(2,1)S(1)}, u32[]{:S(2)}, u32[]{:S(2)}) %collective-permute-start.33) | collective-permute-done | bytes 262176 | tf_op jit(solution)/shard_map/ppermute | solution.py:312
  196.1 3.3 %collective-permute-done.32.received = bf16[32,32,128]{2,1,0:T(8,128)(2,1)S(1)} collective-permute-done((bf16[32,32,128]{2,1,0:T(8,128)(2,1)S(1)}, bf16[32,32,128]{2,1,0:T(8,128)(2,1)S(1)}, u32[]{:S(2)}, u32[]{:S(2)}) %collective-permute-start.32) | collective-permute-done | bytes 262176 | tf_op jit(solution)/shard_map/ppermute | solution.py:312
  (87 shorter events, 56.5 us)
Async XLA Ops:
  9.3 7.5 %collective-permute-start.3 = (bf16[16,64,128]{2,1,0:T(8,128)(2,1)S(1)}, bf16[16,64,128]{2,1,0:T(8,128)(2,1)S(1)}, u32[]{:S(2)}, u32[]{:S(2)}) collective-permute-start(bf16[16,64,128]{2,1,0:T(8,128)(2,1)S(1)} %shard_map.70.refs_0_.own), channel_id=1, source_target_pairs={{0,4},{2,6},{4,0},{6,2},{8,12},{10,14},{12,8},{14,10},{16,20},{18,... | collective-permute-start | bytes 786440 | tf_op jit(solution)/shard_map/ppermute | solution.py:312
  11.1 11.3 %collective-permute-start.2 = (bf16[16,64,128]{2,1,0:T(8,128)(2,1)S(1)}, bf16[16,64,128]{2,1,0:T(8,128)(2,1)S(1)}, u32[]{:S(2)}, u32[]{:S(2)}) collective-permute-start(bf16[16,64,128]{2,1,0:T(8,128)(2,1)S(1)} %shard_map.71.refs_0_.own), channel_id=1, source_target_pairs={{0,4},{2,6},{4,0},{6,2},{8,12},{10,14},{12,8},{14,10},{16,20},{18,... | collective-permute-start | bytes 786440 | tf_op jit(solution)/shard_map/ppermute | solution.py:312
  17.2 13.1 %collective-permute-start.5 = (bf16[16,64,128]{2,1,0:T(8,128)(2,1)S(1)}, bf16[16,64,128]{2,1,0:T(8,128)(2,1)S(1)}, u32[]{:S(2)}, u32[]{:S(2)}) collective-permute-start(bf16[16,64,128]{2,1,0:T(8,128)(2,1)S(1)} %shard_map.72.refs_0_.own), channel_id=1, source_target_pairs={{0,8},{2,10},{4,12},{6,14},{8,0},{10,2},{12,4},{14,6},{16,24},{18,... | collective-permute-start | bytes 786440 | tf_op jit(solution)/shard_map/ppermute | solution.py:312
  22.8 13.1 %collective-permute-start.4 = (bf16[16,64,128]{2,1,0:T(8,128)(2,1)S(1)}, bf16[16,64,128]{2,1,0:T(8,128)(2,1)S(1)}, u32[]{:S(2)}, u32[]{:S(2)}) collective-permute-start(bf16[16,64,128]{2,1,0:T(8,128)(2,1)S(1)} %shard_map.73.refs_0_.own), channel_id=1, source_target_pairs={{0,8},{2,10},{4,12},{6,14},{8,0},{10,2},{12,4},{14,6},{16,24},{18,... | collective-permute-start | bytes 786440 | tf_op jit(solution)/shard_map/ppermute | solution.py:312
  30.7 9.3 %collective-permute-start.7 = (bf16[16,64,128]{2,1,0:T(8,128)(2,1)S(1)}, bf16[16,64,128]{2,1,0:T(8,128)(2,1)S(1)}, u32[]{:S(2)}, u32[]{:S(2)}) collective-permute-start(bf16[16,64,128]{2,1,0:T(8,128)(2,1)S(1)} %shard_map.74.refs_0_.own), channel_id=1, source_target_pairs={{0,16},{2,18},{4,20},{6,22},{8,24},{10,26},{12,28},{14,30},{16,0},... | collective-permute-start | bytes 786440 | tf_op jit(solution)/shard_map/ppermute | solution.py:312
  36.3 9.0 %collective-permute-start.6 = (bf16[16,64,128]{2,1,0:T(8,128)(2,1)S(1)}, bf16[16,64,128]{2,1,0:T(8,128)(2,1)S(1)}, u32[]{:S(2)}, u32[]{:S(2)}) collective-permute-start(bf16[16,64,128]{2,1,0:T(8,128)(2,1)S(1)} %shard_map.75.refs_0_.own), channel_id=1, source_target_pairs={{0,16},{2,18},{4,20},{6,22},{8,24},{10,26},{12,28},{14,30},{16,0},... | collective-permute-start | bytes 786440 | tf_op jit(solution)/shard_map/ppermute | solution.py:312
  40.4 6.7 %collective-permute-start.9 = (bf16[16,64,128]{2,1,0:T(8,128)(2,1)S(1)}, bf16[16,64,128]{2,1,0:T(8,128)(2,1)S(1)}, u32[]{:S(2)}, u32[]{:S(2)}) collective-permute-start(bf16[16,64,128]{2,1,0:T(8,128)(2,1)S(1)} %shard_map.76.refs_0_.own), channel_id=1, source_target_pairs={{0,32},{2,34},{4,36},{6,38},{8,40},{10,42},{12,44},{14,46},{16,48}... | collective-permute-start | bytes 786440 | tf_op jit(solution)/shard_map/ppermute | solution.py:312
  45.7 6.6 %collective-permute-start.8 = (bf16[16,64,128]{2,1,0:T(8,128)(2,1)S(1)}, bf16[16,64,128]{2,1,0:T(8,128)(2,1)S(1)}, u32[]{:S(2)}, u32[]{:S(2)}) collective-permute-start(bf16[16,64,128]{2,1,0:T(8,128)(2,1)S(1)} %shard_map.77.refs_0_.own), channel_id=1, source_target_pairs={{0,32},{2,34},{4,36},{6,38},{8,40},{10,42},{12,44},{14,46},{16,48}... | collective-permute-start | bytes 786440 | tf_op jit(solution)/shard_map/ppermute | solution.py:312
  47.5 12.8 %collective-permute-start.11 = (bf16[16,64,128]{2,1,0:T(8,128)(2,1)S(1)}, bf16[16,64,128]{2,1,0:T(8,128)(2,1)S(1)}, u32[]{:S(2)}, u32[]{:S(2)}) collective-permute-start(bf16[16,64,128]{2,1,0:T(8,128)(2,1)S(1)} %shard_map.78.refs_0_.own), channel_id=1, source_target_pairs={{0,64},{2,66},{4,68},{6,70},{8,72},{10,74},{12,76},{14,78},{16,80}... | collective-permute-start | bytes 786440 | tf_op jit(solution)/shard_map/ppermute | solution.py:312
  52.7 13.2 %collective-permute-start.10 = (bf16[16,64,128]{2,1,0:T(8,128)(2,1)S(1)}, bf16[16,64,128]{2,1,0:T(8,128)(2,1)S(1)}, u32[]{:S(2)}, u32[]{:S(2)}) collective-permute-start(bf16[16,64,128]{2,1,0:T(8,128)(2,1)S(1)} %shard_map.79.refs_0_.own), channel_id=1, source_target_pairs={{0,64},{2,66},{4,68},{6,70},{8,72},{10,74},{12,76},{14,78},{16,80}... | collective-permute-start | bytes 786440 | tf_op jit(solution)/shard_map/ppermute | solution.py:312
  60.8 6.4 %collective-permute-start.13 = (bf16[16,64,128]{2,1,0:T(8,128)(2,1)S(1)}, bf16[16,64,128]{2,1,0:T(8,128)(2,1)S(1)}, u32[]{:S(2)}, u32[]{:S(2)}) collective-permute-start(bf16[16,64,128]{2,1,0:T(8,128)(2,1)S(1)} %shard_map.80.refs_0_.own), channel_id=1, source_target_pairs={{0,1},{1,0},{2,3},{3,2},{4,5},{5,4},{6,7},{7,6},{8,9},{9,8},{10,11... | collective-permute-start | bytes 786440 | tf_op jit(solution)/shard_map/ppermute | solution.py:312
  66.4 8.5 %collective-permute-start.12 = (bf16[16,64,128]{2,1,0:T(8,128)(2,1)S(1)}, bf16[16,64,128]{2,1,0:T(8,128)(2,1)S(1)}, u32[]{:S(2)}, u32[]{:S(2)}) collective-permute-start(bf16[16,64,128]{2,1,0:T(8,128)(2,1)S(1)} %shard_map.81.token.own), channel_id=1, source_target_pairs={{0,1},{1,0},{2,3},{3,2},{4,5},{5,4},{6,7},{7,6},{8,9},{9,8},{10,11... | collective-permute-start | bytes 786440 | tf_op jit(solution)/shard_map/ppermute | solution.py:312
  69.3 8.5 %collective-permute-start.16 = (bf16[16,64,128]{2,1,0:T(8,128)(2,1)S(1)}, bf16[16,64,128]{2,1,0:T(8,128)(2,1)S(1)}, u32[]{:S(2)}, u32[]{:S(2)}) collective-permute-start(bf16[16,64,128]{2,1,0:T(8,128)(2,1)S(1)} %shard_map.82.token), channel_id=1, source_target_pairs={{0,0},{1,1},{2,2},{3,3},{4,68},{5,69},{6,70},{7,71},{8,40},{9,41},... | collective-permute-start | bytes 786440 | tf_op jit(solution)/shard_map/ppermute | solution.py:322
  77.1 6.1 %collective-permute-start.14 = (bf16[16,64,128]{2,1,0:T(8,128)(2,1)S(1)}, bf16[16,64,128]{2,1,0:T(8,128)(2,1)S(1)}, u32[]{:S(2)}, u32[]{:S(2)}) collective-permute-start(bf16[16,64,128]{2,1,0:T(8,128)(2,1)S(1)} %shard_map.83.token), channel_id=1, source_target_pairs={{0,0},{1,1},{2,2},{3,3},{4,68},{5,69},{6,70},{7,71},{8,40},{9,41},... | collective-permute-start | bytes 786440 | tf_op jit(solution)/shard_map/ppermute | solution.py:322
  77.8 9.5 %collective-permute-start.17 = (bf16[16,64,128]{2,1,0:T(8,128)(2,1)S(1)}, bf16[16,64,128]{2,1,0:T(8,128)(2,1)S(1)}, u32[]{:S(2)}, u32[]{:S(2)}) collective-permute-start(bf16[16,64,128]{2,1,0:T(8,128)(2,1)S(1)} %collective-permute-done.16), channel_id=1, source_target_pairs={{0,0},{1,2},{2,1},{3,3},{4,68},{5,70},{6,69},{7,71},{8,40},{9,42},... | collective-permute-start | bytes 786440 | tf_op jit(solution)/shard_map/ppermute | solution.py:322
  83.2 8.2 %collective-permute-start.15 = (bf16[16,64,128]{2,1,0:T(8,128)(2,1)S(1)}, bf16[16,64,128]{2,1,0:T(8,128)(2,1)S(1)}, u32[]{:S(2)}, u32[]{:S(2)}) collective-permute-start(bf16[16,64,128]{2,1,0:T(8,128)(2,1)S(1)} %collective-permute-done.14), channel_id=1, source_target_pairs={{0,0},{1,2},{2,1},{3,3},{4,68},{5,70},{6,69},{7,71},{8,40},{9,42},... | collective-permute-start | bytes 786440 | tf_op jit(solution)/shard_map/ppermute | solution.py:322
  90.8 4.9 %collective-permute-start.20 = (bf16[32,32,128]{2,1,0:T(8,128)(2,1)S(1)}, bf16[32,32,128]{2,1,0:T(8,128)(2,1)S(1)}, u32[]{:S(2)}, u32[]{:S(2)}) collective-permute-start(bf16[32,32,128]{2,1,0:T(8,128)(2,1)S(1)} %get-tuple-element.34.token), channel_id=1, source_target_pairs={{0,0},{1,1},{2,2},{3,3},{4,68},{5,69},{6,70},{7,71},{8,40},{9,41},... | collective-permute-start | bytes 786440 | tf_op jit(solution)/shard_map/ppermute | solution.py:322
  95.7 7.7 %collective-permute-start.21 = (bf16[32,32,128]{2,1,0:T(8,128)(2,1)S(1)}, bf16[32,32,128]{2,1,0:T(8,128)(2,1)S(1)}, u32[]{:S(2)}, u32[]{:S(2)}) collective-permute-start(bf16[32,32,128]{2,1,0:T(8,128)(2,1)S(1)} %collective-permute-done.20), channel_id=1, source_target_pairs={{0,0},{1,2},{2,1},{3,3},{4,68},{5,70},{6,69},{7,71},{8,40},{9,42},... | collective-permute-start | bytes 786440 | tf_op jit(solution)/shard_map/ppermute | solution.py:322
  99.3 7.7 %collective-permute-start.19 = (bf16[32,32,128]{2,1,0:T(8,128)(2,1)S(1)}, bf16[32,32,128]{2,1,0:T(8,128)(2,1)S(1)}, u32[]{:S(2)}, u32[]{:S(2)}) collective-permute-start(bf16[32,32,128]{2,1,0:T(8,128)(2,1)S(1)} %collective-permute-done.18), channel_id=1, source_target_pairs={{0,0},{1,2},{2,1},{3,3},{4,68},{5,70},{6,69},{7,71},{8,40},{9,42},... | collective-permute-start | bytes 786440 | tf_op jit(solution)/shard_map/ppermute | solution.py:322
  105.5 8.1 %collective-permute-start.23 = (bf16[32,32,128]{2,1,0:T(8,128)(2,1)S(1)}, bf16[32,32,128]{2,1,0:T(8,128)(2,1)S(1)}, u32[]{:S(2)}, u32[]{:S(2)}) collective-permute-start(bf16[32,32,128]{2,1,0:T(8,128)(2,1)S(1)} %get-tuple-element.38.token), channel_id=1, source_target_pairs={{0,1},{1,0},{2,3},{3,2},{4,5},{5,4},{6,7},{7,6},{8,9},{9,8},{10,11... | collective-permute-start | bytes 786440 | tf_op jit(solution)/shard_map/ppermute | solution.py:312
  109.1 37.1 %collective-permute-start.22 = (bf16[32,32,128]{2,1,0:T(8,128)(2,1)S(1)}, bf16[32,32,128]{2,1,0:T(8,128)(2,1)S(1)}, u32[]{:S(2)}, u32[]{:S(2)}) collective-permute-start(bf16[32,32,128]{2,1,0:T(8,128)(2,1)S(1)} %get-tuple-element.40.refs_0_), channel_id=1, source_target_pairs={{0,1},{1,0},{2,3},{3,2},{4,5},{5,4},{6,7},{7,6},{8,9},{9,8},{10,11... | collective-permute-start | bytes 786440 | tf_op jit(solution)/shard_map/ppermute | solution.py:312
  114.1 36.9 %collective-permute-start.25 = (bf16[32,32,128]{2,1,0:T(8,128)(2,1)S(1)}, bf16[32,32,128]{2,1,0:T(8,128)(2,1)S(1)}, u32[]{:S(2)}, u32[]{:S(2)}) collective-permute-start(bf16[32,32,128]{2,1,0:T(8,128)(2,1)S(1)} %get-tuple-element.42.refs_0_), channel_id=1, source_target_pairs={{0,64},{2,66},{4,68},{6,70},{8,72},{10,74},{12,76},{14,78},{16,80}... | collective-permute-start | bytes 786440 | tf_op jit(solution)/shard_map/ppermute | solution.py:312
  146.7 10.3 %collective-permute-start.24 = (bf16[32,32,128]{2,1,0:T(8,128)(2,1)S(1)}, bf16[32,32,128]{2,1,0:T(8,128)(2,1)S(1)}, u32[]{:S(2)}, u32[]{:S(2)}) collective-permute-start(bf16[32,32,128]{2,1,0:T(8,128)(2,1)S(1)} %get-tuple-element.44.refs_0_), channel_id=1, source_target_pairs={{0,64},{2,66},{4,68},{6,70},{8,72},{10,74},{12,76},{14,78},{16,80}... | collective-permute-start | bytes 786440 | tf_op jit(solution)/shard_map/ppermute | solution.py:312
  151.5 10.8 %collective-permute-start.27 = (bf16[32,32,128]{2,1,0:T(8,128)(2,1)S(1)}, bf16[32,32,128]{2,1,0:T(8,128)(2,1)S(1)}, u32[]{:S(2)}, u32[]{:S(2)}) collective-permute-start(bf16[32,32,128]{2,1,0:T(8,128)(2,1)S(1)} %get-tuple-element.46.refs_0_), channel_id=1, source_target_pairs={{0,32},{2,34},{4,36},{6,38},{8,40},{10,42},{12,44},{14,46},{16,48}... | collective-permute-start | bytes 786440 | tf_op jit(solution)/shard_map/ppermute | solution.py:312
  157.5 10.2 %collective-permute-start.26 = (bf16[32,32,128]{2,1,0:T(8,128)(2,1)S(1)}, bf16[32,32,128]{2,1,0:T(8,128)(2,1)S(1)}, u32[]{:S(2)}, u32[]{:S(2)}) collective-permute-start(bf16[32,32,128]{2,1,0:T(8,128)(2,1)S(1)} %get-tuple-element.48.refs_0_), channel_id=1, source_target_pairs={{0,32},{2,34},{4,36},{6,38},{8,40},{10,42},{12,44},{14,46},{16,48}... | collective-permute-start | bytes 786440 | tf_op jit(solution)/shard_map/ppermute | solution.py:312
  162.7 9.5 %collective-permute-start.29 = (bf16[32,32,128]{2,1,0:T(8,128)(2,1)S(1)}, bf16[32,32,128]{2,1,0:T(8,128)(2,1)S(1)}, u32[]{:S(2)}, u32[]{:S(2)}) collective-permute-start(bf16[32,32,128]{2,1,0:T(8,128)(2,1)S(1)} %get-tuple-element.50.refs_0_), channel_id=1, source_target_pairs={{0,16},{2,18},{4,20},{6,22},{8,24},{10,26},{12,28},{14,30},{16,0},... | collective-permute-start | bytes 786440 | tf_op jit(solution)/shard_map/ppermute | solution.py:312
  168.1 9.7 %collective-permute-start.28 = (bf16[32,32,128]{2,1,0:T(8,128)(2,1)S(1)}, bf16[32,32,128]{2,1,0:T(8,128)(2,1)S(1)}, u32[]{:S(2)}, u32[]{:S(2)}) collective-permute-start(bf16[32,32,128]{2,1,0:T(8,128)(2,1)S(1)} %get-tuple-element.52.refs_0_), channel_id=1, source_target_pairs={{0,16},{2,18},{4,20},{6,22},{8,24},{10,26},{12,28},{14,30},{16,0},... | collective-permute-start | bytes 786440 | tf_op jit(solution)/shard_map/ppermute | solution.py:312
  172.7 10.5 %collective-permute-start.31 = (bf16[32,32,128]{2,1,0:T(8,128)(2,1)S(1)}, bf16[32,32,128]{2,1,0:T(8,128)(2,1)S(1)}, u32[]{:S(2)}, u32[]{:S(2)}) collective-permute-start(bf16[32,32,128]{2,1,0:T(8,128)(2,1)S(1)} %get-tuple-element.54.refs_0_), channel_id=1, source_target_pairs={{0,8},{2,10},{4,12},{6,14},{8,0},{10,2},{12,4},{14,6},{16,24},{18,... | collective-permute-start | bytes 786440 | tf_op jit(solution)/shard_map/ppermute | solution.py:312
  178.3 10.5 %collective-permute-start.30 = (bf16[32,32,128]{2,1,0:T(8,128)(2,1)S(1)}, bf16[32,32,128]{2,1,0:T(8,128)(2,1)S(1)}, u32[]{:S(2)}, u32[]{:S(2)}) collective-permute-start(bf16[32,32,128]{2,1,0:T(8,128)(2,1)S(1)} %get-tuple-element.56.refs_0_), channel_id=1, source_target_pairs={{0,8},{2,10},{4,12},{6,14},{8,0},{10,2},{12,4},{14,6},{16,24},{18,... | collective-permute-start | bytes 786440 | tf_op jit(solution)/shard_map/ppermute | solution.py:312
  183.7 10.1 %collective-permute-start.33 = (bf16[32,32,128]{2,1,0:T(8,128)(2,1)S(1)}, bf16[32,32,128]{2,1,0:T(8,128)(2,1)S(1)}, u32[]{:S(2)}, u32[]{:S(2)}) collective-permute-start(bf16[32,32,128]{2,1,0:T(8,128)(2,1)S(1)} %get-tuple-element.58.refs_0_), channel_id=1, source_target_pairs={{0,4},{2,6},{4,0},{6,2},{8,12},{10,14},{12,8},{14,10},{16,20},{18,... | collective-permute-start | bytes 786440 | tf_op jit(solution)/shard_map/ppermute | solution.py:312
  189.4 10.1 %collective-permute-start.32 = (bf16[32,32,128]{2,1,0:T(8,128)(2,1)S(1)}, bf16[32,32,128]{2,1,0:T(8,128)(2,1)S(1)}, u32[]{:S(2)}, u32[]{:S(2)}) collective-permute-start(bf16[32,32,128]{2,1,0:T(8,128)(2,1)S(1)} %get-tuple-element.60.refs_0_), channel_id=1, source_target_pairs={{0,4},{2,6},{4,0},{6,2},{8,12},{10,14},{12,8},{14,10},{16,20},{18,... | collective-permute-start | bytes 786440 | tf_op jit(solution)/shard_map/ppermute | solution.py:312
  194.3 6.4 %collective-permute-start.35 = (bf16[32,32,128]{2,1,0:T(8,128)(2,1)S(1)}, bf16[32,32,128]{2,1,0:T(8,128)(2,1)S(1)}, u32[]{:S(2)}, u32[]{:S(2)}) collective-permute-start(bf16[32,32,128]{2,1,0:T(8,128)(2,1)S(1)} %get-tuple-element.62.refs_0_), channel_id=1, source_target_pairs={{0,2},{2,0},{4,6},{6,4},{8,10},{10,8},{12,14},{14,12},{16,18},{18,... | collective-permute-start | bytes 786440 | tf_op jit(solution)/shard_map/ppermute | solution.py:312
  (10 other events, 95.9 us)
where the time goes:
time: 205 us; the launch traced here: 204 us
  starting transfers between devices  92.3 us (45%)
  waiting for transfers between devices  74.2 us (36%)
  Pallas kernels  32.1 us (16%)
  local copies, waits for them, and re-layouts  4.57 us (2%)
    ppermute x28, starting transfers between devices, exchange(): return lax.ppermute(array, axis, [(i, i ^ 1 << bit) for i in range(count)])  76.7 us
    ppermute x28, waiting for transfers between devices, exchange(): return lax.ppermute(array, axis, [(i, i ^ 1 << bit) for i in range(count)])  68.8 us
    ppermute x8, starting transfers between devices, move(): return lax.ppermute(array, ('src', 'hi'), pairs_of)  15.6 us
    pallas_call x2, Pallas kernels, target_call(): call(kernel, (full_shape, pair_shape), specs, (HBM, VMEM), [held, sems, w...  7.01 us
    pallas_call x12, Pallas kernels, adjoint_call(): call(kernel, (kept_shape, pair_shape), specs, (VMEM, VMEM), [], flops, mo...  5.84 us
    ppermute x8, waiting for transfers between devices, move(): return lax.ppermute(array, ('src', 'hi'), pairs_of)  5.45 us
    pallas_call x12, Pallas kernels, cross_call(): call(kernel, forward_shape, specs, VMEM, [], flops, moved, 4)(*operands)  5.16 us
    pallas_call x2, Pallas kernels, local_forward_call(): call(kernel, forward_shape, [VMEM] * 3 + [ANY], VMEM, scratch, 7 * flops,...  4.23 us
  transfers between devices with their start and end apart: 36, of which 23 were waited for; matrix products, arithmetic and copies ran while one was open for 1% of the time, Pallas kernels for 14%

commit v1 on v0

--- a/solution.py
+++ b/solution.py
@@ -47,26 +47,6 @@
     if level < src_bits:
         return (lax.axis_index("src") >> level & 1) == 1
     return (lax.axis_index("hi") >> (level - src_bits) & 1) == 1
-
-
-def shear_x(device):
-    return device ^ reverse_bits(device >> 4 & 3, 2) << 1
-
-
-def shear_y(device):
-    return device ^ reverse_bits(device >> 1 & 3, 2) << 4
-
-
-def swap_ends(device):
-    return device & 62 | device >> 6 | (device & 1) << 6
-
-
-def first_hop(device):
-    return shear_y(device)
-
-
-def second_hop(device):
-    return swap_ends(shear_y(shear_x(device)))
 
 
 def dot(a, b):
@@ -150,17 +130,21 @@
                     target[g] = forward_group(weights, stacked, lane_boxes, rank)
 
 
-def target_kernel(chunk, coeffs, final, observed, token, *refs):
-    residual, adjoint, held, sems, wide, result = refs[-6:]
-    groups, rank = coeffs.shape[0], coeffs.shape[1]
-    vectors, boxes, points = held.shape
-    box_bits = boxes.bit_length() - 1
-    lane_boxes = LANES // vectors
-    own_rows = pl.ds(chunk * vectors, vectors)
-    fetch = pltpu.make_async_copy(observed.at[own_rows], held, sems.at[0])
+def order_kernel(observed, token, out, held, sems, wide):
+    total, boxes, points = held.shape
+    fetch = pltpu.make_async_copy(observed, held, sems.at[0])
     fetch.start()
     fetch.wait()
     wide[...] = held[...].astype(F32).reshape(wide.shape)
+    for t in range(boxes):
+        out[t] = wide[pl.ds(t, total, stride=boxes), :].astype(BF)
+
+
+def target_kernel(chunk, coeffs, final, wanted, token, residual, adjoint):
+    groups, rank = coeffs.shape[0], coeffs.shape[1]
+    boxes, vectors = residual.shape[0], residual.shape[1]
+    box_bits = boxes.bit_length() - 1
+    lane_boxes = LANES // vectors
     for g in range(groups):
         turned = jnp.transpose(coeffs[g].astype(F32)).astype(BF)
         for pair in range(lane_boxes // 2):
@@ -168,16 +152,26 @@
             for b in (2 * pair, 2 * pair + 1):
                 t = reverse_bits(g * lane_boxes + b, box_bits)
                 mat = final[t]
-                rows = pl.ds(t, vectors, stride=boxes)
-                value = dot(turned[b * vectors:(b + 1) * vectors], mat) - wide[rows, :]
-                result[rows, :] = value
+                value = dot(turned[b * vectors:(b + 1) * vectors], mat)
+                target = wanted[t, pl.ds(chunk * vectors, vectors), :].astype(F32)
+                value = (value - target).astype(BF)
+                residual[t] = value
                 kept.append(value)
                 mats.append(mat)
-            rows = jnp.concatenate(kept, axis=0).astype(BF)
-            product = dot_nt(rows, jnp.concatenate(mats, axis=0))
+            product = dot_nt(jnp.concatenate(kept, axis=0), jnp.concatenate(mats, axis=0))
             adjoint[g * lane_boxes // 2 + pair] = pick_lanes(product, vectors, 2, rank).astype(BF)
-    held[...] = result[...].reshape(held.shape).astype(BF)
-    store = pltpu.make_async_copy(held, residual.at[own_rows], sems.at[1])
+
+
+def residual_kernel(chunks, *refs):
+    parts = refs[:chunks]
+    token, residual, done, held, sems, wide = refs[chunks:]
+    boxes, vectors = parts[0].shape[0], parts[0].shape[1]
+    for t in range(boxes):
+        rows = jnp.concatenate([part[t].astype(F32) for part in parts], axis=0)
+        wide[pl.ds(t, chunks * vectors, stride=boxes), :] = rows
+    held[...] = wide[...].reshape(held.shape).astype(BF)
+    done[...] = jnp.zeros(done.shape, done.dtype)
+    store = pltpu.make_async_copy(held, residual, sems.at[0])
     store.start()
     store.wait()
 
@@ -311,33 +305,41 @@
             axis, count, bit = "hi", hi_count, level - src_bits
         return lax.ppermute(array, axis, [(i, i ^ 1 << bit) for i in range(count)])
 
-    def move(array, route):
+    def reversal(array):
         pairs_of = []
         for src in range(src_count):
             for hi in range(hi_count):
-                there = route(hi * src_count + src)
+                there = reverse_bits(hi * src_count + src, device_bits)
                 pairs_of.append(
                     (src * hi_count + hi, there % src_count * hi_count + there // src_count)
                 )
         return lax.ppermute(array, ("src", "hi"), pairs_of)
 
-    def reversal(array):
-        return move(move(array, first_hop), second_hop)
-
-    for device in range(src_count * hi_count):
-        assert second_hop(first_hop(device)) == reverse_bits(device, device_bits)
-
     def leaf_call(chunk):
         kernel = functools.partial(leaf_kernel, chunk)
         scratch = [held, pltpu.VMEM((boxes, rank, points), BF), sems, wide]
         return call(kernel, forward_shape, [HBM, HBM, ANY], VMEM, scratch, flops, 2 * moved, 8)
 
+    whole = [
+        pltpu.VMEM((total, boxes, points), BF), sems, pltpu.VMEM((total * boxes, points), F32)
+    ]
+
+    def order_call(*operands):
+        return call(
+            order_kernel, shape(boxes, total, points), [HBM, ANY], VMEM, whole, 0, 2 * moved, 8
+        )(*operands)
+
     def target_call(chunk, *operands):
         kernel = functools.partial(target_kernel, chunk)
-        specs = [VMEM, VMEM, HBM, ANY] + [HBM] * (len(operands) - 4)
-        return call(
-            kernel, (full_shape, pair_shape), specs, (HBM, VMEM), [held, sems, wide, wide],
-            2 * flops, 4 * moved, 8, {4: 0} if len(operands) > 4 else None,
+        return call(
+            kernel, (shape(boxes, vectors, points), pair_shape), [VMEM] * 3 + [ANY],
+            (VMEM, VMEM), [], 2 * flops, 4 * moved, 8,
+        )(*operands)
+
+    def residual_call(*operands):
+        return call(
+            functools.partial(residual_kernel, CHUNKS), (full_shape, shape(8, LANES, dtype=F32)),
+            [VMEM] * CHUNKS + [ANY], (HBM, VMEM), whole, 0, 2 * moved, 8,
         )(*operands)
 
     def gradient_call(chunk, *operands):
@@ -387,13 +389,15 @@
             coeffs[c] = token = cross_call(
                 level, coeffs[c], exchange(coeffs[c], level), maps, token
             )
+        if level == 2:
+            wanted = token = order_call(wanted, token)
     for c in every:
         coeffs[c] = token = local_forward_call(
             coeffs[c], exchange(coeffs[c], top), levels, token
         )
-    residual = ()
+    residual = [None] * CHUNKS
     for c in every:
-        *residual, sent[c] = target_call(c, reversal(coeffs[c]), final, wanted, token, *residual)
+        residual[c], sent[c] = target_call(c, reversal(coeffs[c]), final, wanted, token)
         token = sent[c]
     for c in every:
         kept[c], sent[c] = local_adjoint_call(reversal(sent[c]), levels, token)
@@ -404,7 +408,8 @@
                 level, kept[c], exchange(sent[c], level + 1), levels, token
             )
             token = sent[c]
-    residual = residual[0]
+        if level == top - 2:
+            residual, token = residual_call(*residual, token)
     gradient = ()
     for c in every:
         gradient = [gradient_call(c, kept[c], exchange(sent[c], 0), leaf, *gradient)]

time: 205 us -> 194 us (0.946)
  waiting for transfers between devices: 74.2 us -> 59 us
  starting transfers between devices: 92.3 us -> 94.7 us
  Pallas kernels: 32.1 us -> 34.2 us
    ppermute x28, waiting for transfers between devices: 68.8 us -> 55.2 us  [exchange(): return lax.ppermute(array, axis, [(i, i ^ 1 << bit) for i in range(count)])]
    ppermute x28, starting transfers between devices: 76.7 us -> 79.5 us  [exchange(): return lax.ppermute(array, axis, [(i, i ^ 1 << bit) for i in range(count)])]
    pallas_call x2 -> x4, Pallas kernels: 7.01 us -> 9.09 us  [the longest x2 4.55 us: target_call(): call(kernel, (shape(boxes, vectors, points), pair_shape), [VMEM] * 3 + [A...]
    ppermute x8 -> x4, waiting for transfers between devices: 5.45 us -> 3.76 us  [reversal(): return lax.ppermute(array, ('src', 'hi'), pairs_of)]
    ppermute x8 -> x4, starting transfers between devices: 15.6 us -> 15.2 us  [reversal(): return lax.ppermute(array, ('src', 'hi'), pairs_of)]
  transfers between devices with their start and end apart: 36 -> 32, of which waited for: 23 -> 18; matrix products, arithmetic and copies ran while one was open for 1% -> 1% of each run, Pallas kernels for 14% -> 16%
where the time goes in v1:
time: 194 us
  starting transfers between devices  94.7 us (49%)
  waiting for transfers between devices  59 us (30%)
  Pallas kernels  34.2 us (18%)
  local copies, waits for them, and re-layouts  4.56 us (2%)
    ppermute x28, starting transfers between devices, exchange(): return lax.ppermute(array, axis, [(i, i ^ 1 << bit) for i in range(count)])  79.5 us
    ppermute x28, waiting for transfers between devices, exchange(): return lax.ppermute(array, axis, [(i, i ^ 1 << bit) for i in range(count)])  55.2 us
    ppermute x4, starting transfers between devices, reversal(): return lax.ppermute(array, ('src', 'hi'), pairs_of)  15.2 us
    pallas_call x12, Pallas kernels, adjoint_call(): call(kernel, (kept_shape, pair_shape), specs, (VMEM, VMEM), [], flops, mo...  5.84 us
    pallas_call x12, Pallas kernels, cross_call(): call(kernel, forward_shape, specs, VMEM, [], flops, moved, 4)(*operands)  5.16 us
    pallas_call x2, Pallas kernels, target_call(): call(kernel, (shape(boxes, vectors, points), pair_shape), [VMEM] * 3 + [A...  4.55 us
    pallas_call x2, Pallas kernels, local_adjoint_call(): call(kernel, (kept_shape, pair_shape), [VMEM] * 2 + [ANY], (VMEM, VMEM),...  4.24 us
    pallas_call x2, Pallas kernels, local_forward_call(): call(kernel, forward_shape, [VMEM] * 3 + [ANY], VMEM, scratch, 7 * flops,...  4.22 us
  transfers between devices with their start and end apart: 32, of which 18 were waited for; matrix products, arithmetic and copies ran while one was open for 1% of the time, Pallas kernels for 16%

profile of v1, /device:TPU:1, one launch (start us, length us, event | category | flops | bytes accessed | tf_op | source)
XLA Modules:
  0.0 193.7 jit_solution(18041269649945977607)
XLA Ops:
  11.3 5.4 %collective-permute-done.1.other = bf16[16,64,128]{2,1,0:T(8,128)(2,1)S(1)} collective-permute-done((bf16[16,64,128]{2,1,0:T(8,128)(2,1)S(1)}, bf16[16,64,128]{2,1,0:T(8,128)(2,1)S(1)}, u32[]{:S(2)}, u32[]{:S(2)}) %collective-permute-start.1) | collective-permute-done | bytes 262176 | tf_op jit(solution)/shard_map/ppermute | solution.py:306
  17.2 2.9 %collective-permute-start.3 = (bf16[16,64,128]{2,1,0:T(8,128)(2,1)S(1)}, bf16[16,64,128]{2,1,0:T(8,128)(2,1)S(1)}, u32[]{:S(2)}, u32[]{:S(2)}) collective-permute-start(bf16[16,64,128]{2,1,0:T(8,128)(2,1)S(1)} %shard_map.72.refs_0_.own), channel_id=1, source_target_pairs={{0,8},{2,10},{4,12},{6,14},{8,0},{10,2},{12,4},{14,6},{16,24},{18,... | collective-permute-start | bytes 786440 | tf_op jit(solution)/shard_map/ppermute | solution.py:306
  20.1 2.3 %collective-permute-done.4.other = bf16[16,64,128]{2,1,0:T(8,128)(2,1)S(1)} collective-permute-done((bf16[16,64,128]{2,1,0:T(8,128)(2,1)S(1)}, bf16[16,64,128]{2,1,0:T(8,128)(2,1)S(1)}, u32[]{:S(2)}, u32[]{:S(2)}) %collective-permute-start.4) | collective-permute-done | bytes 262176 | tf_op jit(solution)/shard_map/ppermute | solution.py:306
  22.8 2.9 %collective-permute-start.6 = (bf16[16,64,128]{2,1,0:T(8,128)(2,1)S(1)}, bf16[16,64,128]{2,1,0:T(8,128)(2,1)S(1)}, u32[]{:S(2)}, u32[]{:S(2)}) collective-permute-start(bf16[16,64,128]{2,1,0:T(8,128)(2,1)S(1)} %shard_map.73.refs_0_.own), channel_id=1, source_target_pairs={{0,8},{2,10},{4,12},{6,14},{8,0},{10,2},{12,4},{14,6},{16,24},{18,... | collective-permute-start | bytes 786440 | tf_op jit(solution)/shard_map/ppermute | solution.py:306
  25.7 4.5 %collective-permute-done.3.other = bf16[16,64,128]{2,1,0:T(8,128)(2,1)S(1)} collective-permute-done((bf16[16,64,128]{2,1,0:T(8,128)(2,1)S(1)}, bf16[16,64,128]{2,1,0:T(8,128)(2,1)S(1)}, u32[]{:S(2)}, u32[]{:S(2)}) %collective-permute-start.3) | collective-permute-done | bytes 262176 | tf_op jit(solution)/shard_map/ppermute | solution.py:306
  30.7 3.7 %collective-permute-start.5 = (bf16[16,64,128]{2,1,0:T(8,128)(2,1)S(1)}, bf16[16,64,128]{2,1,0:T(8,128)(2,1)S(1)}, u32[]{:S(2)}, u32[]{:S(2)}) collective-permute-start(bf16[16,64,128]{2,1,0:T(8,128)(2,1)S(1)} %shard_map.74.refs_0_.own), channel_id=1, source_target_pairs={{0,16},{2,18},{4,20},{6,22},{8,24},{10,26},{12,28},{14,30},{16,0},... | collective-permute-start | bytes 786440 | tf_op jit(solution)/shard_map/ppermute | solution.py:306
  36.3 3.7 %collective-permute-start.8 = (bf16[16,64,128]{2,1,0:T(8,128)(2,1)S(1)}, bf16[16,64,128]{2,1,0:T(8,128)(2,1)S(1)}, u32[]{:S(2)}, u32[]{:S(2)}) collective-permute-start(bf16[16,64,128]{2,1,0:T(8,128)(2,1)S(1)} %shard_map.75.token.own), channel_id=1, source_target_pairs={{0,16},{2,18},{4,20},{6,22},{8,24},{10,26},{12,28},{14,30},{16,0},... | collective-permute-start | bytes 786440 | tf_op jit(solution)/shard_map/ppermute | solution.py:306
  48.5 3.0 %collective-permute-start.9 = (bf16[16,64,128]{2,1,0:T(8,128)(2,1)S(1)}, bf16[16,64,128]{2,1,0:T(8,128)(2,1)S(1)}, u32[]{:S(2)}, u32[]{:S(2)}) collective-permute-start(bf16[16,64,128]{2,1,0:T(8,128)(2,1)S(1)} %shard_map.79.refs_0_.own), channel_id=1, source_target_pairs={{0,64},{2,66},{4,68},{6,70},{8,72},{10,74},{12,76},{14,78},{16,80}... | collective-permute-start | bytes 786440 | tf_op jit(solution)/shard_map/ppermute | solution.py:306
  51.5 2.7 %collective-permute-done.10.other = bf16[16,64,128]{2,1,0:T(8,128)(2,1)S(1)} collective-permute-done((bf16[16,64,128]{2,1,0:T(8,128)(2,1)S(1)}, bf16[16,64,128]{2,1,0:T(8,128)(2,1)S(1)}, u32[]{:S(2)}, u32[]{:S(2)}) %collective-permute-start.10) | collective-permute-done | bytes 262176 | tf_op jit(solution)/shard_map/ppermute | solution.py:306
  54.6 3.0 %collective-permute-start.12 = (bf16[16,64,128]{2,1,0:T(8,128)(2,1)S(1)}, bf16[16,64,128]{2,1,0:T(8,128)(2,1)S(1)}, u32[]{:S(2)}, u32[]{:S(2)}) collective-permute-start(bf16[16,64,128]{2,1,0:T(8,128)(2,1)S(1)} %shard_map.80.refs_0_.own), channel_id=1, source_target_pairs={{0,64},{2,66},{4,68},{6,70},{8,72},{10,74},{12,76},{14,78},{16,80}... | collective-permute-start | bytes 786440 | tf_op jit(solution)/shard_map/ppermute | solution.py:306
  57.6 4.6 %collective-permute-done.9.other = bf16[16,64,128]{2,1,0:T(8,128)(2,1)S(1)} collective-permute-done((bf16[16,64,128]{2,1,0:T(8,128)(2,1)S(1)}, bf16[16,64,128]{2,1,0:T(8,128)(2,1)S(1)}, u32[]{:S(2)}, u32[]{:S(2)}) %collective-permute-start.9) | collective-permute-done | bytes 262176 | tf_op jit(solution)/shard_map/ppermute | solution.py:306
  63.5 4.4 %collective-permute-done.12.other = bf16[16,64,128]{2,1,0:T(8,128)(2,1)S(1)} collective-permute-done((bf16[16,64,128]{2,1,0:T(8,128)(2,1)S(1)}, bf16[16,64,128]{2,1,0:T(8,128)(2,1)S(1)}, u32[]{:S(2)}, u32[]{:S(2)}) %collective-permute-start.12) | collective-permute-done | bytes 262176 | tf_op jit(solution)/shard_map/ppermute | solution.py:306
  71.4 7.3 %collective-permute-start.13 = (bf16[16,64,128]{2,1,0:T(8,128)(2,1)S(1)}, bf16[16,64,128]{2,1,0:T(8,128)(2,1)S(1)}, u32[]{:S(2)}, u32[]{:S(2)}) collective-permute-start(bf16[16,64,128]{2,1,0:T(8,128)(2,1)S(1)} %shard_map.83.token), channel_id=1, source_target_pairs={{0,0},{1,2},{2,1},{3,3},{4,64},{5,66},{6,65},{7,67},{8,32},{9,34},... | collective-permute-start | bytes 786440 | tf_op jit(solution)/shard_map/ppermute | solution.py:316
  80.8 2.3 %collective-permute-start.15 = (bf16[16,64,128]{2,1,0:T(8,128)(2,1)S(1)}, bf16[16,64,128]{2,1,0:T(8,128)(2,1)S(1)}, u32[]{:S(2)}, u32[]{:S(2)}) collective-permute-start(bf16[16,64,128]{2,1,0:T(8,128)(2,1)S(1)} %shard_map.84.token), channel_id=1, source_target_pairs={{0,0},{1,2},{2,1},{3,3},{4,64},{5,66},{6,65},{7,67},{8,32},{9,34},... | collective-permute-start | bytes 786440 | tf_op jit(solution)/shard_map/ppermute | solution.py:316
  83.2 2.3 %shard_map.85 = (bf16[64,32,128]{2,1,0:T(8,128)(2,1)S(1)}, bf16[32,32,128]{2,1,0:T(8,128)(2,1)S(1)}) custom-call(bf16[16,64,128]{2,1,0:T(8,128)(2,1)S(1)} %collective-permute-done.13.coeffs, bf16[64,64,128]{2,1,0:T(8,128)(2,1)S(1)} %bitcast.48, bf16[64,64,128]{2,1,0:T(8,128)(2,1)S(1)} %shard_map.76.refs_0_.wanted, bf16[16,64,128]{2,1,0:T(8,128)(2,1)S(1)} %shard_map.84.token), custom_call_target="tpu_custom_call" | custom-call | flops 67108864 | bytes 4194304 | tf_op jit(solution)/shard_map/pallas_call | solution.py:334
  85.5 3.2 %collective-permute-start.17 = (bf16[32,32,128]{2,1,0:T(8,128)(2,1)S(1)}, bf16[32,32,128]{2,1,0:T(8,128)(2,1)S(1)}, u32[]{:S(2)}, u32[]{:S(2)}) collective-permute-start(bf16[32,32,128]{2,1,0:T(8,128)(2,1)S(1)} %get-tuple-element.37.token), channel_id=1, source_target_pairs={{0,0},{1,2},{2,1},{3,3},{4,64},{5,66},{6,65},{7,67},{8,32},{9,34},... | collective-permute-start | bytes 786440 | tf_op jit(solution)/shard_map/ppermute | solution.py:316
  88.7 2.3 %shard_map.86 = (bf16[64,32,128]{2,1,0:T(8,128)(2,1)S(1)}, bf16[32,32,128]{2,1,0:T(8,128)(2,1)S(1)}) custom-call(bf16[16,64,128]{2,1,0:T(8,128)(2,1)S(1)} %collective-permute-done.15.coeffs, bf16[64,64,128]{2,1,0:T(8,128)(2,1)S(1)} %bitcast.49, bf16[64,64,128]{2,1,0:T(8,128)(2,1)S(1)} %shard_map.76.refs_0_.wanted, ...), custom_call_target="tpu_custom_call" | custom-call | flops 67108864 | bytes 4194304 | tf_op jit(solution)/shard_map/pallas_call | solution.py:334
  91.0 2.3 %collective-permute-start.16 = (bf16[32,32,128]{2,1,0:T(8,128)(2,1)S(1)}, bf16[32,32,128]{2,1,0:T(8,128)(2,1)S(1)}, u32[]{:S(2)}, u32[]{:S(2)}) collective-permute-start(bf16[32,32,128]{2,1,0:T(8,128)(2,1)S(1)} %get-tuple-element.39.token), channel_id=1, source_target_pairs={{0,0},{1,2},{2,1},{3,3},{4,64},{5,66},{6,65},{7,67},{8,32},{9,34},... | collective-permute-start | bytes 786440 | tf_op jit(solution)/shard_map/ppermute | solution.py:316
  93.3 2.1 %shard_map.87 = (f32[32,32,128]{2,1,0:T(8,128)S(1)}, bf16[32,32,128]{2,1,0:T(8,128)(2,1)S(1)}) custom-call(bf16[32,32,128]{2,1,0:T(8,128)(2,1)S(1)} %collective-permute-done.17.adjoint, bf16[13,64,64,128]{3,2,1,0:T(8,128)(2,1)S(1)} %bitcast.27, bf16[32,32,128]{2,1,0:T(8,128)(2,1)S(1)} %get-tuple-element.39.token), custom_call_target="tpu_custom_call" | custom-call | flops 234881024 | bytes 7340032 | tf_op jit(solution)/shard_map/pallas_call | solution.py:375
  95.6 3.8 %collective-permute-done.16.adjoint = bf16[32,32,128]{2,1,0:T(8,128)(2,1)S(1)} collective-permute-done((bf16[32,32,128]{2,1,0:T(8,128)(2,1)S(1)}, bf16[32,32,128]{2,1,0:T(8,128)(2,1)S(1)}, u32[]{:S(2)}, u32[]{:S(2)}) %collective-permute-start.16) | collective-permute-done | bytes 262176 | tf_op jit(solution)/shard_map/ppermute | solution.py:316
  101.5 2.4 %collective-permute-done.19.received = bf16[32,32,128]{2,1,0:T(8,128)(2,1)S(1)} collective-permute-done((bf16[32,32,128]{2,1,0:T(8,128)(2,1)S(1)}, bf16[32,32,128]{2,1,0:T(8,128)(2,1)S(1)}, u32[]{:S(2)}, u32[]{:S(2)}) %collective-permute-start.19) | collective-permute-done | bytes 262176 | tf_op jit(solution)/shard_map/ppermute | solution.py:306
  104.4 24.7 %collective-permute-start.21 = (bf16[32,32,128]{2,1,0:T(8,128)(2,1)S(1)}, bf16[32,32,128]{2,1,0:T(8,128)(2,1)S(1)}, u32[]{:S(2)}, u32[]{:S(2)}) collective-permute-start(bf16[32,32,128]{2,1,0:T(8,128)(2,1)S(1)} %get-tuple-element.44.refs_0_), channel_id=1, source_target_pairs={{0,64},{2,66},{4,68},{6,70},{8,72},{10,74},{12,76},{14,78},{16,80}... | collective-permute-start | bytes 786440 | tf_op jit(solution)/shard_map/ppermute | solution.py:306
  129.6 5.9 %collective-permute-start.20 = (bf16[32,32,128]{2,1,0:T(8,128)(2,1)S(1)}, bf16[32,32,128]{2,1,0:T(8,128)(2,1)S(1)}, u32[]{:S(2)}, u32[]{:S(2)}) collective-permute-start(bf16[32,32,128]{2,1,0:T(8,128)(2,1)S(1)} %get-tuple-element.46.refs_0_), channel_id=1, source_target_pairs={{0,64},{2,66},{4,68},{6,70},{8,72},{10,74},{12,76},{14,78},{16,80}... | collective-permute-start | bytes 786440 | tf_op jit(solution)/shard_map/ppermute | solution.py:306
  137.2 4.9 %collective-permute-done.20.received = bf16[32,32,128]{2,1,0:T(8,128)(2,1)S(1)} collective-permute-done((bf16[32,32,128]{2,1,0:T(8,128)(2,1)S(1)}, bf16[32,32,128]{2,1,0:T(8,128)(2,1)S(1)}, u32[]{:S(2)}, u32[]{:S(2)}) %collective-permute-start.20) | collective-permute-done | bytes 262176 | tf_op jit(solution)/shard_map/ppermute | solution.py:306
  144.1 3.2 %shard_map.93 = (bf16[64,64,128]{2,1,0:T(8,128)(2,1)}, f32[8,128]{1,0:T(8,128)S(1)}) custom-call(bf16[64,32,128]{2,1,0:T(8,128)(2,1)S(1)} %get-tuple-element.36.refs_0_, bf16[64,32,128]{2,1,0:T(8,128)(2,1)S(1)} %get-tuple-element.38.refs_1_, bf16[32,32,128]{2,1,0:T(8,128)(2,1)S(1)} %get-tuple-element.49.refs_2_), custom_call_target="tpu_custom_call" | custom-call | bytes 2097152 | tf_op jit(solution)/shard_map/pallas_call | solution.py:340
  149.5 3.0 %collective-permute-start.25 = (bf16[32,32,128]{2,1,0:T(8,128)(2,1)S(1)}, bf16[32,32,128]{2,1,0:T(8,128)(2,1)S(1)}, u32[]{:S(2)}, u32[]{:S(2)}) collective-permute-start(bf16[32,32,128]{2,1,0:T(8,128)(2,1)S(1)} %get-tuple-element.54.refs_0_), channel_id=1, source_target_pairs={{0,16},{2,18},{4,20},{6,22},{8,24},{10,26},{12,28},{14,30},{16,0},... | collective-permute-start | bytes 786440 | tf_op jit(solution)/shard_map/ppermute | solution.py:306
  155.2 3.0 %collective-permute-start.24 = (bf16[32,32,128]{2,1,0:T(8,128)(2,1)S(1)}, bf16[32,32,128]{2,1,0:T(8,128)(2,1)S(1)}, u32[]{:S(2)}, u32[]{:S(2)}) collective-permute-start(bf16[32,32,128]{2,1,0:T(8,128)(2,1)S(1)} %get-tuple-element.56.refs_0_), channel_id=1, source_target_pairs={{0,16},{2,18},{4,20},{6,22},{8,24},{10,26},{12,28},{14,30},{16,0},... | collective-permute-start | bytes 786440 | tf_op jit(solution)/shard_map/ppermute | solution.py:306
  160.1 4.9 %collective-permute-done.24.received = bf16[32,32,128]{2,1,0:T(8,128)(2,1)S(1)} collective-permute-done((bf16[32,32,128]{2,1,0:T(8,128)(2,1)S(1)}, bf16[32,32,128]{2,1,0:T(8,128)(2,1)S(1)}, u32[]{:S(2)}, u32[]{:S(2)}) %collective-permute-start.24) | collective-permute-done | bytes 262176 | tf_op jit(solution)/shard_map/ppermute | solution.py:306
  168.1 6.2 %collective-permute-done.26.received = bf16[32,32,128]{2,1,0:T(8,128)(2,1)S(1)} collective-permute-done((bf16[32,32,128]{2,1,0:T(8,128)(2,1)S(1)}, bf16[32,32,128]{2,1,0:T(8,128)(2,1)S(1)}, u32[]{:S(2)}, u32[]{:S(2)}) %collective-permute-start.26) | collective-permute-done | bytes 262176 | tf_op jit(solution)/shard_map/ppermute | solution.py:306
  175.0 4.2 %collective-permute-done.29.received = bf16[32,32,128]{2,1,0:T(8,128)(2,1)S(1)} collective-permute-done((bf16[32,32,128]{2,1,0:T(8,128)(2,1)S(1)}, bf16[32,32,128]{2,1,0:T(8,128)(2,1)S(1)}, u32[]{:S(2)}, u32[]{:S(2)}) %collective-permute-start.29) | collective-permute-done | bytes 262176 | tf_op jit(solution)/shard_map/ppermute | solution.py:306
  179.6 7.0 %collective-permute-start.31 = (bf16[32,32,128]{2,1,0:T(8,128)(2,1)S(1)}, bf16[32,32,128]{2,1,0:T(8,128)(2,1)S(1)}, u32[]{:S(2)}, u32[]{:S(2)}) collective-permute-start(bf16[32,32,128]{2,1,0:T(8,128)(2,1)S(1)} %get-tuple-element.66.refs_0_), channel_id=1, source_target_pairs={{0,2},{2,0},{4,6},{6,4},{8,10},{10,8},{12,14},{14,12},{16,18},{18,... | collective-permute-start | bytes 786440 | tf_op jit(solution)/shard_map/ppermute | solution.py:306
  187.1 2.7 %collective-permute-start.30 = (bf16[32,32,128]{2,1,0:T(8,128)(2,1)S(1)}, bf16[32,32,128]{2,1,0:T(8,128)(2,1)S(1)}, u32[]{:S(2)}, u32[]{:S(2)}) collective-permute-start(bf16[32,32,128]{2,1,0:T(8,128)(2,1)S(1)} %get-tuple-element.68), channel_id=1, source_target_pairs={{0,2},{2,0},{4,6},{6,4},{8,10},{10,8},{12,14},{14,12},{16,18},{18,... | collective-permute-start | bytes 786440 | tf_op jit(solution)/shard_map/ppermute | solution.py:306
  (81 shorter events, 51.7 us)
Async XLA Ops:
  4.5 4.3 %collective-permute-start = (bf16[16,64,128]{2,1,0:T(8,128)(2,1)S(1)}, bf16[16,64,128]{2,1,0:T(8,128)(2,1)S(1)}, u32[]{:S(2)}, u32[]{:S(2)}) collective-permute-start(bf16[16,64,128]{2,1,0:T(8,128)(2,1)S(1)} %shard_map.68.token.own), channel_id=1, source_target_pairs={{0,2},{2,0},{4,6},{6,4},{8,10},{10,8},{12,14},{14,12},{16,18},{18,... | collective-permute-start | bytes 786440 | tf_op jit(solution)/shard_map/ppermute | solution.py:306
  7.0 3.6 %collective-permute-start.2 = (bf16[16,64,128]{2,1,0:T(8,128)(2,1)S(1)}, bf16[16,64,128]{2,1,0:T(8,128)(2,1)S(1)}, u32[]{:S(2)}, u32[]{:S(2)}) collective-permute-start(bf16[16,64,128]{2,1,0:T(8,128)(2,1)S(1)} %shard_map.69.refs_0_.own), channel_id=1, source_target_pairs={{0,2},{2,0},{4,6},{6,4},{8,10},{10,8},{12,14},{14,12},{16,18},{18,... | collective-permute-start | bytes 786440 | tf_op jit(solution)/shard_map/ppermute | solution.py:306
  9.3 7.5 %collective-permute-start.1 = (bf16[16,64,128]{2,1,0:T(8,128)(2,1)S(1)}, bf16[16,64,128]{2,1,0:T(8,128)(2,1)S(1)}, u32[]{:S(2)}, u32[]{:S(2)}) collective-permute-start(bf16[16,64,128]{2,1,0:T(8,128)(2,1)S(1)} %shard_map.70.refs_0_.own), channel_id=1, source_target_pairs={{0,4},{2,6},{4,0},{6,2},{8,12},{10,14},{12,8},{14,10},{16,20},{18,... | collective-permute-start | bytes 786440 | tf_op jit(solution)/shard_map/ppermute | solution.py:306
  11.1 11.3 %collective-permute-start.4 = (bf16[16,64,128]{2,1,0:T(8,128)(2,1)S(1)}, bf16[16,64,128]{2,1,0:T(8,128)(2,1)S(1)}, u32[]{:S(2)}, u32[]{:S(2)}) collective-permute-start(bf16[16,64,128]{2,1,0:T(8,128)(2,1)S(1)} %shard_map.71.refs_0_.own), channel_id=1, source_target_pairs={{0,4},{2,6},{4,0},{6,2},{8,12},{10,14},{12,8},{14,10},{16,20},{18,... | collective-permute-start | bytes 786440 | tf_op jit(solution)/shard_map/ppermute | solution.py:306
  17.2 13.1 %collective-permute-start.3 = (bf16[16,64,128]{2,1,0:T(8,128)(2,1)S(1)}, bf16[16,64,128]{2,1,0:T(8,128)(2,1)S(1)}, u32[]{:S(2)}, u32[]{:S(2)}) collective-permute-start(bf16[16,64,128]{2,1,0:T(8,128)(2,1)S(1)} %shard_map.72.refs_0_.own), channel_id=1, source_target_pairs={{0,8},{2,10},{4,12},{6,14},{8,0},{10,2},{12,4},{14,6},{16,24},{18,... | collective-permute-start | bytes 786440 | tf_op jit(solution)/shard_map/ppermute | solution.py:306
  22.8 13.1 %collective-permute-start.6 = (bf16[16,64,128]{2,1,0:T(8,128)(2,1)S(1)}, bf16[16,64,128]{2,1,0:T(8,128)(2,1)S(1)}, u32[]{:S(2)}, u32[]{:S(2)}) collective-permute-start(bf16[16,64,128]{2,1,0:T(8,128)(2,1)S(1)} %shard_map.73.refs_0_.own), channel_id=1, source_target_pairs={{0,8},{2,10},{4,12},{6,14},{8,0},{10,2},{12,4},{14,6},{16,24},{18,... | collective-permute-start | bytes 786440 | tf_op jit(solution)/shard_map/ppermute | solution.py:306
  30.7 10.7 %collective-permute-start.5 = (bf16[16,64,128]{2,1,0:T(8,128)(2,1)S(1)}, bf16[16,64,128]{2,1,0:T(8,128)(2,1)S(1)}, u32[]{:S(2)}, u32[]{:S(2)}) collective-permute-start(bf16[16,64,128]{2,1,0:T(8,128)(2,1)S(1)} %shard_map.74.refs_0_.own), channel_id=1, source_target_pairs={{0,16},{2,18},{4,20},{6,22},{8,24},{10,26},{12,28},{14,30},{16,0},... | collective-permute-start | bytes 786440 | tf_op jit(solution)/shard_map/ppermute | solution.py:306
  36.3 9.0 %collective-permute-start.8 = (bf16[16,64,128]{2,1,0:T(8,128)(2,1)S(1)}, bf16[16,64,128]{2,1,0:T(8,128)(2,1)S(1)}, u32[]{:S(2)}, u32[]{:S(2)}) collective-permute-start(bf16[16,64,128]{2,1,0:T(8,128)(2,1)S(1)} %shard_map.75.token.own), channel_id=1, source_target_pairs={{0,16},{2,18},{4,20},{6,22},{8,24},{10,26},{12,28},{14,30},{16,0},... | collective-permute-start | bytes 786440 | tf_op jit(solution)/shard_map/ppermute | solution.py:306
  41.8 6.3 %collective-permute-start.7 = (bf16[16,64,128]{2,1,0:T(8,128)(2,1)S(1)}, bf16[16,64,128]{2,1,0:T(8,128)(2,1)S(1)}, u32[]{:S(2)}, u32[]{:S(2)}) collective-permute-start(bf16[16,64,128]{2,1,0:T(8,128)(2,1)S(1)} %shard_map.77.refs_0_.own), channel_id=1, source_target_pairs={{0,32},{2,34},{4,36},{6,38},{8,40},{10,42},{12,44},{14,46},{16,48}... | collective-permute-start | bytes 786440 | tf_op jit(solution)/shard_map/ppermute | solution.py:306
  45.7 8.5 %collective-permute-start.10 = (bf16[16,64,128]{2,1,0:T(8,128)(2,1)S(1)}, bf16[16,64,128]{2,1,0:T(8,128)(2,1)S(1)}, u32[]{:S(2)}, u32[]{:S(2)}) collective-permute-start(bf16[16,64,128]{2,1,0:T(8,128)(2,1)S(1)} %shard_map.78.refs_0_.own), channel_id=1, source_target_pairs={{0,32},{2,34},{4,36},{6,38},{8,40},{10,42},{12,44},{14,46},{16,48}... | collective-permute-start | bytes 786440 | tf_op jit(solution)/shard_map/ppermute | solution.py:306
  48.5 13.7 %collective-permute-start.9 = (bf16[16,64,128]{2,1,0:T(8,128)(2,1)S(1)}, bf16[16,64,128]{2,1,0:T(8,128)(2,1)S(1)}, u32[]{:S(2)}, u32[]{:S(2)}) collective-permute-start(bf16[16,64,128]{2,1,0:T(8,128)(2,1)S(1)} %shard_map.79.refs_0_.own), channel_id=1, source_target_pairs={{0,64},{2,66},{4,68},{6,70},{8,72},{10,74},{12,76},{14,78},{16,80}... | collective-permute-start | bytes 786440 | tf_op jit(solution)/shard_map/ppermute | solution.py:306
  54.6 13.2 %collective-permute-start.12 = (bf16[16,64,128]{2,1,0:T(8,128)(2,1)S(1)}, bf16[16,64,128]{2,1,0:T(8,128)(2,1)S(1)}, u32[]{:S(2)}, u32[]{:S(2)}) collective-permute-start(bf16[16,64,128]{2,1,0:T(8,128)(2,1)S(1)} %shard_map.80.refs_0_.own), channel_id=1, source_target_pairs={{0,64},{2,66},{4,68},{6,70},{8,72},{10,74},{12,76},{14,78},{16,80}... | collective-permute-start | bytes 786440 | tf_op jit(solution)/shard_map/ppermute | solution.py:306
  62.7 6.6 %collective-permute-start.11 = (bf16[16,64,128]{2,1,0:T(8,128)(2,1)S(1)}, bf16[16,64,128]{2,1,0:T(8,128)(2,1)S(1)}, u32[]{:S(2)}, u32[]{:S(2)}) collective-permute-start(bf16[16,64,128]{2,1,0:T(8,128)(2,1)S(1)} %shard_map.81.refs_0_.own), channel_id=1, source_target_pairs={{0,1},{1,0},{2,3},{3,2},{4,5},{5,4},{6,7},{7,6},{8,9},{9,8},{10,11... | collective-permute-start | bytes 786440 | tf_op jit(solution)/shard_map/ppermute | solution.py:306
  68.3 10.4 %collective-permute-start.14 = (bf16[16,64,128]{2,1,0:T(8,128)(2,1)S(1)}, bf16[16,64,128]{2,1,0:T(8,128)(2,1)S(1)}, u32[]{:S(2)}, u32[]{:S(2)}) collective-permute-start(bf16[16,64,128]{2,1,0:T(8,128)(2,1)S(1)} %shard_map.82.token.own), channel_id=1, source_target_pairs={{0,1},{1,0},{2,3},{3,2},{4,5},{5,4},{6,7},{7,6},{8,9},{9,8},{10,11... | collective-permute-start | bytes 786440 | tf_op jit(solution)/shard_map/ppermute | solution.py:306
  71.4 11.7 %collective-permute-start.13 = (bf16[16,64,128]{2,1,0:T(8,128)(2,1)S(1)}, bf16[16,64,128]{2,1,0:T(8,128)(2,1)S(1)}, u32[]{:S(2)}, u32[]{:S(2)}) collective-permute-start(bf16[16,64,128]{2,1,0:T(8,128)(2,1)S(1)} %shard_map.83.token), channel_id=1, source_target_pairs={{0,0},{1,2},{2,1},{3,3},{4,64},{5,66},{6,65},{7,67},{8,32},{9,34},... | collective-permute-start | bytes 786440 | tf_op jit(solution)/shard_map/ppermute | solution.py:316
  80.8 7.9 %collective-permute-start.15 = (bf16[16,64,128]{2,1,0:T(8,128)(2,1)S(1)}, bf16[16,64,128]{2,1,0:T(8,128)(2,1)S(1)}, u32[]{:S(2)}, u32[]{:S(2)}) collective-permute-start(bf16[16,64,128]{2,1,0:T(8,128)(2,1)S(1)} %shard_map.84.token), channel_id=1, source_target_pairs={{0,0},{1,2},{2,1},{3,3},{4,64},{5,66},{6,65},{7,67},{8,32},{9,34},... | collective-permute-start | bytes 786440 | tf_op jit(solution)/shard_map/ppermute | solution.py:316
  85.5 7.9 %collective-permute-start.17 = (bf16[32,32,128]{2,1,0:T(8,128)(2,1)S(1)}, bf16[32,32,128]{2,1,0:T(8,128)(2,1)S(1)}, u32[]{:S(2)}, u32[]{:S(2)}) collective-permute-start(bf16[32,32,128]{2,1,0:T(8,128)(2,1)S(1)} %get-tuple-element.37.token), channel_id=1, source_target_pairs={{0,0},{1,2},{2,1},{3,3},{4,64},{5,66},{6,65},{7,67},{8,32},{9,34},... | collective-permute-start | bytes 786440 | tf_op jit(solution)/shard_map/ppermute | solution.py:316
  91.0 8.3 %collective-permute-start.16 = (bf16[32,32,128]{2,1,0:T(8,128)(2,1)S(1)}, bf16[32,32,128]{2,1,0:T(8,128)(2,1)S(1)}, u32[]{:S(2)}, u32[]{:S(2)}) collective-permute-start(bf16[32,32,128]{2,1,0:T(8,128)(2,1)S(1)} %get-tuple-element.39.token), channel_id=1, source_target_pairs={{0,0},{1,2},{2,1},{3,3},{4,64},{5,66},{6,65},{7,67},{8,32},{9,34},... | collective-permute-start | bytes 786440 | tf_op jit(solution)/shard_map/ppermute | solution.py:316
  95.5 8.5 %collective-permute-start.19 = (bf16[32,32,128]{2,1,0:T(8,128)(2,1)S(1)}, bf16[32,32,128]{2,1,0:T(8,128)(2,1)S(1)}, u32[]{:S(2)}, u32[]{:S(2)}) collective-permute-start(bf16[32,32,128]{2,1,0:T(8,128)(2,1)S(1)} %get-tuple-element.40.token), channel_id=1, source_target_pairs={{0,1},{1,0},{2,3},{3,2},{4,5},{5,4},{6,7},{7,6},{8,9},{9,8},{10,11... | collective-permute-start | bytes 786440 | tf_op jit(solution)/shard_map/ppermute | solution.py:306
  101.4 27.7 %collective-permute-start.18 = (bf16[32,32,128]{2,1,0:T(8,128)(2,1)S(1)}, bf16[32,32,128]{2,1,0:T(8,128)(2,1)S(1)}, u32[]{:S(2)}, u32[]{:S(2)}) collective-permute-start(bf16[32,32,128]{2,1,0:T(8,128)(2,1)S(1)} %get-tuple-element.42.refs_0_), channel_id=1, source_target_pairs={{0,1},{1,0},{2,3},{3,2},{4,5},{5,4},{6,7},{7,6},{8,9},{9,8},{10,11... | collective-permute-start | bytes 786440 | tf_op jit(solution)/shard_map/ppermute | solution.py:306
  104.4 31.1 %collective-permute-start.21 = (bf16[32,32,128]{2,1,0:T(8,128)(2,1)S(1)}, bf16[32,32,128]{2,1,0:T(8,128)(2,1)S(1)}, u32[]{:S(2)}, u32[]{:S(2)}) collective-permute-start(bf16[32,32,128]{2,1,0:T(8,128)(2,1)S(1)} %get-tuple-element.44.refs_0_), channel_id=1, source_target_pairs={{0,64},{2,66},{4,68},{6,70},{8,72},{10,74},{12,76},{14,78},{16,80}... | collective-permute-start | bytes 786440 | tf_op jit(solution)/shard_map/ppermute | solution.py:306
  129.6 12.5 %collective-permute-start.20 = (bf16[32,32,128]{2,1,0:T(8,128)(2,1)S(1)}, bf16[32,32,128]{2,1,0:T(8,128)(2,1)S(1)}, u32[]{:S(2)}, u32[]{:S(2)}) collective-permute-start(bf16[32,32,128]{2,1,0:T(8,128)(2,1)S(1)} %get-tuple-element.46.refs_0_), channel_id=1, source_target_pairs={{0,64},{2,66},{4,68},{6,70},{8,72},{10,74},{12,76},{14,78},{16,80}... | collective-permute-start | bytes 786440 | tf_op jit(solution)/shard_map/ppermute | solution.py:306
  136.0 13.1 %collective-permute-start.23 = (bf16[32,32,128]{2,1,0:T(8,128)(2,1)S(1)}, bf16[32,32,128]{2,1,0:T(8,128)(2,1)S(1)}, u32[]{:S(2)}, u32[]{:S(2)}) collective-permute-start(bf16[32,32,128]{2,1,0:T(8,128)(2,1)S(1)} %get-tuple-element.48.refs_0_), channel_id=1, source_target_pairs={{0,32},{2,34},{4,36},{6,38},{8,40},{10,42},{12,44},{14,46},{16,48}... | collective-permute-start | bytes 786440 | tf_op jit(solution)/shard_map/ppermute | solution.py:306
  142.6 12.1 %collective-permute-start.22 = (bf16[32,32,128]{2,1,0:T(8,128)(2,1)S(1)}, bf16[32,32,128]{2,1,0:T(8,128)(2,1)S(1)}, u32[]{:S(2)}, u32[]{:S(2)}) collective-permute-start(bf16[32,32,128]{2,1,0:T(8,128)(2,1)S(1)} %get-tuple-element.49.refs_2_), channel_id=1, source_target_pairs={{0,32},{2,34},{4,36},{6,38},{8,40},{10,42},{12,44},{14,46},{16,48}... | collective-permute-start | bytes 786440 | tf_op jit(solution)/shard_map/ppermute | solution.py:306
  149.5 8.6 %collective-permute-start.25 = (bf16[32,32,128]{2,1,0:T(8,128)(2,1)S(1)}, bf16[32,32,128]{2,1,0:T(8,128)(2,1)S(1)}, u32[]{:S(2)}, u32[]{:S(2)}) collective-permute-start(bf16[32,32,128]{2,1,0:T(8,128)(2,1)S(1)} %get-tuple-element.54.refs_0_), channel_id=1, source_target_pairs={{0,16},{2,18},{4,20},{6,22},{8,24},{10,26},{12,28},{14,30},{16,0},... | collective-permute-start | bytes 786440 | tf_op jit(solution)/shard_map/ppermute | solution.py:306
  155.2 9.8 %collective-permute-start.24 = (bf16[32,32,128]{2,1,0:T(8,128)(2,1)S(1)}, bf16[32,32,128]{2,1,0:T(8,128)(2,1)S(1)}, u32[]{:S(2)}, u32[]{:S(2)}) collective-permute-start(bf16[32,32,128]{2,1,0:T(8,128)(2,1)S(1)} %get-tuple-element.56.refs_0_), channel_id=1, source_target_pairs={{0,16},{2,18},{4,20},{6,22},{8,24},{10,26},{12,28},{14,30},{16,0},... | collective-permute-start | bytes 786440 | tf_op jit(solution)/shard_map/ppermute | solution.py:306
  158.7 7.1 %collective-permute-start.27 = (bf16[32,32,128]{2,1,0:T(8,128)(2,1)S(1)}, bf16[32,32,128]{2,1,0:T(8,128)(2,1)S(1)}, u32[]{:S(2)}, u32[]{:S(2)}) collective-permute-start(bf16[32,32,128]{2,1,0:T(8,128)(2,1)S(1)} %get-tuple-element.58.refs_0_), channel_id=1, source_target_pairs={{0,8},{2,10},{4,12},{6,14},{8,0},{10,2},{12,4},{14,6},{16,24},{18,... | collective-permute-start | bytes 786440 | tf_op jit(solution)/shard_map/ppermute | solution.py:306
  165.4 8.9 %collective-permute-start.26 = (bf16[32,32,128]{2,1,0:T(8,128)(2,1)S(1)}, bf16[32,32,128]{2,1,0:T(8,128)(2,1)S(1)}, u32[]{:S(2)}, u32[]{:S(2)}) collective-permute-start(bf16[32,32,128]{2,1,0:T(8,128)(2,1)S(1)} %get-tuple-element.60.refs_0_), channel_id=1, source_target_pairs={{0,8},{2,10},{4,12},{6,14},{8,0},{10,2},{12,4},{14,6},{16,24},{18,... | collective-permute-start | bytes 786440 | tf_op jit(solution)/shard_map/ppermute | solution.py:306
  166.3 12.8 %collective-permute-start.29 = (bf16[32,32,128]{2,1,0:T(8,128)(2,1)S(1)}, bf16[32,32,128]{2,1,0:T(8,128)(2,1)S(1)}, u32[]{:S(2)}, u32[]{:S(2)}) collective-permute-start(bf16[32,32,128]{2,1,0:T(8,128)(2,1)S(1)} %get-tuple-element.62.refs_0_), channel_id=1, source_target_pairs={{0,4},{2,6},{4,0},{6,2},{8,12},{10,14},{12,8},{14,10},{16,20},{18,... | collective-permute-start | bytes 786440 | tf_op jit(solution)/shard_map/ppermute | solution.py:306
  174.9 11.8 %collective-permute-start.28 = (bf16[32,32,128]{2,1,0:T(8,128)(2,1)S(1)}, bf16[32,32,128]{2,1,0:T(8,128)(2,1)S(1)}, u32[]{:S(2)}, u32[]{:S(2)}) collective-permute-start(bf16[32,32,128]{2,1,0:T(8,128)(2,1)S(1)} %get-tuple-element.64.refs_0_), channel_id=1, source_target_pairs={{0,4},{2,6},{4,0},{6,2},{8,12},{10,14},{12,8},{14,10},{16,20},{18,... | collective-permute-start | bytes 786440 | tf_op jit(solution)/shard_map/ppermute | solution.py:306
  179.6 10.2 %collective-permute-start.31 = (bf16[32,32,128]{2,1,0:T(8,128)(2,1)S(1)}, bf16[32,32,128]{2,1,0:T(8,128)(2,1)S(1)}, u32[]{:S(2)}, u32[]{:S(2)}) collective-permute-start(bf16[32,32,128]{2,1,0:T(8,128)(2,1)S(1)} %get-tuple-element.66.refs_0_), channel_id=1, source_target_pairs={{0,2},{2,0},{4,6},{6,4},{8,10},{10,8},{12,14},{14,12},{16,18},{18,... | collective-permute-start | bytes 786440 | tf_op jit(solution)/shard_map/ppermute | solution.py:306
  187.1 4.5 %collective-permute-start.30 = (bf16[32,32,128]{2,1,0:T(8,128)(2,1)S(1)}, bf16[32,32,128]{2,1,0:T(8,128)(2,1)S(1)}, u32[]{:S(2)}, u32[]{:S(2)}) collective-permute-start(bf16[32,32,128]{2,1,0:T(8,128)(2,1)S(1)} %get-tuple-element.68), channel_id=1, source_target_pairs={{0,2},{2,0},{4,6},{6,4},{8,10},{10,8},{12,14},{14,12},{16,18},{18,... | collective-permute-start | bytes 786440 | tf_op jit(solution)/shard_map/ppermute | solution.py:306
  (6 other events, 67.8 us)

commit v2 on v1

--- a/solution.py
+++ b/solution.py
@@ -8,6 +8,10 @@
 from jax.sharding import PartitionSpec as P
 
 CHUNKS = 2
+PARTS = 4
+EARLY = 2
+LAG = 0
+GAP = 2
 LANES = 128
 BF = jnp.bfloat16
 F32 = jnp.float32
@@ -57,26 +61,36 @@
     return lax.dot_general(a, b, (((1,), (1,)), ((), ())), preferred_element_type=F32)
 
 
-def leaf_kernel(chunk, traces, leaf, token, out, held, mats, sems, wide):
-    vectors, boxes, points = held.shape
+def leaf_kernel(chunks, traces, leaf, *refs):
+    outs = refs[:chunks]
+    held, mats, sems, wide = refs[chunks:]
+    total, boxes, points = held.shape
+    vectors = total // chunks
     lane_boxes = LANES // vectors
     rank = mats.shape[1]
     copies = [
-        pltpu.make_async_copy(traces.at[pl.ds(chunk * vectors, vectors)], held, sems.at[0]),
-        pltpu.make_async_copy(leaf, mats, sems.at[1]),
+        pltpu.make_async_copy(
+            traces.at[pl.ds(c * vectors, vectors)], held.at[pl.ds(c * vectors, vectors)], sems.at[c]
+        )
+        for c in range(chunks)
     ]
+    copies.append(pltpu.make_async_copy(leaf, mats, sems.at[chunks]))
     for copy in copies:
         copy.start()
-    copies[0].wait()
-    wide[...] = held[...].astype(F32).reshape(wide.shape)
-    copies[1].wait()
-    for g in range(boxes // lane_boxes):
-        rows = [
-            wide[pl.ds(g * lane_boxes + b, vectors, stride=boxes), :] for b in range(lane_boxes)
-        ]
-        stacked = jnp.concatenate(rows, axis=0).astype(BF)
-        group = mats[pl.ds(g * lane_boxes, lane_boxes)].reshape(lane_boxes * rank, points)
-        out[g] = pick_lanes(dot_nt(group, stacked), rank, lane_boxes, vectors).astype(BF)
+    for c in range(chunks):
+        copies[c].wait()
+        rows = held[pl.ds(c * vectors, vectors)].astype(F32)
+        wide[...] = rows.reshape(wide.shape)
+        if c == 0:
+            copies[chunks].wait()
+        for g in range(boxes // lane_boxes):
+            rows = [
+                wide[pl.ds(g * lane_boxes + b, vectors, stride=boxes), :]
+                for b in range(lane_boxes)
+            ]
+            stacked = jnp.concatenate(rows, axis=0).astype(BF)
+            group = mats[pl.ds(g * lane_boxes, lane_boxes)].reshape(lane_boxes * rank, points)
+            outs[c][g] = pick_lanes(dot_nt(group, stacked), rank, lane_boxes, vectors).astype(BF)
 
 
 def forward_group(weights, stacked, lane_boxes, rank):
@@ -162,16 +176,16 @@
             adjoint[g * lane_boxes // 2 + pair] = pick_lanes(product, vectors, 2, rank).astype(BF)
 
 
-def residual_kernel(chunks, *refs):
-    parts = refs[:chunks]
-    token, residual, done, held, sems, wide = refs[chunks:]
-    boxes, vectors = parts[0].shape[0], parts[0].shape[1]
+def residual_kernel(chunk, part, token, *refs):
+    residual, done, held, sems, wide = refs[-5:]
+    boxes, vectors = part.shape[0], part.shape[1]
     for t in range(boxes):
-        rows = jnp.concatenate([part[t].astype(F32) for part in parts], axis=0)
-        wide[pl.ds(t, chunks * vectors, stride=boxes), :] = rows
+        wide[pl.ds(t, vectors, stride=boxes), :] = part[t].astype(F32)
     held[...] = wide[...].reshape(held.shape).astype(BF)
     done[...] = jnp.zeros(done.shape, done.dtype)
-    store = pltpu.make_async_copy(held, residual, sems.at[0])
+    store = pltpu.make_async_copy(
+        held, residual.at[pl.ds(chunk * vectors, vectors)], sems.at[0]
+    )
     store.start()
     store.wait()
 
@@ -233,18 +247,27 @@
 def gradient_kernel(chunk, held_part, received, leaf, *refs):
     gradient, held, sems, result = refs[-4:]
     pairs, vectors = held_part.shape[0], held_part.shape[1]
-    boxes = leaf.shape[0]
-    for p in range(pairs):
-        value = (held_part[p] + received[p].astype(F32)).astype(BF)
-        product = dot(split_rows(value), pair_rows(leaf, p))
-        result[pl.ds(2 * p, vectors, stride=boxes), :] = product[:vectors]
-        result[pl.ds(2 * p + 1, vectors, stride=boxes), :] = product[vectors:]
-    held[...] = result[...].reshape(held.shape).astype(BF)
-    store = pltpu.make_async_copy(
-        held, gradient.at[pl.ds(chunk * vectors, vectors)], sems.at[0]
-    )
-    store.start()
-    store.wait()
+    boxes, points = held.shape[1], held.shape[2]
+    stores = []
+    for part in range(PARTS):
+        for p in range(part * pairs // PARTS, (part + 1) * pairs // PARTS):
+            value = (held_part[p] + received[p].astype(F32)).astype(BF)
+            product = dot(split_rows(value), pair_rows(leaf, p))
+            result[pl.ds(2 * p, vectors, stride=boxes), :] = product[:vectors]
+            result[pl.ds(2 * p + 1, vectors, stride=boxes), :] = product[vectors:]
+        own = pl.ds(part * boxes // PARTS, boxes // PARTS)
+        for v in range(vectors):
+            rows = result[pl.ds(v * boxes + part * boxes // PARTS, boxes // PARTS), :]
+            held[v, own, :] = rows.astype(BF)
+        store = pltpu.make_async_copy(
+            held.at[:, own, :],
+            gradient.at[pl.ds(chunk * vectors, vectors), own, :],
+            sems.at[part],
+        )
+        store.start()
+        stores.append(store)
+    for store in stores:
+        store.wait()
 
 
 VMEM = pl.BlockSpec(memory_space=pltpu.VMEM)
@@ -315,10 +338,16 @@
                 )
         return lax.ppermute(array, ("src", "hi"), pairs_of)
 
-    def leaf_call(chunk):
-        kernel = functools.partial(leaf_kernel, chunk)
-        scratch = [held, pltpu.VMEM((boxes, rank, points), BF), sems, wide]
-        return call(kernel, forward_shape, [HBM, HBM, ANY], VMEM, scratch, flops, 2 * moved, 8)
+    def leaf_call(*operands):
+        scratch = [
+            pltpu.VMEM((total, boxes, points), BF), pltpu.VMEM((boxes, rank, points), BF),
+            pltpu.SemaphoreType.DMA((CHUNKS + 1,)), wide,
+        ]
+        return call(
+            functools.partial(leaf_kernel, CHUNKS),
+            (forward_shape,) * CHUNKS, [HBM] * 2, (VMEM,) * CHUNKS, scratch,
+            CHUNKS * flops, 4 * moved, 8,
+        )(*operands)
 
     whole = [
         pltpu.VMEM((total, boxes, points), BF), sems, pltpu.VMEM((total * boxes, points), F32)
@@ -336,17 +365,20 @@
             (VMEM, VMEM), [], 2 * flops, 4 * moved, 8,
         )(*operands)
 
-    def residual_call(*operands):
-        return call(
-            functools.partial(residual_kernel, CHUNKS), (full_shape, shape(8, LANES, dtype=F32)),
-            [VMEM] * CHUNKS + [ANY], (HBM, VMEM), whole, 0, 2 * moved, 8,
+    done_shape = shape(8, LANES, dtype=F32)
+
+    def residual_call(chunk, *operands):
+        return call(
+            functools.partial(residual_kernel, chunk), (full_shape, done_shape),
+            [VMEM, ANY] + [HBM] * (len(operands) - 2), (HBM, VMEM), [held, sems, wide],
+            0, 2 * moved, 8, {2: 0} if len(operands) > 2 else None,
         )(*operands)
 
     def gradient_call(chunk, *operands):
-        kernel = functools.partial(gradient_kernel, chunk)
-        specs = [VMEM] * 3 + [HBM] * (len(operands) - 3)
-        return call(
-            kernel, full_shape, specs, HBM, [held, sems, wide],
+        return call(
+            functools.partial(gradient_kernel, chunk), full_shape,
+            [VMEM] * 3 + [HBM] * (len(operands) - 3), HBM,
+            [held, pltpu.SemaphoreType.DMA((PARTS,)), wide],
             flops, 2 * moved, 8, {3: 0} if len(operands) > 3 else None,
         )(*operands)
 
@@ -380,40 +412,44 @@
     top = device_bits - 1
     every = range(CHUNKS)
     coeffs, kept, sent = [None] * CHUNKS, [None] * CHUNKS, [None] * CHUNKS
-    token = leaf
-    for c in every:
-        coeffs[c] = token = leaf_call(c)(samples, leaf, token)
-    for level in range(top):
-        maps = levels[level:level + 1] if level < 2 else levels
+    coeffs = list(leaf_call(samples, leaf))
+    token = coeffs[0]
+    by_box = [None] * CHUNKS
+    residual, gradient = (), ()
+    first_back = top + 1 + 2 * GAP
+    stages = first_back + top
+    for step in range(stages + LAG * (CHUNKS - 1)):
         for c in every:
-            coeffs[c] = token = cross_call(
-                level, coeffs[c], exchange(coeffs[c], level), maps, token
-            )
-        if level == 2:
-            wanted = token = order_call(wanted, token)
-    for c in every:
-        coeffs[c] = token = local_forward_call(
-            coeffs[c], exchange(coeffs[c], top), levels, token
-        )
-    residual = [None] * CHUNKS
-    for c in every:
-        residual[c], sent[c] = target_call(c, reversal(coeffs[c]), final, wanted, token)
-        token = sent[c]
-    for c in every:
-        kept[c], sent[c] = local_adjoint_call(reversal(sent[c]), levels, token)
-        token = sent[c]
-    for level in reversed(range(top)):
-        for c in every:
-            kept[c], sent[c] = adjoint_call(
-                level, kept[c], exchange(sent[c], level + 1), levels, token
-            )
-            token = sent[c]
-        if level == top - 2:
-            residual, token = residual_call(*residual, token)
-    gradient = ()
+            stage = step - LAG * c
+            if 0 <= stage < top:
+                level = stage
+                maps = levels[level:level + 1] if level < EARLY else levels
+                coeffs[c] = token = cross_call(
+                    level, coeffs[c], exchange(coeffs[c], level), maps, token
+                )
+            elif stage == top:
+                coeffs[c] = token = local_forward_call(
+                    coeffs[c], exchange(coeffs[c], top), levels, token
+                )
+            elif stage == top + GAP:
+                by_box[c], sent[c] = target_call(c, reversal(coeffs[c]), final, wanted, token)
+                token = sent[c]
+            elif stage == top + 2 * GAP:
+                kept[c], sent[c] = local_adjoint_call(reversal(sent[c]), levels, token)
+                token = sent[c]
+            elif first_back <= stage < stages:
+                level = top - 1 - (stage - first_back)
+                kept[c], sent[c] = adjoint_call(
+                    level, kept[c], exchange(sent[c], level + 1), levels, token
+                )
+                token = sent[c]
+            if (stage, c) == (2, CHUNKS - 1):
+                wanted = token = order_call(wanted, token)
+            if stage == first_back + 2:
+                *residual, token = residual_call(c, by_box[c], token, *residual)
     for c in every:
         gradient = [gradient_call(c, kept[c], exchange(sent[c], 0), leaf, *gradient)]
-    gradient = gradient[0]
+    residual, gradient = residual[0], gradient[0]
     return (
         residual.reshape(total, 1, 1, boxes, points),
         gradient.reshape(total, boxes, 1, 1, points),

time: 194 us -> 194 us (level)
  no operation moved by 1% of the time
where the time goes in v2:
time: 194 us
  starting transfers between devices  93.2 us (48%)
  waiting for transfers between devices  60 us (31%)
  Pallas kernels  34.5 us (18%)
  local copies, waits for them, and re-layouts  4.56 us (2%)
    ppermute x28, starting transfers between devices, exchange(): return lax.ppermute(array, axis, [(i, i ^ 1 << bit) for i in range(count)])  78.3 us
    ppermute x28, waiting for transfers between devices, exchange(): return lax.ppermute(array, axis, [(i, i ^ 1 << bit) for i in range(count)])  56.6 us
    ppermute x4, starting transfers between devices, reversal(): return lax.ppermute(array, ('src', 'hi'), pairs_of)  15 us
    pallas_call x12, Pallas kernels, adjoint_call(): call(kernel, (kept_shape, pair_shape), specs, (VMEM, VMEM), [], flops, mo...  5.9 us
    pallas_call x12, Pallas kernels, cross_call(): call(kernel, forward_shape, specs, VMEM, [], flops, moved, 4)(*operands)  5.16 us
    pallas_call x2, Pallas kernels, target_call(): call(kernel, (shape(boxes, vectors, points), pair_shape), [VMEM] * 3 + [A...  4.55 us
    pallas_call x2, Pallas kernels, local_adjoint_call(): call(kernel, (kept_shape, pair_shape), [VMEM] * 2 + [ANY], (VMEM, VMEM),...  4.24 us
    pallas_call x2, Pallas kernels, local_forward_call(): call(kernel, forward_shape, [VMEM] * 3 + [ANY], VMEM, scratch, 7 * flops,...  4.23 us
  transfers between devices with their start and end apart: 32, of which 18 were waited for; matrix products, arithmetic and copies ran while one was open for 1% of the time, Pallas kernels for 16%

profile of v2, /device:TPU:1, one launch (start us, length us, event | category | flops | bytes accessed | tf_op | source)
XLA Modules:
  0.0 193.5 jit_solution(2424664391437715427)
XLA Ops:
  11.3 5.5 %collective-permute-done.3.other = bf16[16,64,128]{2,1,0:T(8,128)(2,1)S(1)} collective-permute-done((bf16[16,64,128]{2,1,0:T(8,128)(2,1)S(1)}, bf16[16,64,128]{2,1,0:T(8,128)(2,1)S(1)}, u32[]{:S(2)}, u32[]{:S(2)}) %collective-permute-start.3) | collective-permute-done | bytes 262176 | tf_op jit(solution)/shard_map/ppermute | solution.py:329
  17.2 2.9 %collective-permute-start.5 = (bf16[16,64,128]{2,1,0:T(8,128)(2,1)S(1)}, bf16[16,64,128]{2,1,0:T(8,128)(2,1)S(1)}, u32[]{:S(2)}, u32[]{:S(2)}) collective-permute-start(bf16[16,64,128]{2,1,0:T(8,128)(2,1)S(1)} %shard_map.71.refs_0_.own), channel_id=1, source_target_pairs={{0,8},{2,10},{4,12},{6,14},{8,0},{10,2},{12,4},{14,6},{16,24},{18,... | collective-permute-start | bytes 786440 | tf_op jit(solution)/shard_map/ppermute | solution.py:329
  20.1 2.3 %collective-permute-done.2.other = bf16[16,64,128]{2,1,0:T(8,128)(2,1)S(1)} collective-permute-done((bf16[16,64,128]{2,1,0:T(8,128)(2,1)S(1)}, bf16[16,64,128]{2,1,0:T(8,128)(2,1)S(1)}, u32[]{:S(2)}, u32[]{:S(2)}) %collective-permute-start.2) | collective-permute-done | bytes 262176 | tf_op jit(solution)/shard_map/ppermute | solution.py:329
  22.8 2.9 %collective-permute-start.4 = (bf16[16,64,128]{2,1,0:T(8,128)(2,1)S(1)}, bf16[16,64,128]{2,1,0:T(8,128)(2,1)S(1)}, u32[]{:S(2)}, u32[]{:S(2)}) collective-permute-start(bf16[16,64,128]{2,1,0:T(8,128)(2,1)S(1)} %shard_map.72.refs_0_.own), channel_id=1, source_target_pairs={{0,8},{2,10},{4,12},{6,14},{8,0},{10,2},{12,4},{14,6},{16,24},{18,... | collective-permute-start | bytes 786440 | tf_op jit(solution)/shard_map/ppermute | solution.py:329
  25.7 4.5 %collective-permute-done.5.other = bf16[16,64,128]{2,1,0:T(8,128)(2,1)S(1)} collective-permute-done((bf16[16,64,128]{2,1,0:T(8,128)(2,1)S(1)}, bf16[16,64,128]{2,1,0:T(8,128)(2,1)S(1)}, u32[]{:S(2)}, u32[]{:S(2)}) %collective-permute-start.5) | collective-permute-done | bytes 262176 | tf_op jit(solution)/shard_map/ppermute | solution.py:329
  30.7 3.7 %collective-permute-start.7 = (bf16[16,64,128]{2,1,0:T(8,128)(2,1)S(1)}, bf16[16,64,128]{2,1,0:T(8,128)(2,1)S(1)}, u32[]{:S(2)}, u32[]{:S(2)}) collective-permute-start(bf16[16,64,128]{2,1,0:T(8,128)(2,1)S(1)} %shard_map.73.refs_0_.own), channel_id=1, source_target_pairs={{0,16},{2,18},{4,20},{6,22},{8,24},{10,26},{12,28},{14,30},{16,0},... | collective-permute-start | bytes 786440 | tf_op jit(solution)/shard_map/ppermute | solution.py:329
  36.3 3.7 %collective-permute-start.6 = (bf16[16,64,128]{2,1,0:T(8,128)(2,1)S(1)}, bf16[16,64,128]{2,1,0:T(8,128)(2,1)S(1)}, u32[]{:S(2)}, u32[]{:S(2)}) collective-permute-start(bf16[16,64,128]{2,1,0:T(8,128)(2,1)S(1)} %shard_map.74.token.own), channel_id=1, source_target_pairs={{0,16},{2,18},{4,20},{6,22},{8,24},{10,26},{12,28},{14,30},{16,0},... | collective-permute-start | bytes 786440 | tf_op jit(solution)/shard_map/ppermute | solution.py:329
  43.2 2.2 %collective-permute-done.6.other = bf16[16,64,128]{2,1,0:T(8,128)(2,1)S(1)} collective-permute-done((bf16[16,64,128]{2,1,0:T(8,128)(2,1)S(1)}, bf16[16,64,128]{2,1,0:T(8,128)(2,1)S(1)}, u32[]{:S(2)}, u32[]{:S(2)}) %collective-permute-start.6) | collective-permute-done | bytes 262176 | tf_op jit(solution)/shard_map/ppermute | solution.py:329
  48.6 3.0 %collective-permute-start.11 = (bf16[16,64,128]{2,1,0:T(8,128)(2,1)S(1)}, bf16[16,64,128]{2,1,0:T(8,128)(2,1)S(1)}, u32[]{:S(2)}, u32[]{:S(2)}) collective-permute-start(bf16[16,64,128]{2,1,0:T(8,128)(2,1)S(1)} %shard_map.78.refs_0_.own), channel_id=1, source_target_pairs={{0,64},{2,66},{4,68},{6,70},{8,72},{10,74},{12,76},{14,78},{16,80}... | collective-permute-start | bytes 786440 | tf_op jit(solution)/shard_map/ppermute | solution.py:329
  51.6 2.7 %collective-permute-done.8.other = bf16[16,64,128]{2,1,0:T(8,128)(2,1)S(1)} collective-permute-done((bf16[16,64,128]{2,1,0:T(8,128)(2,1)S(1)}, bf16[16,64,128]{2,1,0:T(8,128)(2,1)S(1)}, u32[]{:S(2)}, u32[]{:S(2)}) %collective-permute-start.8) | collective-permute-done | bytes 262176 | tf_op jit(solution)/shard_map/ppermute | solution.py:329
  54.7 3.0 %collective-permute-start.10 = (bf16[16,64,128]{2,1,0:T(8,128)(2,1)S(1)}, bf16[16,64,128]{2,1,0:T(8,128)(2,1)S(1)}, u32[]{:S(2)}, u32[]{:S(2)}) collective-permute-start(bf16[16,64,128]{2,1,0:T(8,128)(2,1)S(1)} %shard_map.79.refs_0_.own), channel_id=1, source_target_pairs={{0,64},{2,66},{4,68},{6,70},{8,72},{10,74},{12,76},{14,78},{16,80}... | collective-permute-start | bytes 786440 | tf_op jit(solution)/shard_map/ppermute | solution.py:329
  57.7 4.6 %collective-permute-done.11.other = bf16[16,64,128]{2,1,0:T(8,128)(2,1)S(1)} collective-permute-done((bf16[16,64,128]{2,1,0:T(8,128)(2,1)S(1)}, bf16[16,64,128]{2,1,0:T(8,128)(2,1)S(1)}, u32[]{:S(2)}, u32[]{:S(2)}) %collective-permute-start.11) | collective-permute-done | bytes 262176 | tf_op jit(solution)/shard_map/ppermute | solution.py:329
  63.6 4.4 %collective-permute-done.10.other = bf16[16,64,128]{2,1,0:T(8,128)(2,1)S(1)} collective-permute-done((bf16[16,64,128]{2,1,0:T(8,128)(2,1)S(1)}, bf16[16,64,128]{2,1,0:T(8,128)(2,1)S(1)}, u32[]{:S(2)}, u32[]{:S(2)}) %collective-permute-start.10) | collective-permute-done | bytes 262176 | tf_op jit(solution)/shard_map/ppermute | solution.py:329
  71.6 6.9 %collective-permute-start.15 = (bf16[16,64,128]{2,1,0:T(8,128)(2,1)S(1)}, bf16[16,64,128]{2,1,0:T(8,128)(2,1)S(1)}, u32[]{:S(2)}, u32[]{:S(2)}) collective-permute-start(bf16[16,64,128]{2,1,0:T(8,128)(2,1)S(1)} %shard_map.82.token), channel_id=1, source_target_pairs={{0,0},{1,2},{2,1},{3,3},{4,64},{5,66},{6,65},{7,67},{8,32},{9,34},... | collective-permute-start | bytes 786440 | tf_op jit(solution)/shard_map/ppermute | solution.py:339
  80.6 2.5 %collective-permute-start.14 = (bf16[16,64,128]{2,1,0:T(8,128)(2,1)S(1)}, bf16[16,64,128]{2,1,0:T(8,128)(2,1)S(1)}, u32[]{:S(2)}, u32[]{:S(2)}) collective-permute-start(bf16[16,64,128]{2,1,0:T(8,128)(2,1)S(1)} %shard_map.83.token), channel_id=1, source_target_pairs={{0,0},{1,2},{2,1},{3,3},{4,64},{5,66},{6,65},{7,67},{8,32},{9,34},... | collective-permute-start | bytes 786440 | tf_op jit(solution)/shard_map/ppermute | solution.py:339
  83.1 2.3 %shard_map.84 = (bf16[64,32,128]{2,1,0:T(8,128)(2,1)S(1)}, bf16[32,32,128]{2,1,0:T(8,128)(2,1)S(1)}) custom-call(bf16[16,64,128]{2,1,0:T(8,128)(2,1)S(1)} %collective-permute-done.15.coeffs, bf16[64,64,128]{2,1,0:T(8,128)(2,1)S(1)} %bitcast.44, bf16[64,64,128]{2,1,0:T(8,128)(2,1)S(1)} %shard_map.75.refs_0_.wanted, bf16[16,64,128]{2,1,0:T(8,128)(2,1)S(1)} %shard_map.83.token), custom_call_target="tpu_custom_call" | custom-call | flops 67108864 | bytes 4194304 | tf_op jit(solution)/shard_map/pallas_call | solution.py:363
  85.4 3.1 %collective-permute-start.17 = (bf16[32,32,128]{2,1,0:T(8,128)(2,1)S(1)}, bf16[32,32,128]{2,1,0:T(8,128)(2,1)S(1)}, u32[]{:S(2)}, u32[]{:S(2)}) collective-permute-start(bf16[32,32,128]{2,1,0:T(8,128)(2,1)S(1)} %get-tuple-element.42.token), channel_id=1, source_target_pairs={{0,0},{1,2},{2,1},{3,3},{4,64},{5,66},{6,65},{7,67},{8,32},{9,34},... | collective-permute-start | bytes 786440 | tf_op jit(solution)/shard_map/ppermute | solution.py:339
  88.5 2.3 %shard_map.85 = (bf16[64,32,128]{2,1,0:T(8,128)(2,1)S(1)}, bf16[32,32,128]{2,1,0:T(8,128)(2,1)S(1)}) custom-call(bf16[16,64,128]{2,1,0:T(8,128)(2,1)S(1)} %collective-permute-done.14.coeffs, bf16[64,64,128]{2,1,0:T(8,128)(2,1)S(1)} %bitcast.45, bf16[64,64,128]{2,1,0:T(8,128)(2,1)S(1)} %shard_map.75.refs_0_.wanted, ...), custom_call_target="tpu_custom_call" | custom-call | flops 67108864 | bytes 4194304 | tf_op jit(solution)/shard_map/pallas_call | solution.py:363
  90.8 2.5 %collective-permute-start.16 = (bf16[32,32,128]{2,1,0:T(8,128)(2,1)S(1)}, bf16[32,32,128]{2,1,0:T(8,128)(2,1)S(1)}, u32[]{:S(2)}, u32[]{:S(2)}) collective-permute-start(bf16[32,32,128]{2,1,0:T(8,128)(2,1)S(1)} %get-tuple-element.44.token), channel_id=1, source_target_pairs={{0,0},{1,2},{2,1},{3,3},{4,64},{5,66},{6,65},{7,67},{8,32},{9,34},... | collective-permute-start | bytes 786440 | tf_op jit(solution)/shard_map/ppermute | solution.py:339
  93.3 2.1 %shard_map.86 = (f32[32,32,128]{2,1,0:T(8,128)S(1)}, bf16[32,32,128]{2,1,0:T(8,128)(2,1)S(1)}) custom-call(bf16[32,32,128]{2,1,0:T(8,128)(2,1)S(1)} %collective-permute-done.17.adjoint, bf16[13,64,64,128]{3,2,1,0:T(8,128)(2,1)S(1)} %bitcast.27, bf16[32,32,128]{2,1,0:T(8,128)(2,1)S(1)} %get-tuple-element.44.token), custom_call_target="tpu_custom_call" | custom-call | flops 234881024 | bytes 7340032 | tf_op jit(solution)/shard_map/pallas_call | solution.py:407
  95.5 3.4 %collective-permute-done.16.adjoint = bf16[32,32,128]{2,1,0:T(8,128)(2,1)S(1)} collective-permute-done((bf16[32,32,128]{2,1,0:T(8,128)(2,1)S(1)}, bf16[32,32,128]{2,1,0:T(8,128)(2,1)S(1)}, u32[]{:S(2)}, u32[]{:S(2)}) %collective-permute-start.16) | collective-permute-done | bytes 262176 | tf_op jit(solution)/shard_map/ppermute | solution.py:339
  101.1 2.8 %collective-permute-done.19.received = bf16[32,32,128]{2,1,0:T(8,128)(2,1)S(1)} collective-permute-done((bf16[32,32,128]{2,1,0:T(8,128)(2,1)S(1)}, bf16[32,32,128]{2,1,0:T(8,128)(2,1)S(1)}, u32[]{:S(2)}, u32[]{:S(2)}) %collective-permute-start.19) | collective-permute-done | bytes 262176 | tf_op jit(solution)/shard_map/ppermute | solution.py:329
  104.4 24.6 %collective-permute-start.21 = (bf16[32,32,128]{2,1,0:T(8,128)(2,1)S(1)}, bf16[32,32,128]{2,1,0:T(8,128)(2,1)S(1)}, u32[]{:S(2)}, u32[]{:S(2)}) collective-permute-start(bf16[32,32,128]{2,1,0:T(8,128)(2,1)S(1)} %get-tuple-element.49.refs_0_), channel_id=1, source_target_pairs={{0,64},{2,66},{4,68},{6,70},{8,72},{10,74},{12,76},{14,78},{16,80}... | collective-permute-start | bytes 786440 | tf_op jit(solution)/shard_map/ppermute | solution.py:329
  129.4 5.8 %collective-permute-start.20 = (bf16[32,32,128]{2,1,0:T(8,128)(2,1)S(1)}, bf16[32,32,128]{2,1,0:T(8,128)(2,1)S(1)}, u32[]{:S(2)}, u32[]{:S(2)}) collective-permute-start(bf16[32,32,128]{2,1,0:T(8,128)(2,1)S(1)} %get-tuple-element.51.refs_0_), channel_id=1, source_target_pairs={{0,64},{2,66},{4,68},{6,70},{8,72},{10,74},{12,76},{14,78},{16,80}... | collective-permute-start | bytes 786440 | tf_op jit(solution)/shard_map/ppermute | solution.py:329
  137.1 4.6 %collective-permute-done.20.received = bf16[32,32,128]{2,1,0:T(8,128)(2,1)S(1)} collective-permute-done((bf16[32,32,128]{2,1,0:T(8,128)(2,1)S(1)}, bf16[32,32,128]{2,1,0:T(8,128)(2,1)S(1)}, u32[]{:S(2)}, u32[]{:S(2)}) %collective-permute-start.20) | collective-permute-done | bytes 262176 | tf_op jit(solution)/shard_map/ppermute | solution.py:329
  143.9 5.1 %collective-permute-done.23.received = bf16[32,32,128]{2,1,0:T(8,128)(2,1)S(1)} collective-permute-done((bf16[32,32,128]{2,1,0:T(8,128)(2,1)S(1)}, bf16[32,32,128]{2,1,0:T(8,128)(2,1)S(1)}, u32[]{:S(2)}, u32[]{:S(2)}) %collective-permute-start.23) | collective-permute-done | bytes 262176 | tf_op jit(solution)/shard_map/ppermute | solution.py:329
  159.6 2.2 %collective-permute-start.27 = (bf16[32,32,128]{2,1,0:T(8,128)(2,1)S(1)}, bf16[32,32,128]{2,1,0:T(8,128)(2,1)S(1)}, u32[]{:S(2)}, u32[]{:S(2)}) collective-permute-start(bf16[32,32,128]{2,1,0:T(8,128)(2,1)S(1)} %get-tuple-element.66.refs_0_), channel_id=1, source_target_pairs={{0,8},{2,10},{4,12},{6,14},{8,0},{10,2},{12,4},{14,6},{16,24},{18,... | collective-permute-start | bytes 786440 | tf_op jit(solution)/shard_map/ppermute | solution.py:329
  161.8 2.6 %collective-permute-done.24.received = bf16[32,32,128]{2,1,0:T(8,128)(2,1)S(1)} collective-permute-done((bf16[32,32,128]{2,1,0:T(8,128)(2,1)S(1)}, bf16[32,32,128]{2,1,0:T(8,128)(2,1)S(1)}, u32[]{:S(2)}, u32[]{:S(2)}) %collective-permute-start.24) | collective-permute-done | bytes 262176 | tf_op jit(solution)/shard_map/ppermute | solution.py:329
  167.6 5.8 %collective-permute-done.26.received = bf16[32,32,128]{2,1,0:T(8,128)(2,1)S(1)} collective-permute-done((bf16[32,32,128]{2,1,0:T(8,128)(2,1)S(1)}, bf16[32,32,128]{2,1,0:T(8,128)(2,1)S(1)}, u32[]{:S(2)}, u32[]{:S(2)}) %collective-permute-start.26) | collective-permute-done | bytes 262176 | tf_op jit(solution)/shard_map/ppermute | solution.py:329
  173.9 4.3 %collective-permute-done.29.received = bf16[32,32,128]{2,1,0:T(8,128)(2,1)S(1)} collective-permute-done((bf16[32,32,128]{2,1,0:T(8,128)(2,1)S(1)}, bf16[32,32,128]{2,1,0:T(8,128)(2,1)S(1)}, u32[]{:S(2)}, u32[]{:S(2)}) %collective-permute-start.29) | collective-permute-done | bytes 262176 | tf_op jit(solution)/shard_map/ppermute | solution.py:329
  178.7 6.1 %collective-permute-start.31 = (bf16[32,32,128]{2,1,0:T(8,128)(2,1)S(1)}, bf16[32,32,128]{2,1,0:T(8,128)(2,1)S(1)}, u32[]{:S(2)}, u32[]{:S(2)}) collective-permute-start(bf16[32,32,128]{2,1,0:T(8,128)(2,1)S(1)} %get-tuple-element.74.refs_0_), channel_id=1, source_target_pairs={{0,2},{2,0},{4,6},{6,4},{8,10},{10,8},{12,14},{14,12},{16,18},{18,... | collective-permute-start | bytes 786440 | tf_op jit(solution)/shard_map/ppermute | solution.py:329
  185.3 4.6 %collective-permute-start.30 = (bf16[32,32,128]{2,1,0:T(8,128)(2,1)S(1)}, bf16[32,32,128]{2,1,0:T(8,128)(2,1)S(1)}, u32[]{:S(2)}, u32[]{:S(2)}) collective-permute-start(bf16[32,32,128]{2,1,0:T(8,128)(2,1)S(1)} %get-tuple-element.76), channel_id=1, source_target_pairs={{0,2},{2,0},{4,6},{6,4},{8,10},{10,8},{12,14},{14,12},{16,18},{18,... | collective-permute-start | bytes 786440 | tf_op jit(solution)/shard_map/ppermute | solution.py:329
  (81 shorter events, 53.4 us)
Async XLA Ops:
  5.5 5.1 %collective-permute-start = (bf16[16,64,128]{2,1,0:T(8,128)(2,1)S(1)}, bf16[16,64,128]{2,1,0:T(8,128)(2,1)S(1)}, u32[]{:S(2)}, u32[]{:S(2)}) collective-permute-start(bf16[16,64,128]{2,1,0:T(8,128)(2,1)S(1)} %get-tuple-element.40.own), channel_id=1, source_target_pairs={{0,2},{2,0},{4,6},{6,4},{8,10},{10,8},{12,14},{14,12},{16,18},{18,... | collective-permute-start | bytes 786440 | tf_op jit(solution)/shard_map/ppermute | solution.py:329
  7.0 1.8 collective-permute-start.1
  9.2 7.5 %collective-permute-start.3 = (bf16[16,64,128]{2,1,0:T(8,128)(2,1)S(1)}, bf16[16,64,128]{2,1,0:T(8,128)(2,1)S(1)}, u32[]{:S(2)}, u32[]{:S(2)}) collective-permute-start(bf16[16,64,128]{2,1,0:T(8,128)(2,1)S(1)} %shard_map.69.refs_0_.own), channel_id=1, source_target_pairs={{0,4},{2,6},{4,0},{6,2},{8,12},{10,14},{12,8},{14,10},{16,20},{18,... | collective-permute-start | bytes 786440 | tf_op jit(solution)/shard_map/ppermute | solution.py:329
  11.0 11.3 %collective-permute-start.2 = (bf16[16,64,128]{2,1,0:T(8,128)(2,1)S(1)}, bf16[16,64,128]{2,1,0:T(8,128)(2,1)S(1)}, u32[]{:S(2)}, u32[]{:S(2)}) collective-permute-start(bf16[16,64,128]{2,1,0:T(8,128)(2,1)S(1)} %shard_map.70.refs_0_.own), channel_id=1, source_target_pairs={{0,4},{2,6},{4,0},{6,2},{8,12},{10,14},{12,8},{14,10},{16,20},{18,... | collective-permute-start | bytes 786440 | tf_op jit(solution)/shard_map/ppermute | solution.py:329
  17.2 13.1 %collective-permute-start.5 = (bf16[16,64,128]{2,1,0:T(8,128)(2,1)S(1)}, bf16[16,64,128]{2,1,0:T(8,128)(2,1)S(1)}, u32[]{:S(2)}, u32[]{:S(2)}) collective-permute-start(bf16[16,64,128]{2,1,0:T(8,128)(2,1)S(1)} %shard_map.71.refs_0_.own), channel_id=1, source_target_pairs={{0,8},{2,10},{4,12},{6,14},{8,0},{10,2},{12,4},{14,6},{16,24},{18,... | collective-permute-start | bytes 786440 | tf_op jit(solution)/shard_map/ppermute | solution.py:329
  22.8 13.1 %collective-permute-start.4 = (bf16[16,64,128]{2,1,0:T(8,128)(2,1)S(1)}, bf16[16,64,128]{2,1,0:T(8,128)(2,1)S(1)}, u32[]{:S(2)}, u32[]{:S(2)}) collective-permute-start(bf16[16,64,128]{2,1,0:T(8,128)(2,1)S(1)} %shard_map.72.refs_0_.own), channel_id=1, source_target_pairs={{0,8},{2,10},{4,12},{6,14},{8,0},{10,2},{12,4},{14,6},{16,24},{18,... | collective-permute-start | bytes 786440 | tf_op jit(solution)/shard_map/ppermute | solution.py:329
  30.7 10.7 %collective-permute-start.7 = (bf16[16,64,128]{2,1,0:T(8,128)(2,1)S(1)}, bf16[16,64,128]{2,1,0:T(8,128)(2,1)S(1)}, u32[]{:S(2)}, u32[]{:S(2)}) collective-permute-start(bf16[16,64,128]{2,1,0:T(8,128)(2,1)S(1)} %shard_map.73.refs_0_.own), channel_id=1, source_target_pairs={{0,16},{2,18},{4,20},{6,22},{8,24},{10,26},{12,28},{14,30},{16,0},... | collective-permute-start | bytes 786440 | tf_op jit(solution)/shard_map/ppermute | solution.py:329
  36.3 9.1 %collective-permute-start.6 = (bf16[16,64,128]{2,1,0:T(8,128)(2,1)S(1)}, bf16[16,64,128]{2,1,0:T(8,128)(2,1)S(1)}, u32[]{:S(2)}, u32[]{:S(2)}) collective-permute-start(bf16[16,64,128]{2,1,0:T(8,128)(2,1)S(1)} %shard_map.74.token.own), channel_id=1, source_target_pairs={{0,16},{2,18},{4,20},{6,22},{8,24},{10,26},{12,28},{14,30},{16,0},... | collective-permute-start | bytes 786440 | tf_op jit(solution)/shard_map/ppermute | solution.py:329
  41.9 6.3 %collective-permute-start.9 = (bf16[16,64,128]{2,1,0:T(8,128)(2,1)S(1)}, bf16[16,64,128]{2,1,0:T(8,128)(2,1)S(1)}, u32[]{:S(2)}, u32[]{:S(2)}) collective-permute-start(bf16[16,64,128]{2,1,0:T(8,128)(2,1)S(1)} %shard_map.76.refs_0_.own), channel_id=1, source_target_pairs={{0,32},{2,34},{4,36},{6,38},{8,40},{10,42},{12,44},{14,46},{16,48}... | collective-permute-start | bytes 786440 | tf_op jit(solution)/shard_map/ppermute | solution.py:329
  45.8 8.5 %collective-permute-start.8 = (bf16[16,64,128]{2,1,0:T(8,128)(2,1)S(1)}, bf16[16,64,128]{2,1,0:T(8,128)(2,1)S(1)}, u32[]{:S(2)}, u32[]{:S(2)}) collective-permute-start(bf16[16,64,128]{2,1,0:T(8,128)(2,1)S(1)} %shard_map.77.refs_0_.own), channel_id=1, source_target_pairs={{0,32},{2,34},{4,36},{6,38},{8,40},{10,42},{12,44},{14,46},{16,48}... | collective-permute-start | bytes 786440 | tf_op jit(solution)/shard_map/ppermute | solution.py:329
  48.6 13.7 %collective-permute-start.11 = (bf16[16,64,128]{2,1,0:T(8,128)(2,1)S(1)}, bf16[16,64,128]{2,1,0:T(8,128)(2,1)S(1)}, u32[]{:S(2)}, u32[]{:S(2)}) collective-permute-start(bf16[16,64,128]{2,1,0:T(8,128)(2,1)S(1)} %shard_map.78.refs_0_.own), channel_id=1, source_target_pairs={{0,64},{2,66},{4,68},{6,70},{8,72},{10,74},{12,76},{14,78},{16,80}... | collective-permute-start | bytes 786440 | tf_op jit(solution)/shard_map/ppermute | solution.py:329
  54.7 13.3 %collective-permute-start.10 = (bf16[16,64,128]{2,1,0:T(8,128)(2,1)S(1)}, bf16[16,64,128]{2,1,0:T(8,128)(2,1)S(1)}, u32[]{:S(2)}, u32[]{:S(2)}) collective-permute-start(bf16[16,64,128]{2,1,0:T(8,128)(2,1)S(1)} %shard_map.79.refs_0_.own), channel_id=1, source_target_pairs={{0,64},{2,66},{4,68},{6,70},{8,72},{10,74},{12,76},{14,78},{16,80}... | collective-permute-start | bytes 786440 | tf_op jit(solution)/shard_map/ppermute | solution.py:329
  62.8 6.6 %collective-permute-start.13 = (bf16[16,64,128]{2,1,0:T(8,128)(2,1)S(1)}, bf16[16,64,128]{2,1,0:T(8,128)(2,1)S(1)}, u32[]{:S(2)}, u32[]{:S(2)}) collective-permute-start(bf16[16,64,128]{2,1,0:T(8,128)(2,1)S(1)} %shard_map.80.refs_0_.own), channel_id=1, source_target_pairs={{0,1},{1,0},{2,3},{3,2},{4,5},{5,4},{6,7},{7,6},{8,9},{9,8},{10,11... | collective-permute-start | bytes 786440 | tf_op jit(solution)/shard_map/ppermute | solution.py:329
  68.4 10.0 %collective-permute-start.12 = (bf16[16,64,128]{2,1,0:T(8,128)(2,1)S(1)}, bf16[16,64,128]{2,1,0:T(8,128)(2,1)S(1)}, u32[]{:S(2)}, u32[]{:S(2)}) collective-permute-start(bf16[16,64,128]{2,1,0:T(8,128)(2,1)S(1)} %shard_map.81.token.own), channel_id=1, source_target_pairs={{0,1},{1,0},{2,3},{3,2},{4,5},{5,4},{6,7},{7,6},{8,9},{9,8},{10,11... | collective-permute-start | bytes 786440 | tf_op jit(solution)/shard_map/ppermute | solution.py:329
  71.6 11.6 %collective-permute-start.15 = (bf16[16,64,128]{2,1,0:T(8,128)(2,1)S(1)}, bf16[16,64,128]{2,1,0:T(8,128)(2,1)S(1)}, u32[]{:S(2)}, u32[]{:S(2)}) collective-permute-start(bf16[16,64,128]{2,1,0:T(8,128)(2,1)S(1)} %shard_map.82.token), channel_id=1, source_target_pairs={{0,0},{1,2},{2,1},{3,3},{4,64},{5,66},{6,65},{7,67},{8,32},{9,34},... | collective-permute-start | bytes 786440 | tf_op jit(solution)/shard_map/ppermute | solution.py:339
  80.6 7.9 %collective-permute-start.14 = (bf16[16,64,128]{2,1,0:T(8,128)(2,1)S(1)}, bf16[16,64,128]{2,1,0:T(8,128)(2,1)S(1)}, u32[]{:S(2)}, u32[]{:S(2)}) collective-permute-start(bf16[16,64,128]{2,1,0:T(8,128)(2,1)S(1)} %shard_map.83.token), channel_id=1, source_target_pairs={{0,0},{1,2},{2,1},{3,3},{4,64},{5,66},{6,65},{7,67},{8,32},{9,34},... | collective-permute-start | bytes 786440 | tf_op jit(solution)/shard_map/ppermute | solution.py:339
  85.4 7.9 %collective-permute-start.17 = (bf16[32,32,128]{2,1,0:T(8,128)(2,1)S(1)}, bf16[32,32,128]{2,1,0:T(8,128)(2,1)S(1)}, u32[]{:S(2)}, u32[]{:S(2)}) collective-permute-start(bf16[32,32,128]{2,1,0:T(8,128)(2,1)S(1)} %get-tuple-element.42.token), channel_id=1, source_target_pairs={{0,0},{1,2},{2,1},{3,3},{4,64},{5,66},{6,65},{7,67},{8,32},{9,34},... | collective-permute-start | bytes 786440 | tf_op jit(solution)/shard_map/ppermute | solution.py:339
  90.8 8.2 %collective-permute-start.16 = (bf16[32,32,128]{2,1,0:T(8,128)(2,1)S(1)}, bf16[32,32,128]{2,1,0:T(8,128)(2,1)S(1)}, u32[]{:S(2)}, u32[]{:S(2)}) collective-permute-start(bf16[32,32,128]{2,1,0:T(8,128)(2,1)S(1)} %get-tuple-element.44.token), channel_id=1, source_target_pairs={{0,0},{1,2},{2,1},{3,3},{4,64},{5,66},{6,65},{7,67},{8,32},{9,34},... | collective-permute-start | bytes 786440 | tf_op jit(solution)/shard_map/ppermute | solution.py:339
  95.4 8.5 %collective-permute-start.19 = (bf16[32,32,128]{2,1,0:T(8,128)(2,1)S(1)}, bf16[32,32,128]{2,1,0:T(8,128)(2,1)S(1)}, u32[]{:S(2)}, u32[]{:S(2)}) collective-permute-start(bf16[32,32,128]{2,1,0:T(8,128)(2,1)S(1)} %get-tuple-element.45.token), channel_id=1, source_target_pairs={{0,1},{1,0},{2,3},{3,2},{4,5},{5,4},{6,7},{7,6},{8,9},{9,8},{10,11... | collective-permute-start | bytes 786440 | tf_op jit(solution)/shard_map/ppermute | solution.py:329
  101.0 27.9 %collective-permute-start.18 = (bf16[32,32,128]{2,1,0:T(8,128)(2,1)S(1)}, bf16[32,32,128]{2,1,0:T(8,128)(2,1)S(1)}, u32[]{:S(2)}, u32[]{:S(2)}) collective-permute-start(bf16[32,32,128]{2,1,0:T(8,128)(2,1)S(1)} %get-tuple-element.47.refs_0_), channel_id=1, source_target_pairs={{0,1},{1,0},{2,3},{3,2},{4,5},{5,4},{6,7},{7,6},{8,9},{9,8},{10,11... | collective-permute-start | bytes 786440 | tf_op jit(solution)/shard_map/ppermute | solution.py:329
  104.4 30.9 %collective-permute-start.21 = (bf16[32,32,128]{2,1,0:T(8,128)(2,1)S(1)}, bf16[32,32,128]{2,1,0:T(8,128)(2,1)S(1)}, u32[]{:S(2)}, u32[]{:S(2)}) collective-permute-start(bf16[32,32,128]{2,1,0:T(8,128)(2,1)S(1)} %get-tuple-element.49.refs_0_), channel_id=1, source_target_pairs={{0,64},{2,66},{4,68},{6,70},{8,72},{10,74},{12,76},{14,78},{16,80}... | collective-permute-start | bytes 786440 | tf_op jit(solution)/shard_map/ppermute | solution.py:329
  129.4 12.3 %collective-permute-start.20 = (bf16[32,32,128]{2,1,0:T(8,128)(2,1)S(1)}, bf16[32,32,128]{2,1,0:T(8,128)(2,1)S(1)}, u32[]{:S(2)}, u32[]{:S(2)}) collective-permute-start(bf16[32,32,128]{2,1,0:T(8,128)(2,1)S(1)} %get-tuple-element.51.refs_0_), channel_id=1, source_target_pairs={{0,64},{2,66},{4,68},{6,70},{8,72},{10,74},{12,76},{14,78},{16,80}... | collective-permute-start | bytes 786440 | tf_op jit(solution)/shard_map/ppermute | solution.py:329
  135.8 13.3 %collective-permute-start.23 = (bf16[32,32,128]{2,1,0:T(8,128)(2,1)S(1)}, bf16[32,32,128]{2,1,0:T(8,128)(2,1)S(1)}, u32[]{:S(2)}, u32[]{:S(2)}) collective-permute-start(bf16[32,32,128]{2,1,0:T(8,128)(2,1)S(1)} %get-tuple-element.53.refs_0_), channel_id=1, source_target_pairs={{0,32},{2,34},{4,36},{6,38},{8,40},{10,42},{12,44},{14,46},{16,48}... | collective-permute-start | bytes 786440 | tf_op jit(solution)/shard_map/ppermute | solution.py:329
  142.3 12.4 %collective-permute-start.22 = (bf16[32,32,128]{2,1,0:T(8,128)(2,1)S(1)}, bf16[32,32,128]{2,1,0:T(8,128)(2,1)S(1)}, u32[]{:S(2)}, u32[]{:S(2)}) collective-permute-start(bf16[32,32,128]{2,1,0:T(8,128)(2,1)S(1)} %get-tuple-element.55.refs_0_), channel_id=1, source_target_pairs={{0,32},{2,34},{4,36},{6,38},{8,40},{10,42},{12,44},{14,46},{16,48}... | collective-permute-start | bytes 786440 | tf_op jit(solution)/shard_map/ppermute | solution.py:329
  149.5 9.6 %collective-permute-start.25 = (bf16[32,32,128]{2,1,0:T(8,128)(2,1)S(1)}, bf16[32,32,128]{2,1,0:T(8,128)(2,1)S(1)}, u32[]{:S(2)}, u32[]{:S(2)}) collective-permute-start(bf16[32,32,128]{2,1,0:T(8,128)(2,1)S(1)} %get-tuple-element.58.token), channel_id=1, source_target_pairs={{0,16},{2,18},{4,20},{6,22},{8,24},{10,26},{12,28},{14,30},{16,0},... | collective-permute-start | bytes 786440 | tf_op jit(solution)/shard_map/ppermute | solution.py:329
  155.2 9.3 %collective-permute-start.24 = (bf16[32,32,128]{2,1,0:T(8,128)(2,1)S(1)}, bf16[32,32,128]{2,1,0:T(8,128)(2,1)S(1)}, u32[]{:S(2)}, u32[]{:S(2)}) collective-permute-start(bf16[32,32,128]{2,1,0:T(8,128)(2,1)S(1)} %get-tuple-element.60.token), channel_id=1, source_target_pairs={{0,16},{2,18},{4,20},{6,22},{8,24},{10,26},{12,28},{14,30},{16,0},... | collective-permute-start | bytes 786440 | tf_op jit(solution)/shard_map/ppermute | solution.py:329
  159.6 7.1 %collective-permute-start.27 = (bf16[32,32,128]{2,1,0:T(8,128)(2,1)S(1)}, bf16[32,32,128]{2,1,0:T(8,128)(2,1)S(1)}, u32[]{:S(2)}, u32[]{:S(2)}) collective-permute-start(bf16[32,32,128]{2,1,0:T(8,128)(2,1)S(1)} %get-tuple-element.66.refs_0_), channel_id=1, source_target_pairs={{0,8},{2,10},{4,12},{6,14},{8,0},{10,2},{12,4},{14,6},{16,24},{18,... | collective-permute-start | bytes 786440 | tf_op jit(solution)/shard_map/ppermute | solution.py:329
  165.0 8.4 %collective-permute-start.26 = (bf16[32,32,128]{2,1,0:T(8,128)(2,1)S(1)}, bf16[32,32,128]{2,1,0:T(8,128)(2,1)S(1)}, u32[]{:S(2)}, u32[]{:S(2)}) collective-permute-start(bf16[32,32,128]{2,1,0:T(8,128)(2,1)S(1)} %get-tuple-element.68.refs_0_), channel_id=1, source_target_pairs={{0,8},{2,10},{4,12},{6,14},{8,0},{10,2},{12,4},{14,6},{16,24},{18,... | collective-permute-start | bytes 786440 | tf_op jit(solution)/shard_map/ppermute | solution.py:329
  167.2 11.0 %collective-permute-start.29 = (bf16[32,32,128]{2,1,0:T(8,128)(2,1)S(1)}, bf16[32,32,128]{2,1,0:T(8,128)(2,1)S(1)}, u32[]{:S(2)}, u32[]{:S(2)}) collective-permute-start(bf16[32,32,128]{2,1,0:T(8,128)(2,1)S(1)} %get-tuple-element.70.refs_0_), channel_id=1, source_target_pairs={{0,4},{2,6},{4,0},{6,2},{8,12},{10,14},{12,8},{14,10},{16,20},{18,... | collective-permute-start | bytes 786440 | tf_op jit(solution)/shard_map/ppermute | solution.py:329
  173.8 11.0 %collective-permute-start.28 = (bf16[32,32,128]{2,1,0:T(8,128)(2,1)S(1)}, bf16[32,32,128]{2,1,0:T(8,128)(2,1)S(1)}, u32[]{:S(2)}, u32[]{:S(2)}) collective-permute-start(bf16[32,32,128]{2,1,0:T(8,128)(2,1)S(1)} %get-tuple-element.72.refs_0_), channel_id=1, source_target_pairs={{0,4},{2,6},{4,0},{6,2},{8,12},{10,14},{12,8},{14,10},{16,20},{18,... | collective-permute-start | bytes 786440 | tf_op jit(solution)/shard_map/ppermute | solution.py:329
  178.7 11.2 %collective-permute-start.31 = (bf16[32,32,128]{2,1,0:T(8,128)(2,1)S(1)}, bf16[32,32,128]{2,1,0:T(8,128)(2,1)S(1)}, u32[]{:S(2)}, u32[]{:S(2)}) collective-permute-start(bf16[32,32,128]{2,1,0:T(8,128)(2,1)S(1)} %get-tuple-element.74.refs_0_), channel_id=1, source_target_pairs={{0,2},{2,0},{4,6},{6,4},{8,10},{10,8},{12,14},{14,12},{16,18},{18,... | collective-permute-start | bytes 786440 | tf_op jit(solution)/shard_map/ppermute | solution.py:329
  185.3 6.3 %collective-permute-start.30 = (bf16[32,32,128]{2,1,0:T(8,128)(2,1)S(1)}, bf16[32,32,128]{2,1,0:T(8,128)(2,1)S(1)}, u32[]{:S(2)}, u32[]{:S(2)}) collective-permute-start(bf16[32,32,128]{2,1,0:T(8,128)(2,1)S(1)} %get-tuple-element.76), channel_id=1, source_target_pairs={{0,2},{2,0},{4,6},{6,4},{8,10},{10,8},{12,14},{14,12},{16,18},{18,... | collective-permute-start | bytes 786440 | tf_op jit(solution)/shard_map/ppermute | solution.py:329
  (6 other events, 68.6 us)

commit v3 on v2

--- a/solution.py
+++ b/solution.py
@@ -9,8 +9,8 @@
 
 CHUNKS = 2
 PARTS = 4
-EARLY = 2
-LAG = 0
+EARLY = 3
+LAG = 2
 GAP = 2
 LANES = 128
 BF = jnp.bfloat16
@@ -244,8 +244,9 @@
         adjoint_cross_pair(value, pair_rows(maps.at[level], p), kept, sent, p, high)
 
 
-def gradient_kernel(chunk, held_part, received, leaf, *refs):
-    gradient, held, sems, result = refs[-4:]
+def gradient_kernel(chunk, held_part, received, leaf, token, *refs):
+    gradient, done, held, sems, result = refs[-5:]
+    done[...] = jnp.zeros(done.shape, done.dtype)
     pairs, vectors = held_part.shape[0], held_part.shape[1]
     boxes, points = held.shape[1], held.shape[2]
     stores = []
@@ -376,10 +377,10 @@
 
     def gradient_call(chunk, *operands):
         return call(
-            functools.partial(gradient_kernel, chunk), full_shape,
-            [VMEM] * 3 + [HBM] * (len(operands) - 3), HBM,
+            functools.partial(gradient_kernel, chunk), (full_shape, done_shape),
+            [VMEM] * 3 + [ANY] + [HBM] * (len(operands) - 4), (HBM, VMEM),
             [held, pltpu.SemaphoreType.DMA((PARTS,)), wide],
-            flops, 2 * moved, 8, {3: 0} if len(operands) > 3 else None,
+            flops, 2 * moved, 8, {4: 0} if len(operands) > 4 else None,
         )(*operands)
 
     def cross_call(level, *operands):
@@ -418,7 +419,7 @@
     residual, gradient = (), ()
     first_back = top + 1 + 2 * GAP
     stages = first_back + top
-    for step in range(stages + LAG * (CHUNKS - 1)):
+    for step in range(stages + 1 + LAG * (CHUNKS - 1)):
         for c in every:
             stage = step - LAG * c
             if 0 <= stage < top:
@@ -443,12 +444,14 @@
                     level, kept[c], exchange(sent[c], level + 1), levels, token
                 )
                 token = sent[c]
+            elif stage == stages:
+                *gradient, token = gradient_call(
+                    c, kept[c], exchange(sent[c], 0), leaf, token, *gradient
+                )
             if (stage, c) == (2, CHUNKS - 1):
                 wanted = token = order_call(wanted, token)
             if stage == first_back + 2:
                 *residual, token = residual_call(c, by_box[c], token, *residual)
-    for c in every:
-        gradient = [gradient_call(c, kept[c], exchange(sent[c], 0), leaf, *gradient)]
     residual, gradient = residual[0], gradient[0]
     return (
         residual.reshape(total, 1, 1, boxes, points),

time: 194 us -> 202 us (1.041)
  starting transfers between devices: 93.2 us -> 103 us
  waiting for transfers between devices: 60 us -> 56.3 us
    ppermute x4, starting transfers between devices: 15 us -> 27.6 us  [reversal(): return lax.ppermute(array, ('src', 'hi'), pairs_of)]
    ppermute x28, waiting for transfers between devices: 56.6 us -> 49.8 us  [exchange(): return lax.ppermute(array, axis, [(i, i ^ 1 << bit) for i in range(count)])]
    ppermute x4, waiting for transfers between devices: 3.41 us -> 6.54 us  [reversal(): return lax.ppermute(array, ('src', 'hi'), pairs_of)]
    ppermute x28, starting transfers between devices: 78.3 us -> 75.6 us  [exchange(): return lax.ppermute(array, axis, [(i, i ^ 1 << bit) for i in range(count)])]
  transfers between devices with their start and end apart: 32 -> 32, of which waited for: 18 -> 18; matrix products, arithmetic and copies ran while one was open for 1% -> 1% of each run, Pallas kernels for 16% -> 14%
where the time goes in v3:
time: 202 us
  starting transfers between devices  103 us (51%)
  waiting for transfers between devices  56.3 us (28%)
  Pallas kernels  35.4 us (18%)
  local copies, waits for them, and re-layouts  5.39 us (3%)
    ppermute x28, starting transfers between devices, exchange(): return lax.ppermute(array, axis, [(i, i ^ 1 << bit) for i in range(count)])  75.6 us
    ppermute x28, waiting for transfers between devices, exchange(): return lax.ppermute(array, axis, [(i, i ^ 1 << bit) for i in range(count)])  49.8 us
    ppermute x4, starting transfers between devices, reversal(): return lax.ppermute(array, ('src', 'hi'), pairs_of)  27.6 us
    ppermute x4, waiting for transfers between devices, reversal(): return lax.ppermute(array, ('src', 'hi'), pairs_of)  6.54 us
    pallas_call x12, Pallas kernels, adjoint_call(): call(kernel, (kept_shape, pair_shape), specs, (VMEM, VMEM), [], flops, mo...  5.96 us
    pallas_call x12, Pallas kernels, cross_call(): call(kernel, forward_shape, specs, VMEM, [], flops, moved, 4)(*operands)  5.29 us
    pallas_call x2, Pallas kernels, target_call(): call(kernel, (shape(boxes, vectors, points), pair_shape), [VMEM] * 3 + [A...  4.54 us
    pallas_call x2, Pallas kernels, local_adjoint_call(): call(kernel, (kept_shape, pair_shape), [VMEM] * 2 + [ANY], (VMEM, VMEM),...  4.31 us
  transfers between devices with their start and end apart: 32, of which 18 were waited for; matrix products, arithmetic and copies ran while one was open for 1% of the time, Pallas kernels for 14%

profile of v3, /device:TPU:1, one launch (start us, length us, event | category | flops | bytes accessed | tf_op | source)
XLA Modules:
  0.0 201.6 jit_solution(3944280241188006953)
XLA Ops:
  7.0 2.5 %slice_bitcast_fusion = (bf16[1,64,64,128]{3,2,1,0:T(8,128)(2,1)S(1)}, bf16[1,64,64,128]{3,2,1,0:T(8,128)(2,1)S(1)}, bf16[1,64,64,128]{3,2,1,0:T(8,128)(2,1)S(1)}) fusion(bf16[13,64,1,1,64,128]{5,4,1,3,2,0:T(8,128)(2,1)} %bitcast.18), kind=kLoop, calls=%fused_computation | loop fusion | bytes 6291456 | tf_op jit(solution)/shard_map/slice | solution.py:427
  11.3 6.6 %collective-permute-done.2.other = bf16[16,64,128]{2,1,0:T(8,128)(2,1)S(1)} collective-permute-done((bf16[16,64,128]{2,1,0:T(8,128)(2,1)S(1)}, bf16[16,64,128]{2,1,0:T(8,128)(2,1)S(1)}, u32[]{:S(2)}, u32[]{:S(2)}) %collective-permute-start.2) | collective-permute-done | bytes 262176 | tf_op jit(solution)/shard_map/ppermute | solution.py:330
  18.4 2.9 %collective-permute-start.3 = (bf16[16,64,128]{2,1,0:T(8,128)(2,1)S(1)}, bf16[16,64,128]{2,1,0:T(8,128)(2,1)S(1)}, u32[]{:S(2)}, u32[]{:S(2)}) collective-permute-start(bf16[16,64,128]{2,1,0:T(8,128)(2,1)S(1)} %shard_map.70.own.refs_0_), channel_id=1, source_target_pairs={{0,8},{2,10},{4,12},{6,14},{8,0},{10,2},{12,4},{14,6},{16,24},{18,... | collective-permute-start | bytes 786440 | tf_op jit(solution)/shard_map/ppermute | solution.py:330
  22.4 4.6 %collective-permute-done.3.other = bf16[16,64,128]{2,1,0:T(8,128)(2,1)S(1)} collective-permute-done((bf16[16,64,128]{2,1,0:T(8,128)(2,1)S(1)}, bf16[16,64,128]{2,1,0:T(8,128)(2,1)S(1)}, u32[]{:S(2)}, u32[]{:S(2)}) %collective-permute-start.3) | collective-permute-done | bytes 262176 | tf_op jit(solution)/shard_map/ppermute | solution.py:330
  27.5 3.8 %collective-permute-start.5 = (bf16[16,64,128]{2,1,0:T(8,128)(2,1)S(1)}, bf16[16,64,128]{2,1,0:T(8,128)(2,1)S(1)}, u32[]{:S(2)}, u32[]{:S(2)}) collective-permute-start(bf16[16,64,128]{2,1,0:T(8,128)(2,1)S(1)} %shard_map.71.refs_0_.own), channel_id=1, source_target_pairs={{0,16},{2,18},{4,20},{6,22},{8,24},{10,26},{12,28},{14,30},{16,0},... | collective-permute-start | bytes 786440 | tf_op jit(solution)/shard_map/ppermute | solution.py:330
  33.0 3.2 %collective-permute-done.5.other = bf16[16,64,128]{2,1,0:T(8,128)(2,1)S(1)} collective-permute-done((bf16[16,64,128]{2,1,0:T(8,128)(2,1)S(1)}, bf16[16,64,128]{2,1,0:T(8,128)(2,1)S(1)}, u32[]{:S(2)}, u32[]{:S(2)}) %collective-permute-start.5) | collective-permute-done | bytes 262176 | tf_op jit(solution)/shard_map/ppermute | solution.py:330
  38.5 2.8 %collective-permute-start.6 = (bf16[16,64,128]{2,1,0:T(8,128)(2,1)S(1)}, bf16[16,64,128]{2,1,0:T(8,128)(2,1)S(1)}, u32[]{:S(2)}, u32[]{:S(2)}) collective-permute-start(bf16[16,64,128]{2,1,0:T(8,128)(2,1)S(1)} %shard_map.74.refs_0_.own), channel_id=1, source_target_pairs={{0,8},{2,10},{4,12},{6,14},{8,0},{10,2},{12,4},{14,6},{16,24},{18,... | collective-permute-start | bytes 786440 | tf_op jit(solution)/shard_map/ppermute | solution.py:330
  42.4 3.0 %collective-permute-start.9 = (bf16[16,64,128]{2,1,0:T(8,128)(2,1)S(1)}, bf16[16,64,128]{2,1,0:T(8,128)(2,1)S(1)}, u32[]{:S(2)}, u32[]{:S(2)}) collective-permute-start(bf16[16,64,128]{2,1,0:T(8,128)(2,1)S(1)} %shard_map.75.refs_0_.own), channel_id=1, source_target_pairs={{0,64},{2,66},{4,68},{6,70},{8,72},{10,74},{12,76},{14,78},{16,80}... | collective-permute-start | bytes 786440 | tf_op jit(solution)/shard_map/ppermute | solution.py:330
  45.8 2.8 %collective-permute-start.8 = (bf16[16,64,128]{2,1,0:T(8,128)(2,1)S(1)}, bf16[16,64,128]{2,1,0:T(8,128)(2,1)S(1)}, u32[]{:S(2)}, u32[]{:S(2)}) collective-permute-start(bf16[16,64,128]{2,1,0:T(8,128)(2,1)S(1)} %shard_map.76.token.own), channel_id=1, source_target_pairs={{0,16},{2,18},{4,20},{6,22},{8,24},{10,26},{12,28},{14,30},{16,0},... | collective-permute-start | bytes 786440 | tf_op jit(solution)/shard_map/ppermute | solution.py:330
  54.1 3.1 %collective-permute-done.11.other = bf16[16,64,128]{2,1,0:T(8,128)(2,1)S(1)} collective-permute-done((bf16[16,64,128]{2,1,0:T(8,128)(2,1)S(1)}, bf16[16,64,128]{2,1,0:T(8,128)(2,1)S(1)}, u32[]{:S(2)}, u32[]{:S(2)}) %collective-permute-start.11) | collective-permute-done | bytes 262176 | tf_op jit(solution)/shard_map/ppermute | solution.py:330
  59.8 2.6 %collective-permute-start.12 = (bf16[16,64,128]{2,1,0:T(8,128)(2,1)S(1)}, bf16[16,64,128]{2,1,0:T(8,128)(2,1)S(1)}, u32[]{:S(2)}, u32[]{:S(2)}) collective-permute-start(bf16[16,64,128]{2,1,0:T(8,128)(2,1)S(1)} %shard_map.81.own.refs_0_), channel_id=1, source_target_pairs={{0,64},{2,66},{4,68},{6,70},{8,72},{10,74},{12,76},{14,78},{16,80}... | collective-permute-start | bytes 786440 | tf_op jit(solution)/shard_map/ppermute | solution.py:330
  62.4 14.8 %collective-permute-start.14 = (bf16[16,64,128]{2,1,0:T(8,128)(2,1)S(1)}, bf16[16,64,128]{2,1,0:T(8,128)(2,1)S(1)}, u32[]{:S(2)}, u32[]{:S(2)}) collective-permute-start(bf16[16,64,128]{2,1,0:T(8,128)(2,1)S(1)} %shard_map.80.refs_0_), channel_id=1, source_target_pairs={{0,0},{1,2},{2,1},{3,3},{4,64},{5,66},{6,65},{7,67},{8,32},{9,34},... | collective-permute-start | bytes 786440 | tf_op jit(solution)/shard_map/ppermute | solution.py:340
  77.8 4.5 %collective-permute-done.14.coeffs = bf16[16,64,128]{2,1,0:T(8,128)(2,1)S(1)} collective-permute-done((bf16[16,64,128]{2,1,0:T(8,128)(2,1)S(1)}, bf16[16,64,128]{2,1,0:T(8,128)(2,1)S(1)}, u32[]{:S(2)}, u32[]{:S(2)}) %collective-permute-start.14) | collective-permute-done | bytes 262176 | tf_op jit(solution)/shard_map/ppermute | solution.py:340
  82.3 2.3 %shard_map.83 = (bf16[64,32,128]{2,1,0:T(8,128)(2,1)S(1)}, bf16[32,32,128]{2,1,0:T(8,128)(2,1)S(1)}) custom-call(bf16[16,64,128]{2,1,0:T(8,128)(2,1)S(1)} %collective-permute-done.14.coeffs, bf16[64,64,128]{2,1,0:T(8,128)(2,1)S(1)} %bitcast.44, bf16[64,64,128]{2,1,0:T(8,128)(2,1)S(1)} %shard_map.77.refs_0_.wanted, bf16[16,64,128]{2,1,0:T(8,128)(2,1)S(1)} %shard_map.82.token.own), custom_call_target="tpu_custom_call" | custom-call | flops 67108864 | bytes 4194304 | tf_op jit(solution)/shard_map/pallas_call | solution.py:364
  84.6 3.4 %collective-permute-start.16 = (bf16[32,32,128]{2,1,0:T(8,128)(2,1)S(1)}, bf16[32,32,128]{2,1,0:T(8,128)(2,1)S(1)}, u32[]{:S(2)}, u32[]{:S(2)}) collective-permute-start(bf16[32,32,128]{2,1,0:T(8,128)(2,1)S(1)} %get-tuple-element.45.token), channel_id=1, source_target_pairs={{0,0},{1,2},{2,1},{3,3},{4,64},{5,66},{6,65},{7,67},{8,32},{9,34},... | collective-permute-start | bytes 786440 | tf_op jit(solution)/shard_map/ppermute | solution.py:340
  90.1 4.0 %collective-permute-start.15 = (bf16[16,64,128]{2,1,0:T(8,128)(2,1)S(1)}, bf16[16,64,128]{2,1,0:T(8,128)(2,1)S(1)}, u32[]{:S(2)}, u32[]{:S(2)}) collective-permute-start(bf16[16,64,128]{2,1,0:T(8,128)(2,1)S(1)} %shard_map.84.token), channel_id=1, source_target_pairs={{0,0},{1,2},{2,1},{3,3},{4,64},{5,66},{6,65},{7,67},{8,32},{9,34},... | collective-permute-start | bytes 786440 | tf_op jit(solution)/shard_map/ppermute | solution.py:340
  94.2 2.2 %shard_map.85 = (f32[32,32,128]{2,1,0:T(8,128)S(1)}, bf16[32,32,128]{2,1,0:T(8,128)(2,1)S(1)}) custom-call(bf16[32,32,128]{2,1,0:T(8,128)(2,1)S(1)} %collective-permute-done.16.adjoint, bf16[13,64,64,128]{3,2,1,0:T(8,128)(2,1)S(1)} %bitcast.27, bf16[16,64,128]{2,1,0:T(8,128)(2,1)S(1)} %shard_map.84.token), custom_call_target="tpu_custom_call" | custom-call | flops 234881024 | bytes 7340032 | tf_op jit(solution)/shard_map/pallas_call | solution.py:408
  98.2 2.3 %shard_map.86 = (bf16[64,32,128]{2,1,0:T(8,128)(2,1)S(1)}, bf16[32,32,128]{2,1,0:T(8,128)(2,1)S(1)}) custom-call(bf16[16,64,128]{2,1,0:T(8,128)(2,1)S(1)} %collective-permute-done.15.coeffs, bf16[64,64,128]{2,1,0:T(8,128)(2,1)S(1)} %bitcast.45, bf16[64,64,128]{2,1,0:T(8,128)(2,1)S(1)} %shard_map.77.refs_0_.wanted, ...), custom_call_target="tpu_custom_call" | custom-call | flops 67108864 | bytes 4194304 | tf_op jit(solution)/shard_map/pallas_call | solution.py:364
  100.5 3.3 %collective-permute-done.18.received = bf16[32,32,128]{2,1,0:T(8,128)(2,1)S(1)} collective-permute-done((bf16[32,32,128]{2,1,0:T(8,128)(2,1)S(1)}, bf16[32,32,128]{2,1,0:T(8,128)(2,1)S(1)}, u32[]{:S(2)}, u32[]{:S(2)}) %collective-permute-start.18) | collective-permute-done | bytes 262176 | tf_op jit(solution)/shard_map/ppermute | solution.py:330
  104.3 17.9 %collective-permute-start.19 = (bf16[32,32,128]{2,1,0:T(8,128)(2,1)S(1)}, bf16[32,32,128]{2,1,0:T(8,128)(2,1)S(1)}, u32[]{:S(2)}, u32[]{:S(2)}) collective-permute-start(bf16[32,32,128]{2,1,0:T(8,128)(2,1)S(1)} %get-tuple-element.51.refs_0_), channel_id=1, source_target_pairs={{0,64},{2,66},{4,68},{6,70},{8,72},{10,74},{12,76},{14,78},{16,80}... | collective-permute-start | bytes 786440 | tf_op jit(solution)/shard_map/ppermute | solution.py:330
  122.2 5.3 %collective-permute-start.17 = (bf16[32,32,128]{2,1,0:T(8,128)(2,1)S(1)}, bf16[32,32,128]{2,1,0:T(8,128)(2,1)S(1)}, u32[]{:S(2)}, u32[]{:S(2)}) collective-permute-start(bf16[32,32,128]{2,1,0:T(8,128)(2,1)S(1)} %get-tuple-element.48.refs_0_), channel_id=1, source_target_pairs={{0,0},{1,2},{2,1},{3,3},{4,64},{5,66},{6,65},{7,67},{8,32},{9,34},... | collective-permute-start | bytes 786440 | tf_op jit(solution)/shard_map/ppermute | solution.py:340
  128.1 3.3 %collective-permute-start.21 = (bf16[32,32,128]{2,1,0:T(8,128)(2,1)S(1)}, bf16[32,32,128]{2,1,0:T(8,128)(2,1)S(1)}, u32[]{:S(2)}, u32[]{:S(2)}) collective-permute-start(bf16[32,32,128]{2,1,0:T(8,128)(2,1)S(1)} %get-tuple-element.52.token), channel_id=1, source_target_pairs={{0,32},{2,34},{4,36},{6,38},{8,40},{10,42},{12,44},{14,46},{16,48}... | collective-permute-start | bytes 786440 | tf_op jit(solution)/shard_map/ppermute | solution.py:330
  133.9 11.4 %collective-permute-done.21.received = bf16[32,32,128]{2,1,0:T(8,128)(2,1)S(1)} collective-permute-done((bf16[32,32,128]{2,1,0:T(8,128)(2,1)S(1)}, bf16[32,32,128]{2,1,0:T(8,128)(2,1)S(1)}, u32[]{:S(2)}, u32[]{:S(2)}) %collective-permute-start.21) | collective-permute-done | bytes 262176 | tf_op jit(solution)/shard_map/ppermute | solution.py:330
  145.7 3.0 %collective-permute-start.23 = (bf16[32,32,128]{2,1,0:T(8,128)(2,1)S(1)}, bf16[32,32,128]{2,1,0:T(8,128)(2,1)S(1)}, u32[]{:S(2)}, u32[]{:S(2)}) collective-permute-start(bf16[32,32,128]{2,1,0:T(8,128)(2,1)S(1)} %get-tuple-element.57.token), channel_id=1, source_target_pairs={{0,16},{2,18},{4,20},{6,22},{8,24},{10,26},{12,28},{14,30},{16,0},... | collective-permute-start | bytes 786440 | tf_op jit(solution)/shard_map/ppermute | solution.py:330
  151.1 3.7 %collective-permute-done.23.received = bf16[32,32,128]{2,1,0:T(8,128)(2,1)S(1)} collective-permute-done((bf16[32,32,128]{2,1,0:T(8,128)(2,1)S(1)}, bf16[32,32,128]{2,1,0:T(8,128)(2,1)S(1)}, u32[]{:S(2)}, u32[]{:S(2)}) %collective-permute-start.23) | collective-permute-done | bytes 262176 | tf_op jit(solution)/shard_map/ppermute | solution.py:330
  155.4 2.7 %collective-permute-start.25 = (bf16[32,32,128]{2,1,0:T(8,128)(2,1)S(1)}, bf16[32,32,128]{2,1,0:T(8,128)(2,1)S(1)}, u32[]{:S(2)}, u32[]{:S(2)}) collective-permute-start(bf16[32,32,128]{2,1,0:T(8,128)(2,1)S(1)} %get-tuple-element.62.refs_0_), channel_id=1, source_target_pairs={{0,8},{2,10},{4,12},{6,14},{8,0},{10,2},{12,4},{14,6},{16,24},{18,... | collective-permute-start | bytes 786440 | tf_op jit(solution)/shard_map/ppermute | solution.py:330
  162.7 2.5 %collective-permute-start.27 = (bf16[32,32,128]{2,1,0:T(8,128)(2,1)S(1)}, bf16[32,32,128]{2,1,0:T(8,128)(2,1)S(1)}, u32[]{:S(2)}, u32[]{:S(2)}) collective-permute-start(bf16[32,32,128]{2,1,0:T(8,128)(2,1)S(1)} %get-tuple-element.66.refs_0_), channel_id=1, source_target_pairs={{0,4},{2,6},{4,0},{6,2},{8,12},{10,14},{12,8},{14,10},{16,20},{18,... | collective-permute-start | bytes 786440 | tf_op jit(solution)/shard_map/ppermute | solution.py:330
  171.0 3.4 %collective-permute-start.29 = (bf16[32,32,128]{2,1,0:T(8,128)(2,1)S(1)}, bf16[32,32,128]{2,1,0:T(8,128)(2,1)S(1)}, u32[]{:S(2)}, u32[]{:S(2)}) collective-permute-start(bf16[32,32,128]{2,1,0:T(8,128)(2,1)S(1)} %get-tuple-element.73.refs_0_), channel_id=1, source_target_pairs={{0,2},{2,0},{4,6},{6,4},{8,10},{10,8},{12,14},{14,12},{16,18},{18,... | collective-permute-start | bytes 786440 | tf_op jit(solution)/shard_map/ppermute | solution.py:330
  174.8 5.2 %collective-permute-start.28 = (bf16[32,32,128]{2,1,0:T(8,128)(2,1)S(1)}, bf16[32,32,128]{2,1,0:T(8,128)(2,1)S(1)}, u32[]{:S(2)}, u32[]{:S(2)}) collective-permute-start(bf16[32,32,128]{2,1,0:T(8,128)(2,1)S(1)} %get-tuple-element.75.token), channel_id=1, source_target_pairs={{0,8},{2,10},{4,12},{6,14},{8,0},{10,2},{12,4},{14,6},{16,24},{18,... | collective-permute-start | bytes 786440 | tf_op jit(solution)/shard_map/ppermute | solution.py:330
  186.2 5.0 %collective-permute-done.30.received = bf16[32,32,128]{2,1,0:T(8,128)(2,1)S(1)} collective-permute-done((bf16[32,32,128]{2,1,0:T(8,128)(2,1)S(1)}, bf16[32,32,128]{2,1,0:T(8,128)(2,1)S(1)}, u32[]{:S(2)}, u32[]{:S(2)}) %collective-permute-start.30) | collective-permute-done | bytes 262176 | tf_op jit(solution)/shard_map/ppermute | solution.py:330
  191.7 6.3 %collective-permute-start.31 = (bf16[32,32,128]{2,1,0:T(8,128)(2,1)S(1)}, bf16[32,32,128]{2,1,0:T(8,128)(2,1)S(1)}, u32[]{:S(2)}, u32[]{:S(2)}) collective-permute-start(bf16[32,32,128]{2,1,0:T(8,128)(2,1)S(1)} %get-tuple-element.81.token), channel_id=1, source_target_pairs={{0,2},{2,0},{4,6},{6,4},{8,10},{10,8},{12,14},{14,12},{16,18},{18,... | collective-permute-start | bytes 786440 | tf_op jit(solution)/shard_map/ppermute | solution.py:330
  199.1 2.3 %shard_map.103 = (bf16[64,64,128]{2,1,0:T(8,128)(2,1)}, f32[8,128]{1,0:T(8,128)}) custom-call(f32[32,32,128]{2,1,0:T(8,128)S(1)} %get-tuple-element.80.held_part, bf16[32,32,128]{2,1,0:T(8,128)(2,1)S(1)} %collective-permute-done.31.received, bf16[64,64,128]{2,1,0:T(8,128)(2,1)S(1)} %bitcast.43, ...), custom_call_target="tpu_custom_call", output_to_operand_aliasing={{0}: (4, {})} | custom-call | flops 33554432 | bytes 2097152 | tf_op jit(solution)/shard_map/pallas_call | solution.py:379
  (81 shorter events, 53.7 us)
Async XLA Ops:
  5.5 4.1 %collective-permute-start.1 = (bf16[16,64,128]{2,1,0:T(8,128)(2,1)S(1)}, bf16[16,64,128]{2,1,0:T(8,128)(2,1)S(1)}, u32[]{:S(2)}, u32[]{:S(2)}) collective-permute-start(bf16[16,64,128]{2,1,0:T(8,128)(2,1)S(1)} %get-tuple-element.44.own.refs_0_), channel_id=1, source_target_pairs={{0,2},{2,0},{4,6},{6,4},{8,10},{10,8},{12,14},{14,12},{16,18},{18,... | collective-permute-start | bytes 786440 | tf_op jit(solution)/shard_map/ppermute | solution.py:330
  10.0 8.0 %collective-permute-start.2 = (bf16[16,64,128]{2,1,0:T(8,128)(2,1)S(1)}, bf16[16,64,128]{2,1,0:T(8,128)(2,1)S(1)}, u32[]{:S(2)}, u32[]{:S(2)}) collective-permute-start(bf16[16,64,128]{2,1,0:T(8,128)(2,1)S(1)} %shard_map.69.own.refs_0_), channel_id=1, source_target_pairs={{0,4},{2,6},{4,0},{6,2},{8,12},{10,14},{12,8},{14,10},{16,20},{18,... | collective-permute-start | bytes 786440 | tf_op jit(solution)/shard_map/ppermute | solution.py:330
  18.4 8.6 %collective-permute-start.3 = (bf16[16,64,128]{2,1,0:T(8,128)(2,1)S(1)}, bf16[16,64,128]{2,1,0:T(8,128)(2,1)S(1)}, u32[]{:S(2)}, u32[]{:S(2)}) collective-permute-start(bf16[16,64,128]{2,1,0:T(8,128)(2,1)S(1)} %shard_map.70.own.refs_0_), channel_id=1, source_target_pairs={{0,8},{2,10},{4,12},{6,14},{8,0},{10,2},{12,4},{14,6},{16,24},{18,... | collective-permute-start | bytes 786440 | tf_op jit(solution)/shard_map/ppermute | solution.py:330
  21.3 9.9 %collective-permute-start = (bf16[16,64,128]{2,1,0:T(8,128)(2,1)S(1)}, bf16[16,64,128]{2,1,0:T(8,128)(2,1)S(1)}, u32[]{:S(2)}, u32[]{:S(2)}) collective-permute-start(bf16[16,64,128]{2,1,0:T(8,128)(2,1)S(1)} %get-tuple-element.43.own), channel_id=1, source_target_pairs={{0,2},{2,0},{4,6},{6,4},{8,10},{10,8},{12,14},{14,12},{16,18},{18,... | collective-permute-start | bytes 786440 | tf_op jit(solution)/shard_map/ppermute | solution.py:330
  27.5 8.7 %collective-permute-start.5 = (bf16[16,64,128]{2,1,0:T(8,128)(2,1)S(1)}, bf16[16,64,128]{2,1,0:T(8,128)(2,1)S(1)}, u32[]{:S(2)}, u32[]{:S(2)}) collective-permute-start(bf16[16,64,128]{2,1,0:T(8,128)(2,1)S(1)} %shard_map.71.refs_0_.own), channel_id=1, source_target_pairs={{0,16},{2,18},{4,20},{6,22},{8,24},{10,26},{12,28},{14,30},{16,0},... | collective-permute-start | bytes 786440 | tf_op jit(solution)/shard_map/ppermute | solution.py:330
  31.7 6.3 %collective-permute-start.4 = (bf16[16,64,128]{2,1,0:T(8,128)(2,1)S(1)}, bf16[16,64,128]{2,1,0:T(8,128)(2,1)S(1)}, u32[]{:S(2)}, u32[]{:S(2)}) collective-permute-start(bf16[16,64,128]{2,1,0:T(8,128)(2,1)S(1)} %shard_map.72.refs_0_.own), channel_id=1, source_target_pairs={{0,4},{2,6},{4,0},{6,2},{8,12},{10,14},{12,8},{14,10},{16,20},{18,... | collective-permute-start | bytes 786440 | tf_op jit(solution)/shard_map/ppermute | solution.py:330
  36.6 5.3 %collective-permute-start.7 = (bf16[16,64,128]{2,1,0:T(8,128)(2,1)S(1)}, bf16[16,64,128]{2,1,0:T(8,128)(2,1)S(1)}, u32[]{:S(2)}, u32[]{:S(2)}) collective-permute-start(bf16[16,64,128]{2,1,0:T(8,128)(2,1)S(1)} %shard_map.73.refs_0_.own), channel_id=1, source_target_pairs={{0,32},{2,34},{4,36},{6,38},{8,40},{10,42},{12,44},{14,46},{16,48}... | collective-permute-start | bytes 786440 | tf_op jit(solution)/shard_map/ppermute | solution.py:330
  38.5 6.9 %collective-permute-start.6 = (bf16[16,64,128]{2,1,0:T(8,128)(2,1)S(1)}, bf16[16,64,128]{2,1,0:T(8,128)(2,1)S(1)}, u32[]{:S(2)}, u32[]{:S(2)}) collective-permute-start(bf16[16,64,128]{2,1,0:T(8,128)(2,1)S(1)} %shard_map.74.refs_0_.own), channel_id=1, source_target_pairs={{0,8},{2,10},{4,12},{6,14},{8,0},{10,2},{12,4},{14,6},{16,24},{18,... | collective-permute-start | bytes 786440 | tf_op jit(solution)/shard_map/ppermute | solution.py:330
  42.4 7.6 %collective-permute-start.9 = (bf16[16,64,128]{2,1,0:T(8,128)(2,1)S(1)}, bf16[16,64,128]{2,1,0:T(8,128)(2,1)S(1)}, u32[]{:S(2)}, u32[]{:S(2)}) collective-permute-start(bf16[16,64,128]{2,1,0:T(8,128)(2,1)S(1)} %shard_map.75.refs_0_.own), channel_id=1, source_target_pairs={{0,64},{2,66},{4,68},{6,70},{8,72},{10,74},{12,76},{14,78},{16,80}... | collective-permute-start | bytes 786440 | tf_op jit(solution)/shard_map/ppermute | solution.py:330
  45.8 7.1 %collective-permute-start.8 = (bf16[16,64,128]{2,1,0:T(8,128)(2,1)S(1)}, bf16[16,64,128]{2,1,0:T(8,128)(2,1)S(1)}, u32[]{:S(2)}, u32[]{:S(2)}) collective-permute-start(bf16[16,64,128]{2,1,0:T(8,128)(2,1)S(1)} %shard_map.76.token.own), channel_id=1, source_target_pairs={{0,16},{2,18},{4,20},{6,22},{8,24},{10,26},{12,28},{14,30},{16,0},... | collective-permute-start | bytes 786440 | tf_op jit(solution)/shard_map/ppermute | solution.py:330
  50.4 6.8 %collective-permute-start.11 = (bf16[16,64,128]{2,1,0:T(8,128)(2,1)S(1)}, bf16[16,64,128]{2,1,0:T(8,128)(2,1)S(1)}, u32[]{:S(2)}, u32[]{:S(2)}) collective-permute-start(bf16[16,64,128]{2,1,0:T(8,128)(2,1)S(1)} %shard_map.78.refs_0_.own), channel_id=1, source_target_pairs={{0,1},{1,0},{2,3},{3,2},{4,5},{5,4},{6,7},{7,6},{8,9},{9,8},{10,11... | collective-permute-start | bytes 786440 | tf_op jit(solution)/shard_map/ppermute | solution.py:330
  53.4 6.0 %collective-permute-start.10 = (bf16[16,64,128]{2,1,0:T(8,128)(2,1)S(1)}, bf16[16,64,128]{2,1,0:T(8,128)(2,1)S(1)}, u32[]{:S(2)}, u32[]{:S(2)}) collective-permute-start(bf16[16,64,128]{2,1,0:T(8,128)(2,1)S(1)} %shard_map.79.token.own), channel_id=1, source_target_pairs={{0,32},{2,34},{4,36},{6,38},{8,40},{10,42},{12,44},{14,46},{16,48}... | collective-permute-start | bytes 786440 | tf_op jit(solution)/shard_map/ppermute | solution.py:330
  59.8 17.4 %collective-permute-start.12 = (bf16[16,64,128]{2,1,0:T(8,128)(2,1)S(1)}, bf16[16,64,128]{2,1,0:T(8,128)(2,1)S(1)}, u32[]{:S(2)}, u32[]{:S(2)}) collective-permute-start(bf16[16,64,128]{2,1,0:T(8,128)(2,1)S(1)} %shard_map.81.own.refs_0_), channel_id=1, source_target_pairs={{0,64},{2,66},{4,68},{6,70},{8,72},{10,74},{12,76},{14,78},{16,80}... | collective-permute-start | bytes 786440 | tf_op jit(solution)/shard_map/ppermute | solution.py:330
  62.4 19.9 %collective-permute-start.14 = (bf16[16,64,128]{2,1,0:T(8,128)(2,1)S(1)}, bf16[16,64,128]{2,1,0:T(8,128)(2,1)S(1)}, u32[]{:S(2)}, u32[]{:S(2)}) collective-permute-start(bf16[16,64,128]{2,1,0:T(8,128)(2,1)S(1)} %shard_map.80.refs_0_), channel_id=1, source_target_pairs={{0,0},{1,2},{2,1},{3,3},{4,64},{5,66},{6,65},{7,67},{8,32},{9,34},... | collective-permute-start | bytes 786440 | tf_op jit(solution)/shard_map/ppermute | solution.py:340
  77.7 10.2 %collective-permute-start.13 = (bf16[16,64,128]{2,1,0:T(8,128)(2,1)S(1)}, bf16[16,64,128]{2,1,0:T(8,128)(2,1)S(1)}, u32[]{:S(2)}, u32[]{:S(2)}) collective-permute-start(bf16[16,64,128]{2,1,0:T(8,128)(2,1)S(1)} %shard_map.82.token.own), channel_id=1, source_target_pairs={{0,1},{1,0},{2,3},{3,2},{4,5},{5,4},{6,7},{7,6},{8,9},{9,8},{10,11... | collective-permute-start | bytes 786440 | tf_op jit(solution)/shard_map/ppermute | solution.py:330
  84.6 9.6 %collective-permute-start.16 = (bf16[32,32,128]{2,1,0:T(8,128)(2,1)S(1)}, bf16[32,32,128]{2,1,0:T(8,128)(2,1)S(1)}, u32[]{:S(2)}, u32[]{:S(2)}) collective-permute-start(bf16[32,32,128]{2,1,0:T(8,128)(2,1)S(1)} %get-tuple-element.45.token), channel_id=1, source_target_pairs={{0,0},{1,2},{2,1},{3,3},{4,64},{5,66},{6,65},{7,67},{8,32},{9,34},... | collective-permute-start | bytes 786440 | tf_op jit(solution)/shard_map/ppermute | solution.py:340
  90.1 8.1 %collective-permute-start.15 = (bf16[16,64,128]{2,1,0:T(8,128)(2,1)S(1)}, bf16[16,64,128]{2,1,0:T(8,128)(2,1)S(1)}, u32[]{:S(2)}, u32[]{:S(2)}) collective-permute-start(bf16[16,64,128]{2,1,0:T(8,128)(2,1)S(1)} %shard_map.84.token), channel_id=1, source_target_pairs={{0,0},{1,2},{2,1},{3,3},{4,64},{5,66},{6,65},{7,67},{8,32},{9,34},... | collective-permute-start | bytes 786440 | tf_op jit(solution)/shard_map/ppermute | solution.py:340
  96.4 7.5 %collective-permute-start.18 = (bf16[32,32,128]{2,1,0:T(8,128)(2,1)S(1)}, bf16[32,32,128]{2,1,0:T(8,128)(2,1)S(1)}, u32[]{:S(2)}, u32[]{:S(2)}) collective-permute-start(bf16[32,32,128]{2,1,0:T(8,128)(2,1)S(1)} %get-tuple-element.46.token), channel_id=1, source_target_pairs={{0,1},{1,0},{2,3},{3,2},{4,5},{5,4},{6,7},{7,6},{8,9},{9,8},{10,11... | collective-permute-start | bytes 786440 | tf_op jit(solution)/shard_map/ppermute | solution.py:330
  104.3 23.2 %collective-permute-start.19 = (bf16[32,32,128]{2,1,0:T(8,128)(2,1)S(1)}, bf16[32,32,128]{2,1,0:T(8,128)(2,1)S(1)}, u32[]{:S(2)}, u32[]{:S(2)}) collective-permute-start(bf16[32,32,128]{2,1,0:T(8,128)(2,1)S(1)} %get-tuple-element.51.refs_0_), channel_id=1, source_target_pairs={{0,64},{2,66},{4,68},{6,70},{8,72},{10,74},{12,76},{14,78},{16,80}... | collective-permute-start | bytes 786440 | tf_op jit(solution)/shard_map/ppermute | solution.py:330
  122.2 9.4 %collective-permute-start.17 = (bf16[32,32,128]{2,1,0:T(8,128)(2,1)S(1)}, bf16[32,32,128]{2,1,0:T(8,128)(2,1)S(1)}, u32[]{:S(2)}, u32[]{:S(2)}) collective-permute-start(bf16[32,32,128]{2,1,0:T(8,128)(2,1)S(1)} %get-tuple-element.48.refs_0_), channel_id=1, source_target_pairs={{0,0},{1,2},{2,1},{3,3},{4,64},{5,66},{6,65},{7,67},{8,32},{9,34},... | collective-permute-start | bytes 786440 | tf_op jit(solution)/shard_map/ppermute | solution.py:340
  128.1 17.1 %collective-permute-start.21 = (bf16[32,32,128]{2,1,0:T(8,128)(2,1)S(1)}, bf16[32,32,128]{2,1,0:T(8,128)(2,1)S(1)}, u32[]{:S(2)}, u32[]{:S(2)}) collective-permute-start(bf16[32,32,128]{2,1,0:T(8,128)(2,1)S(1)} %get-tuple-element.52.token), channel_id=1, source_target_pairs={{0,32},{2,34},{4,36},{6,38},{8,40},{10,42},{12,44},{14,46},{16,48}... | collective-permute-start | bytes 786440 | tf_op jit(solution)/shard_map/ppermute | solution.py:330
  133.8 16.8 %collective-permute-start.20 = (bf16[32,32,128]{2,1,0:T(8,128)(2,1)S(1)}, bf16[32,32,128]{2,1,0:T(8,128)(2,1)S(1)}, u32[]{:S(2)}, u32[]{:S(2)}) collective-permute-start(bf16[32,32,128]{2,1,0:T(8,128)(2,1)S(1)} %get-tuple-element.54.refs_0_), channel_id=1, source_target_pairs={{0,1},{1,0},{2,3},{3,2},{4,5},{5,4},{6,7},{7,6},{8,9},{9,8},{10,11... | collective-permute-start | bytes 786440 | tf_op jit(solution)/shard_map/ppermute | solution.py:330
  145.7 9.2 %collective-permute-start.23 = (bf16[32,32,128]{2,1,0:T(8,128)(2,1)S(1)}, bf16[32,32,128]{2,1,0:T(8,128)(2,1)S(1)}, u32[]{:S(2)}, u32[]{:S(2)}) collective-permute-start(bf16[32,32,128]{2,1,0:T(8,128)(2,1)S(1)} %get-tuple-element.57.token), channel_id=1, source_target_pairs={{0,16},{2,18},{4,20},{6,22},{8,24},{10,26},{12,28},{14,30},{16,0},... | collective-permute-start | bytes 786440 | tf_op jit(solution)/shard_map/ppermute | solution.py:330
  151.1 8.8 %collective-permute-start.22 = (bf16[32,32,128]{2,1,0:T(8,128)(2,1)S(1)}, bf16[32,32,128]{2,1,0:T(8,128)(2,1)S(1)}, u32[]{:S(2)}, u32[]{:S(2)}) collective-permute-start(bf16[32,32,128]{2,1,0:T(8,128)(2,1)S(1)} %get-tuple-element.60.refs_0_), channel_id=1, source_target_pairs={{0,64},{2,66},{4,68},{6,70},{8,72},{10,74},{12,76},{14,78},{16,80}... | collective-permute-start | bytes 786440 | tf_op jit(solution)/shard_map/ppermute | solution.py:330
  155.4 6.8 %collective-permute-start.25 = (bf16[32,32,128]{2,1,0:T(8,128)(2,1)S(1)}, bf16[32,32,128]{2,1,0:T(8,128)(2,1)S(1)}, u32[]{:S(2)}, u32[]{:S(2)}) collective-permute-start(bf16[32,32,128]{2,1,0:T(8,128)(2,1)S(1)} %get-tuple-element.62.refs_0_), channel_id=1, source_target_pairs={{0,8},{2,10},{4,12},{6,14},{8,0},{10,2},{12,4},{14,6},{16,24},{18,... | collective-permute-start | bytes 786440 | tf_op jit(solution)/shard_map/ppermute | solution.py:330
  160.3 5.6 %collective-permute-start.24 = (bf16[32,32,128]{2,1,0:T(8,128)(2,1)S(1)}, bf16[32,32,128]{2,1,0:T(8,128)(2,1)S(1)}, u32[]{:S(2)}, u32[]{:S(2)}) collective-permute-start(bf16[32,32,128]{2,1,0:T(8,128)(2,1)S(1)} %get-tuple-element.64.refs_0_), channel_id=1, source_target_pairs={{0,32},{2,34},{4,36},{6,38},{8,40},{10,42},{12,44},{14,46},{16,48}... | collective-permute-start | bytes 786440 | tf_op jit(solution)/shard_map/ppermute | solution.py:330
  162.7 7.8 %collective-permute-start.27 = (bf16[32,32,128]{2,1,0:T(8,128)(2,1)S(1)}, bf16[32,32,128]{2,1,0:T(8,128)(2,1)S(1)}, u32[]{:S(2)}, u32[]{:S(2)}) collective-permute-start(bf16[32,32,128]{2,1,0:T(8,128)(2,1)S(1)} %get-tuple-element.66.refs_0_), channel_id=1, source_target_pairs={{0,4},{2,6},{4,0},{6,2},{8,12},{10,14},{12,8},{14,10},{16,20},{18,... | collective-permute-start | bytes 786440 | tf_op jit(solution)/shard_map/ppermute | solution.py:330
  166.5 7.9 %collective-permute-start.26 = (bf16[32,32,128]{2,1,0:T(8,128)(2,1)S(1)}, bf16[32,32,128]{2,1,0:T(8,128)(2,1)S(1)}, u32[]{:S(2)}, u32[]{:S(2)}) collective-permute-start(bf16[32,32,128]{2,1,0:T(8,128)(2,1)S(1)} %get-tuple-element.67.token), channel_id=1, source_target_pairs={{0,16},{2,18},{4,20},{6,22},{8,24},{10,26},{12,28},{14,30},{16,0},... | collective-permute-start | bytes 786440 | tf_op jit(solution)/shard_map/ppermute | solution.py:330
  171.0 9.1 %collective-permute-start.29 = (bf16[32,32,128]{2,1,0:T(8,128)(2,1)S(1)}, bf16[32,32,128]{2,1,0:T(8,128)(2,1)S(1)}, u32[]{:S(2)}, u32[]{:S(2)}) collective-permute-start(bf16[32,32,128]{2,1,0:T(8,128)(2,1)S(1)} %get-tuple-element.73.refs_0_), channel_id=1, source_target_pairs={{0,2},{2,0},{4,6},{6,4},{8,10},{10,8},{12,14},{14,12},{16,18},{18,... | collective-permute-start | bytes 786440 | tf_op jit(solution)/shard_map/ppermute | solution.py:330
  174.8 9.0 %collective-permute-start.28 = (bf16[32,32,128]{2,1,0:T(8,128)(2,1)S(1)}, bf16[32,32,128]{2,1,0:T(8,128)(2,1)S(1)}, u32[]{:S(2)}, u32[]{:S(2)}) collective-permute-start(bf16[32,32,128]{2,1,0:T(8,128)(2,1)S(1)} %get-tuple-element.75.token), channel_id=1, source_target_pairs={{0,8},{2,10},{4,12},{6,14},{8,0},{10,2},{12,4},{14,6},{16,24},{18,... | collective-permute-start | bytes 786440 | tf_op jit(solution)/shard_map/ppermute | solution.py:330
  184.3 6.8 %collective-permute-start.30 = (bf16[32,32,128]{2,1,0:T(8,128)(2,1)S(1)}, bf16[32,32,128]{2,1,0:T(8,128)(2,1)S(1)}, u32[]{:S(2)}, u32[]{:S(2)}) collective-permute-start(bf16[32,32,128]{2,1,0:T(8,128)(2,1)S(1)} %get-tuple-element.79.refs_0_), channel_id=1, source_target_pairs={{0,4},{2,6},{4,0},{6,2},{8,12},{10,14},{12,8},{14,10},{16,20},{18,... | collective-permute-start | bytes 786440 | tf_op jit(solution)/shard_map/ppermute | solution.py:330
  191.7 7.4 %collective-permute-start.31 = (bf16[32,32,128]{2,1,0:T(8,128)(2,1)S(1)}, bf16[32,32,128]{2,1,0:T(8,128)(2,1)S(1)}, u32[]{:S(2)}, u32[]{:S(2)}) collective-permute-start(bf16[32,32,128]{2,1,0:T(8,128)(2,1)S(1)} %get-tuple-element.81.token), channel_id=1, source_target_pairs={{0,2},{2,0},{4,6},{6,4},{8,10},{10,8},{12,14},{14,12},{16,18},{18,... | collective-permute-start | bytes 786440 | tf_op jit(solution)/shard_map/ppermute | solution.py:330
  (6 other events, 83.4 us)

commit v4 on v3

--- a/solution.py
+++ b/solution.py
@@ -10,7 +10,7 @@
 CHUNKS = 2
 PARTS = 4
 EARLY = 3
-LAG = 2
+LAG = 1
 GAP = 2
 LANES = 128
 BF = jnp.bfloat16

time: 202 us -> 192 us (0.950)
  starting transfers between devices: 103 us -> 94.2 us
    ppermute x4, starting transfers between devices: 27.6 us -> 17.4 us  [reversal(): return lax.ppermute(array, ('src', 'hi'), pairs_of)]
    ppermute x4, waiting for transfers between devices: 6.54 us -> 3.48 us  [reversal(): return lax.ppermute(array, ('src', 'hi'), pairs_of)]
    ppermute x28, waiting for transfers between devices: 49.8 us -> 51.9 us  [exchange(): return lax.ppermute(array, axis, [(i, i ^ 1 << bit) for i in range(count)])]
  transfers between devices with their start and end apart: 32 -> 32, of which waited for: 18 -> 16; matrix products, arithmetic and copies ran while one was open for 1% -> 1% of each run, Pallas kernels for 14% -> 14%
where the time goes in v4:
time: 192 us
  starting transfers between devices  94.2 us (49%)
  waiting for transfers between devices  55.4 us (29%)
  Pallas kernels  35.4 us (18%)
  local copies, waits for them, and re-layouts  5.39 us (3%)
    ppermute x28, starting transfers between devices, exchange(): return lax.ppermute(array, axis, [(i, i ^ 1 << bit) for i in range(count)])  76.8 us
    ppermute x28, waiting for transfers between devices, exchange(): return lax.ppermute(array, axis, [(i, i ^ 1 << bit) for i in range(count)])  51.9 us
    ppermute x4, starting transfers between devices, reversal(): return lax.ppermute(array, ('src', 'hi'), pairs_of)  17.4 us
    pallas_call x12, Pallas kernels, adjoint_call(): call(kernel, (kept_shape, pair_shape), specs, (VMEM, VMEM), [], flops, mo...  5.96 us
    pallas_call x12, Pallas kernels, cross_call(): call(kernel, forward_shape, specs, VMEM, [], flops, moved, 4)(*operands)  5.28 us
    pallas_call x2, Pallas kernels, target_call(): call(kernel, (shape(boxes, vectors, points), pair_shape), [VMEM] * 3 + [A...  4.55 us
    pallas_call x2, Pallas kernels, local_adjoint_call(): call(kernel, (kept_shape, pair_shape), [VMEM] * 2 + [ANY], (VMEM, VMEM),...  4.31 us
    pallas_call x2, Pallas kernels, local_forward_call(): call(kernel, forward_shape, [VMEM] * 3 + [ANY], VMEM, scratch, 7 * flops,...  4.28 us
  transfers between devices with their start and end apart: 32, of which 16 were waited for; matrix products, arithmetic and copies ran while one was open for 1% of the time, Pallas kernels for 14%

profile of v4, /device:TPU:1, one launch (start us, length us, event | category | flops | bytes accessed | tf_op | source)
XLA Modules:
  0.0 191.6 jit_solution(12022270433254852760)
XLA Ops:
  3.5 2.0 %shard_map.68 = (bf16[16,64,128]{2,1,0:T(8,128)(2,1)S(1)}, bf16[16,64,128]{2,1,0:T(8,128)(2,1)S(1)}) custom-call(bf16[64,64,128]{2,1,0:T(8,128)(2,1)S(1)} %bitcast.46, bf16[64,64,128]{2,1,0:T(8,128)(2,1)S(1)} %bitcast.41), custom_call_target="tpu_custom_call" | custom-call | flops 67108864 | bytes 4194304 | tf_op jit(solution)/shard_map/pallas_call | solution.py:347
  7.0 2.5 %slice_bitcast_fusion = (bf16[1,64,64,128]{3,2,1,0:T(8,128)(2,1)S(1)}, bf16[1,64,64,128]{3,2,1,0:T(8,128)(2,1)S(1)}, bf16[1,64,64,128]{3,2,1,0:T(8,128)(2,1)S(1)}) fusion(bf16[13,64,1,1,64,128]{5,4,1,3,2,0:T(8,128)(2,1)} %bitcast.18), kind=kLoop, calls=%fused_computation | loop fusion | bytes 6291456 | tf_op jit(solution)/shard_map/slice | solution.py:427
  11.7 6.3 %collective-permute-done.2.other = bf16[16,64,128]{2,1,0:T(8,128)(2,1)S(1)} collective-permute-done((bf16[16,64,128]{2,1,0:T(8,128)(2,1)S(1)}, bf16[16,64,128]{2,1,0:T(8,128)(2,1)S(1)}, u32[]{:S(2)}, u32[]{:S(2)}) %collective-permute-start.2) | collective-permute-done | bytes 262176 | tf_op jit(solution)/shard_map/ppermute | solution.py:330
  18.4 2.9 %collective-permute-start.4 = (bf16[16,64,128]{2,1,0:T(8,128)(2,1)S(1)}, bf16[16,64,128]{2,1,0:T(8,128)(2,1)S(1)}, u32[]{:S(2)}, u32[]{:S(2)}) collective-permute-start(bf16[16,64,128]{2,1,0:T(8,128)(2,1)S(1)} %shard_map.70.refs_0_.own), channel_id=1, source_target_pairs={{0,8},{2,10},{4,12},{6,14},{8,0},{10,2},{12,4},{14,6},{16,24},{18,... | collective-permute-start | bytes 786440 | tf_op jit(solution)/shard_map/ppermute | solution.py:330
  22.2 4.9 %collective-permute-done.4.other = bf16[16,64,128]{2,1,0:T(8,128)(2,1)S(1)} collective-permute-done((bf16[16,64,128]{2,1,0:T(8,128)(2,1)S(1)}, bf16[16,64,128]{2,1,0:T(8,128)(2,1)S(1)}, u32[]{:S(2)}, u32[]{:S(2)}) %collective-permute-start.4) | collective-permute-done | bytes 262176 | tf_op jit(solution)/shard_map/ppermute | solution.py:330
  27.5 3.8 %collective-permute-start.6 = (bf16[16,64,128]{2,1,0:T(8,128)(2,1)S(1)}, bf16[16,64,128]{2,1,0:T(8,128)(2,1)S(1)}, u32[]{:S(2)}, u32[]{:S(2)}) collective-permute-start(bf16[16,64,128]{2,1,0:T(8,128)(2,1)S(1)} %shard_map.72.refs_0_.own), channel_id=1, source_target_pairs={{0,16},{2,18},{4,20},{6,22},{8,24},{10,26},{12,28},{14,30},{16,0},... | collective-permute-start | bytes 786440 | tf_op jit(solution)/shard_map/ppermute | solution.py:330
  36.9 4.0 %collective-permute-done.5.other = bf16[16,64,128]{2,1,0:T(8,128)(2,1)S(1)} collective-permute-done((bf16[16,64,128]{2,1,0:T(8,128)(2,1)S(1)}, bf16[16,64,128]{2,1,0:T(8,128)(2,1)S(1)}, u32[]{:S(2)}, u32[]{:S(2)}) %collective-permute-start.5) | collective-permute-done | bytes 262176 | tf_op jit(solution)/shard_map/ppermute | solution.py:330
  41.4 3.7 %collective-permute-start.7 = (bf16[16,64,128]{2,1,0:T(8,128)(2,1)S(1)}, bf16[16,64,128]{2,1,0:T(8,128)(2,1)S(1)}, u32[]{:S(2)}, u32[]{:S(2)}) collective-permute-start(bf16[16,64,128]{2,1,0:T(8,128)(2,1)S(1)} %shard_map.75.token.own), channel_id=1, source_target_pairs={{0,16},{2,18},{4,20},{6,22},{8,24},{10,26},{12,28},{14,30},{16,0},... | collective-permute-start | bytes 786440 | tf_op jit(solution)/shard_map/ppermute | solution.py:330
  47.0 3.0 %collective-permute-start.10 = (bf16[16,64,128]{2,1,0:T(8,128)(2,1)S(1)}, bf16[16,64,128]{2,1,0:T(8,128)(2,1)S(1)}, u32[]{:S(2)}, u32[]{:S(2)}) collective-permute-start(bf16[16,64,128]{2,1,0:T(8,128)(2,1)S(1)} %shard_map.77.refs_0_.own), channel_id=1, source_target_pairs={{0,64},{2,66},{4,68},{6,70},{8,72},{10,74},{12,76},{14,78},{16,80}... | collective-permute-start | bytes 786440 | tf_op jit(solution)/shard_map/ppermute | solution.py:330
  50.9 2.9 %collective-permute-done.10.other = bf16[16,64,128]{2,1,0:T(8,128)(2,1)S(1)} collective-permute-done((bf16[16,64,128]{2,1,0:T(8,128)(2,1)S(1)}, bf16[16,64,128]{2,1,0:T(8,128)(2,1)S(1)}, u32[]{:S(2)}, u32[]{:S(2)}) %collective-permute-start.10) | collective-permute-done | bytes 262176 | tf_op jit(solution)/shard_map/ppermute | solution.py:330
  55.0 4.4 %collective-permute-done.9.other = bf16[16,64,128]{2,1,0:T(8,128)(2,1)S(1)} collective-permute-done((bf16[16,64,128]{2,1,0:T(8,128)(2,1)S(1)}, bf16[16,64,128]{2,1,0:T(8,128)(2,1)S(1)}, u32[]{:S(2)}, u32[]{:S(2)}) %collective-permute-start.9) | collective-permute-done | bytes 262176 | tf_op jit(solution)/shard_map/ppermute | solution.py:330
  61.7 2.1 %shard_map.81.refs_0_ = bf16[16,64,128]{2,1,0:T(8,128)(2,1)S(1)} custom-call(bf16[16,64,128]{2,1,0:T(8,128)(2,1)S(1)} %shard_map.79.refs_0_.own, bf16[16,64,128]{2,1,0:T(8,128)(2,1)S(1)} %collective-permute-done.12.other, bf16[13,64,64,128]{3,2,1,0:T(8,128)(2,1)S(1)} %bitcast.24, bf16[16,64,128]{2,1,0:T(8,128)(2,1)S(1)} %shard_map.80.token.own), custom_call_target="tpu_custom_call" | custom-call | flops 234881024 | bytes 7340032 | tf_op jit(solution)/shard_map/pallas_call | solution.py:401
  63.8 3.0 %collective-permute-done.11.other = bf16[16,64,128]{2,1,0:T(8,128)(2,1)S(1)} collective-permute-done((bf16[16,64,128]{2,1,0:T(8,128)(2,1)S(1)}, bf16[16,64,128]{2,1,0:T(8,128)(2,1)S(1)}, u32[]{:S(2)}, u32[]{:S(2)}) %collective-permute-start.11) | collective-permute-done | bytes 262176 | tf_op jit(solution)/shard_map/ppermute | solution.py:330
  68.1 7.8 %collective-permute-start.15 = (bf16[16,64,128]{2,1,0:T(8,128)(2,1)S(1)}, bf16[16,64,128]{2,1,0:T(8,128)(2,1)S(1)}, u32[]{:S(2)}, u32[]{:S(2)}) collective-permute-start(bf16[16,64,128]{2,1,0:T(8,128)(2,1)S(1)} %shard_map.81.refs_0_), channel_id=1, source_target_pairs={{0,0},{1,2},{2,1},{3,3},{4,64},{5,66},{6,65},{7,67},{8,32},{9,34},... | collective-permute-start | bytes 786440 | tf_op jit(solution)/shard_map/ppermute | solution.py:340
  75.9 2.1 %shard_map.83.token = bf16[16,64,128]{2,1,0:T(8,128)(2,1)S(1)} custom-call(bf16[16,64,128]{2,1,0:T(8,128)(2,1)S(1)} %shard_map.82.own.token, bf16[16,64,128]{2,1,0:T(8,128)(2,1)S(1)} %collective-permute-done.13.other, bf16[13,64,64,128]{3,2,1,0:T(8,128)(2,1)S(1)} %bitcast.26, bf16[16,64,128]{2,1,0:T(8,128)(2,1)S(1)} %shard_map.82.own.token), custom_call_target="tpu_custom_call" | custom-call | flops 234881024 | bytes 7340032 | tf_op jit(solution)/shard_map/pallas_call | solution.py:401
  78.0 5.8 %collective-permute-start.14 = (bf16[16,64,128]{2,1,0:T(8,128)(2,1)S(1)}, bf16[16,64,128]{2,1,0:T(8,128)(2,1)S(1)}, u32[]{:S(2)}, u32[]{:S(2)}) collective-permute-start(bf16[16,64,128]{2,1,0:T(8,128)(2,1)S(1)} %shard_map.83.token), channel_id=1, source_target_pairs={{0,0},{1,2},{2,1},{3,3},{4,64},{5,66},{6,65},{7,67},{8,32},{9,34},... | collective-permute-start | bytes 786440 | tf_op jit(solution)/shard_map/ppermute | solution.py:340
  83.8 2.3 %shard_map.84 = (bf16[64,32,128]{2,1,0:T(8,128)(2,1)S(1)}, bf16[32,32,128]{2,1,0:T(8,128)(2,1)S(1)}) custom-call(bf16[16,64,128]{2,1,0:T(8,128)(2,1)S(1)} %collective-permute-done.15.coeffs, bf16[64,64,128]{2,1,0:T(8,128)(2,1)S(1)} %bitcast.44, bf16[64,64,128]{2,1,0:T(8,128)(2,1)S(1)} %shard_map.76.refs_0_.wanted, bf16[16,64,128]{2,1,0:T(8,128)(2,1)S(1)} %shard_map.83.token), custom_call_target="tpu_custom_call" | custom-call | flops 67108864 | bytes 4194304 | tf_op jit(solution)/shard_map/pallas_call | solution.py:364
  88.0 2.3 %shard_map.85 = (bf16[64,32,128]{2,1,0:T(8,128)(2,1)S(1)}, bf16[32,32,128]{2,1,0:T(8,128)(2,1)S(1)}) custom-call(bf16[16,64,128]{2,1,0:T(8,128)(2,1)S(1)} %collective-permute-done.14.coeffs, bf16[64,64,128]{2,1,0:T(8,128)(2,1)S(1)} %bitcast.45, bf16[64,64,128]{2,1,0:T(8,128)(2,1)S(1)} %shard_map.76.refs_0_.wanted, ...), custom_call_target="tpu_custom_call" | custom-call | flops 67108864 | bytes 4194304 | tf_op jit(solution)/shard_map/pallas_call | solution.py:364
  90.3 3.5 %collective-permute-done.17.adjoint = bf16[32,32,128]{2,1,0:T(8,128)(2,1)S(1)} collective-permute-done((bf16[32,32,128]{2,1,0:T(8,128)(2,1)S(1)}, bf16[32,32,128]{2,1,0:T(8,128)(2,1)S(1)}, u32[]{:S(2)}, u32[]{:S(2)}) %collective-permute-start.17) | collective-permute-done | bytes 262176 | tf_op jit(solution)/shard_map/ppermute | solution.py:340
  93.8 2.1 %shard_map.86 = (f32[32,32,128]{2,1,0:T(8,128)S(1)}, bf16[32,32,128]{2,1,0:T(8,128)(2,1)S(1)}) custom-call(bf16[32,32,128]{2,1,0:T(8,128)(2,1)S(1)} %collective-permute-done.17.adjoint, bf16[13,64,64,128]{3,2,1,0:T(8,128)(2,1)S(1)} %bitcast.27, bf16[32,32,128]{2,1,0:T(8,128)(2,1)S(1)} %get-tuple-element.47.token), custom_call_target="tpu_custom_call" | custom-call | flops 234881024 | bytes 7340032 | tf_op jit(solution)/shard_map/pallas_call | solution.py:408
  98.0 6.1 %collective-permute-done.18.received = bf16[32,32,128]{2,1,0:T(8,128)(2,1)S(1)} collective-permute-done((bf16[32,32,128]{2,1,0:T(8,128)(2,1)S(1)}, bf16[32,32,128]{2,1,0:T(8,128)(2,1)S(1)}, u32[]{:S(2)}, u32[]{:S(2)}) %collective-permute-start.18) | collective-permute-done | bytes 262176 | tf_op jit(solution)/shard_map/ppermute | solution.py:330
  104.6 20.1 %collective-permute-start.20 = (bf16[32,32,128]{2,1,0:T(8,128)(2,1)S(1)}, bf16[32,32,128]{2,1,0:T(8,128)(2,1)S(1)}, u32[]{:S(2)}, u32[]{:S(2)}) collective-permute-start(bf16[32,32,128]{2,1,0:T(8,128)(2,1)S(1)} %get-tuple-element.50.token), channel_id=1, source_target_pairs={{0,64},{2,66},{4,68},{6,70},{8,72},{10,74},{12,76},{14,78},{16,80}... | collective-permute-start | bytes 786440 | tf_op jit(solution)/shard_map/ppermute | solution.py:330
  124.7 2.2 %shard_map.88 = (f32[32,32,128]{2,1,0:T(8,128)S(1)}, bf16[32,32,128]{2,1,0:T(8,128)(2,1)S(1)}) custom-call(bf16[32,32,128]{2,1,0:T(8,128)(2,1)S(1)} %collective-permute-done.16.adjoint, bf16[13,64,64,128]{3,2,1,0:T(8,128)(2,1)S(1)} %bitcast.29, bf16[32,32,128]{2,1,0:T(8,128)(2,1)S(1)} %get-tuple-element.50.token), custom_call_target="tpu_custom_call" | custom-call | flops 234881024 | bytes 7340032 | tf_op jit(solution)/shard_map/pallas_call | solution.py:408
  127.2 8.8 %collective-permute-done.20.received = bf16[32,32,128]{2,1,0:T(8,128)(2,1)S(1)} collective-permute-done((bf16[32,32,128]{2,1,0:T(8,128)(2,1)S(1)}, bf16[32,32,128]{2,1,0:T(8,128)(2,1)S(1)}, u32[]{:S(2)}, u32[]{:S(2)}) %collective-permute-start.20) | collective-permute-done | bytes 262176 | tf_op jit(solution)/shard_map/ppermute | solution.py:330
  137.1 7.0 %collective-permute-start.21 = (bf16[32,32,128]{2,1,0:T(8,128)(2,1)S(1)}, bf16[32,32,128]{2,1,0:T(8,128)(2,1)S(1)}, u32[]{:S(2)}, u32[]{:S(2)}) collective-permute-start(bf16[32,32,128]{2,1,0:T(8,128)(2,1)S(1)} %get-tuple-element.56.refs_0_), channel_id=1, source_target_pairs={{0,64},{2,66},{4,68},{6,70},{8,72},{10,74},{12,76},{14,78},{16,80}... | collective-permute-start | bytes 786440 | tf_op jit(solution)/shard_map/ppermute | solution.py:330
  147.8 3.0 %collective-permute-done.21.received = bf16[32,32,128]{2,1,0:T(8,128)(2,1)S(1)} collective-permute-done((bf16[32,32,128]{2,1,0:T(8,128)(2,1)S(1)}, bf16[32,32,128]{2,1,0:T(8,128)(2,1)S(1)}, u32[]{:S(2)}, u32[]{:S(2)}) %collective-permute-start.21) | collective-permute-done | bytes 262176 | tf_op jit(solution)/shard_map/ppermute | solution.py:330
  153.0 5.3 %collective-permute-start.26 = (bf16[32,32,128]{2,1,0:T(8,128)(2,1)S(1)}, bf16[32,32,128]{2,1,0:T(8,128)(2,1)S(1)}, u32[]{:S(2)}, u32[]{:S(2)}) collective-permute-start(bf16[32,32,128]{2,1,0:T(8,128)(2,1)S(1)} %get-tuple-element.64.refs_0_), channel_id=1, source_target_pairs={{0,8},{2,10},{4,12},{6,14},{8,0},{10,2},{12,4},{14,6},{16,24},{18,... | collective-permute-start | bytes 786440 | tf_op jit(solution)/shard_map/ppermute | solution.py:330
  166.1 6.2 %collective-permute-start.27 = (bf16[32,32,128]{2,1,0:T(8,128)(2,1)S(1)}, bf16[32,32,128]{2,1,0:T(8,128)(2,1)S(1)}, u32[]{:S(2)}, u32[]{:S(2)}) collective-permute-start(bf16[32,32,128]{2,1,0:T(8,128)(2,1)S(1)} %get-tuple-element.73.refs_0_), channel_id=1, source_target_pairs={{0,8},{2,10},{4,12},{6,14},{8,0},{10,2},{12,4},{14,6},{16,24},{18,... | collective-permute-start | bytes 786440 | tf_op jit(solution)/shard_map/ppermute | solution.py:330
  172.9 3.8 %collective-permute-start.30 = (bf16[32,32,128]{2,1,0:T(8,128)(2,1)S(1)}, bf16[32,32,128]{2,1,0:T(8,128)(2,1)S(1)}, u32[]{:S(2)}, u32[]{:S(2)}) collective-permute-start(bf16[32,32,128]{2,1,0:T(8,128)(2,1)S(1)} %get-tuple-element.75.refs_0_), channel_id=1, source_target_pairs={{0,2},{2,0},{4,6},{6,4},{8,10},{10,8},{12,14},{14,12},{16,18},{18,... | collective-permute-start | bytes 786440 | tf_op jit(solution)/shard_map/ppermute | solution.py:330
  180.3 2.8 %collective-permute-done.29.received = bf16[32,32,128]{2,1,0:T(8,128)(2,1)S(1)} collective-permute-done((bf16[32,32,128]{2,1,0:T(8,128)(2,1)S(1)}, bf16[32,32,128]{2,1,0:T(8,128)(2,1)S(1)}, u32[]{:S(2)}, u32[]{:S(2)}) %collective-permute-start.29) | collective-permute-done | bytes 262176 | tf_op jit(solution)/shard_map/ppermute | solution.py:330
  183.6 4.3 %collective-permute-start.31 = (bf16[32,32,128]{2,1,0:T(8,128)(2,1)S(1)}, bf16[32,32,128]{2,1,0:T(8,128)(2,1)S(1)}, u32[]{:S(2)}, u32[]{:S(2)}) collective-permute-start(bf16[32,32,128]{2,1,0:T(8,128)(2,1)S(1)} %get-tuple-element.81.token), channel_id=1, source_target_pairs={{0,2},{2,0},{4,6},{6,4},{8,10},{10,8},{12,14},{14,12},{16,18},{18,... | collective-permute-start | bytes 786440 | tf_op jit(solution)/shard_map/ppermute | solution.py:330
  189.1 2.3 %shard_map.103 = (bf16[64,64,128]{2,1,0:T(8,128)(2,1)}, f32[8,128]{1,0:T(8,128)}) custom-call(f32[32,32,128]{2,1,0:T(8,128)S(1)} %get-tuple-element.80.held_part, bf16[32,32,128]{2,1,0:T(8,128)(2,1)S(1)} %collective-permute-done.31.received, bf16[64,64,128]{2,1,0:T(8,128)(2,1)S(1)} %bitcast.43, ...), custom_call_target="tpu_custom_call", output_to_operand_aliasing={{0}: (4, {})} | custom-call | flops 33554432 | bytes 2097152 | tf_op jit(solution)/shard_map/pallas_call | solution.py:379
  (81 shorter events, 47.0 us)
Async XLA Ops:
  5.5 4.1 %collective-permute-start.1 = (bf16[16,64,128]{2,1,0:T(8,128)(2,1)S(1)}, bf16[16,64,128]{2,1,0:T(8,128)(2,1)S(1)}, u32[]{:S(2)}, u32[]{:S(2)}) collective-permute-start(bf16[16,64,128]{2,1,0:T(8,128)(2,1)S(1)} %get-tuple-element.44.own.refs_0_), channel_id=1, source_target_pairs={{0,2},{2,0},{4,6},{6,4},{8,10},{10,8},{12,14},{14,12},{16,18},{18,... | collective-permute-start | bytes 786440 | tf_op jit(solution)/shard_map/ppermute | solution.py:330
  10.0 8.0 %collective-permute-start.2 = (bf16[16,64,128]{2,1,0:T(8,128)(2,1)S(1)}, bf16[16,64,128]{2,1,0:T(8,128)(2,1)S(1)}, u32[]{:S(2)}, u32[]{:S(2)}) collective-permute-start(bf16[16,64,128]{2,1,0:T(8,128)(2,1)S(1)} %shard_map.69.own.refs_0_), channel_id=1, source_target_pairs={{0,4},{2,6},{4,0},{6,2},{8,12},{10,14},{12,8},{14,10},{16,20},{18,... | collective-permute-start | bytes 786440 | tf_op jit(solution)/shard_map/ppermute | solution.py:330
  11.4 10.0 %collective-permute-start = (bf16[16,64,128]{2,1,0:T(8,128)(2,1)S(1)}, bf16[16,64,128]{2,1,0:T(8,128)(2,1)S(1)}, u32[]{:S(2)}, u32[]{:S(2)}) collective-permute-start(bf16[16,64,128]{2,1,0:T(8,128)(2,1)S(1)} %get-tuple-element.43.own), channel_id=1, source_target_pairs={{0,2},{2,0},{4,6},{6,4},{8,10},{10,8},{12,14},{14,12},{16,18},{18,... | collective-permute-start | bytes 786440 | tf_op jit(solution)/shard_map/ppermute | solution.py:330
  18.4 8.6 %collective-permute-start.4 = (bf16[16,64,128]{2,1,0:T(8,128)(2,1)S(1)}, bf16[16,64,128]{2,1,0:T(8,128)(2,1)S(1)}, u32[]{:S(2)}, u32[]{:S(2)}) collective-permute-start(bf16[16,64,128]{2,1,0:T(8,128)(2,1)S(1)} %shard_map.70.refs_0_.own), channel_id=1, source_target_pairs={{0,8},{2,10},{4,12},{6,14},{8,0},{10,2},{12,4},{14,6},{16,24},{18,... | collective-permute-start | bytes 786440 | tf_op jit(solution)/shard_map/ppermute | solution.py:330
  21.8 11.0 %collective-permute-start.3 = (bf16[16,64,128]{2,1,0:T(8,128)(2,1)S(1)}, bf16[16,64,128]{2,1,0:T(8,128)(2,1)S(1)}, u32[]{:S(2)}, u32[]{:S(2)}) collective-permute-start(bf16[16,64,128]{2,1,0:T(8,128)(2,1)S(1)} %shard_map.71.refs_0_.own), channel_id=1, source_target_pairs={{0,4},{2,6},{4,0},{6,2},{8,12},{10,14},{12,8},{14,10},{16,20},{18,... | collective-permute-start | bytes 786440 | tf_op jit(solution)/shard_map/ppermute | solution.py:330
  27.5 7.6 %collective-permute-start.6 = (bf16[16,64,128]{2,1,0:T(8,128)(2,1)S(1)}, bf16[16,64,128]{2,1,0:T(8,128)(2,1)S(1)}, u32[]{:S(2)}, u32[]{:S(2)}) collective-permute-start(bf16[16,64,128]{2,1,0:T(8,128)(2,1)S(1)} %shard_map.72.refs_0_.own), channel_id=1, source_target_pairs={{0,16},{2,18},{4,20},{6,22},{8,24},{10,26},{12,28},{14,30},{16,0},... | collective-permute-start | bytes 786440 | tf_op jit(solution)/shard_map/ppermute | solution.py:330
  33.3 7.7 %collective-permute-start.5 = (bf16[16,64,128]{2,1,0:T(8,128)(2,1)S(1)}, bf16[16,64,128]{2,1,0:T(8,128)(2,1)S(1)}, u32[]{:S(2)}, u32[]{:S(2)}) collective-permute-start(bf16[16,64,128]{2,1,0:T(8,128)(2,1)S(1)} %shard_map.73.refs_0_.own), channel_id=1, source_target_pairs={{0,8},{2,10},{4,12},{6,14},{8,0},{10,2},{12,4},{14,6},{16,24},{18,... | collective-permute-start | bytes 786440 | tf_op jit(solution)/shard_map/ppermute | solution.py:330
  35.5 11.0 %collective-permute-start.8 = (bf16[16,64,128]{2,1,0:T(8,128)(2,1)S(1)}, bf16[16,64,128]{2,1,0:T(8,128)(2,1)S(1)}, u32[]{:S(2)}, u32[]{:S(2)}) collective-permute-start(bf16[16,64,128]{2,1,0:T(8,128)(2,1)S(1)} %shard_map.74.refs_0_.own), channel_id=1, source_target_pairs={{0,32},{2,34},{4,36},{6,38},{8,40},{10,42},{12,44},{14,46},{16,48}... | collective-permute-start | bytes 786440 | tf_op jit(solution)/shard_map/ppermute | solution.py:330
  41.4 8.5 %collective-permute-start.7 = (bf16[16,64,128]{2,1,0:T(8,128)(2,1)S(1)}, bf16[16,64,128]{2,1,0:T(8,128)(2,1)S(1)}, u32[]{:S(2)}, u32[]{:S(2)}) collective-permute-start(bf16[16,64,128]{2,1,0:T(8,128)(2,1)S(1)} %shard_map.75.token.own), channel_id=1, source_target_pairs={{0,16},{2,18},{4,20},{6,22},{8,24},{10,26},{12,28},{14,30},{16,0},... | collective-permute-start | bytes 786440 | tf_op jit(solution)/shard_map/ppermute | solution.py:330
  47.0 6.8 %collective-permute-start.10 = (bf16[16,64,128]{2,1,0:T(8,128)(2,1)S(1)}, bf16[16,64,128]{2,1,0:T(8,128)(2,1)S(1)}, u32[]{:S(2)}, u32[]{:S(2)}) collective-permute-start(bf16[16,64,128]{2,1,0:T(8,128)(2,1)S(1)} %shard_map.77.refs_0_.own), channel_id=1, source_target_pairs={{0,64},{2,66},{4,68},{6,70},{8,72},{10,74},{12,76},{14,78},{16,80}... | collective-permute-start | bytes 786440 | tf_op jit(solution)/shard_map/ppermute | solution.py:330
  50.4 9.0 %collective-permute-start.9 = (bf16[16,64,128]{2,1,0:T(8,128)(2,1)S(1)}, bf16[16,64,128]{2,1,0:T(8,128)(2,1)S(1)}, u32[]{:S(2)}, u32[]{:S(2)}) collective-permute-start(bf16[16,64,128]{2,1,0:T(8,128)(2,1)S(1)} %shard_map.78.refs_0_.own), channel_id=1, source_target_pairs={{0,32},{2,34},{4,36},{6,38},{8,40},{10,42},{12,44},{14,46},{16,48}... | collective-permute-start | bytes 786440 | tf_op jit(solution)/shard_map/ppermute | solution.py:330
  54.2 7.5 %collective-permute-start.12 = (bf16[16,64,128]{2,1,0:T(8,128)(2,1)S(1)}, bf16[16,64,128]{2,1,0:T(8,128)(2,1)S(1)}, u32[]{:S(2)}, u32[]{:S(2)}) collective-permute-start(bf16[16,64,128]{2,1,0:T(8,128)(2,1)S(1)} %shard_map.79.refs_0_.own), channel_id=1, source_target_pairs={{0,1},{1,0},{2,3},{3,2},{4,5},{5,4},{6,7},{7,6},{8,9},{9,8},{10,11... | collective-permute-start | bytes 786440 | tf_op jit(solution)/shard_map/ppermute | solution.py:330
  59.9 7.0 %collective-permute-start.11 = (bf16[16,64,128]{2,1,0:T(8,128)(2,1)S(1)}, bf16[16,64,128]{2,1,0:T(8,128)(2,1)S(1)}, u32[]{:S(2)}, u32[]{:S(2)}) collective-permute-start(bf16[16,64,128]{2,1,0:T(8,128)(2,1)S(1)} %shard_map.80.token.own), channel_id=1, source_target_pairs={{0,64},{2,66},{4,68},{6,70},{8,72},{10,74},{12,76},{14,78},{16,80}... | collective-permute-start | bytes 786440 | tf_op jit(solution)/shard_map/ppermute | solution.py:330
  67.3 8.6 %collective-permute-start.13 = (bf16[16,64,128]{2,1,0:T(8,128)(2,1)S(1)}, bf16[16,64,128]{2,1,0:T(8,128)(2,1)S(1)}, u32[]{:S(2)}, u32[]{:S(2)}) collective-permute-start(bf16[16,64,128]{2,1,0:T(8,128)(2,1)S(1)} %shard_map.82.own.token), channel_id=1, source_target_pairs={{0,1},{1,0},{2,3},{3,2},{4,5},{5,4},{6,7},{7,6},{8,9},{9,8},{10,11... | collective-permute-start | bytes 786440 | tf_op jit(solution)/shard_map/ppermute | solution.py:330
  68.1 15.7 %collective-permute-start.15 = (bf16[16,64,128]{2,1,0:T(8,128)(2,1)S(1)}, bf16[16,64,128]{2,1,0:T(8,128)(2,1)S(1)}, u32[]{:S(2)}, u32[]{:S(2)}) collective-permute-start(bf16[16,64,128]{2,1,0:T(8,128)(2,1)S(1)} %shard_map.81.refs_0_), channel_id=1, source_target_pairs={{0,0},{1,2},{2,1},{3,3},{4,64},{5,66},{6,65},{7,67},{8,32},{9,34},... | collective-permute-start | bytes 786440 | tf_op jit(solution)/shard_map/ppermute | solution.py:340
  78.0 10.0 %collective-permute-start.14 = (bf16[16,64,128]{2,1,0:T(8,128)(2,1)S(1)}, bf16[16,64,128]{2,1,0:T(8,128)(2,1)S(1)}, u32[]{:S(2)}, u32[]{:S(2)}) collective-permute-start(bf16[16,64,128]{2,1,0:T(8,128)(2,1)S(1)} %shard_map.83.token), channel_id=1, source_target_pairs={{0,0},{1,2},{2,1},{3,3},{4,64},{5,66},{6,65},{7,67},{8,32},{9,34},... | collective-permute-start | bytes 786440 | tf_op jit(solution)/shard_map/ppermute | solution.py:340
  86.1 7.7 %collective-permute-start.17 = (bf16[32,32,128]{2,1,0:T(8,128)(2,1)S(1)}, bf16[32,32,128]{2,1,0:T(8,128)(2,1)S(1)}, u32[]{:S(2)}, u32[]{:S(2)}) collective-permute-start(bf16[32,32,128]{2,1,0:T(8,128)(2,1)S(1)} %get-tuple-element.45.token), channel_id=1, source_target_pairs={{0,0},{1,2},{2,1},{3,3},{4,64},{5,66},{6,65},{7,67},{8,32},{9,34},... | collective-permute-start | bytes 786440 | tf_op jit(solution)/shard_map/ppermute | solution.py:340
  96.0 8.1 %collective-permute-start.18 = (bf16[32,32,128]{2,1,0:T(8,128)(2,1)S(1)}, bf16[32,32,128]{2,1,0:T(8,128)(2,1)S(1)}, u32[]{:S(2)}, u32[]{:S(2)}) collective-permute-start(bf16[32,32,128]{2,1,0:T(8,128)(2,1)S(1)} %get-tuple-element.49.refs_0_), channel_id=1, source_target_pairs={{0,1},{1,0},{2,3},{3,2},{4,5},{5,4},{6,7},{7,6},{8,9},{9,8},{10,11... | collective-permute-start | bytes 786440 | tf_op jit(solution)/shard_map/ppermute | solution.py:330
  96.0 28.7 %collective-permute-start.16 = (bf16[32,32,128]{2,1,0:T(8,128)(2,1)S(1)}, bf16[32,32,128]{2,1,0:T(8,128)(2,1)S(1)}, u32[]{:S(2)}, u32[]{:S(2)}) collective-permute-start(bf16[32,32,128]{2,1,0:T(8,128)(2,1)S(1)} %get-tuple-element.47.token), channel_id=1, source_target_pairs={{0,0},{1,2},{2,1},{3,3},{4,64},{5,66},{6,65},{7,67},{8,32},{9,34},... | collective-permute-start | bytes 786440 | tf_op jit(solution)/shard_map/ppermute | solution.py:340
  104.6 31.4 %collective-permute-start.20 = (bf16[32,32,128]{2,1,0:T(8,128)(2,1)S(1)}, bf16[32,32,128]{2,1,0:T(8,128)(2,1)S(1)}, u32[]{:S(2)}, u32[]{:S(2)}) collective-permute-start(bf16[32,32,128]{2,1,0:T(8,128)(2,1)S(1)} %get-tuple-element.50.token), channel_id=1, source_target_pairs={{0,64},{2,66},{4,68},{6,70},{8,72},{10,74},{12,76},{14,78},{16,80}... | collective-permute-start | bytes 786440 | tf_op jit(solution)/shard_map/ppermute | solution.py:330
  126.9 9.7 %collective-permute-start.19 = (bf16[32,32,128]{2,1,0:T(8,128)(2,1)S(1)}, bf16[32,32,128]{2,1,0:T(8,128)(2,1)S(1)}, u32[]{:S(2)}, u32[]{:S(2)}) collective-permute-start(bf16[32,32,128]{2,1,0:T(8,128)(2,1)S(1)} %get-tuple-element.52.refs_0_), channel_id=1, source_target_pairs={{0,1},{1,0},{2,3},{3,2},{4,5},{5,4},{6,7},{7,6},{8,9},{9,8},{10,11... | collective-permute-start | bytes 786440 | tf_op jit(solution)/shard_map/ppermute | solution.py:330
  136.5 7.6 %collective-permute-start.22 = (bf16[32,32,128]{2,1,0:T(8,128)(2,1)S(1)}, bf16[32,32,128]{2,1,0:T(8,128)(2,1)S(1)}, u32[]{:S(2)}, u32[]{:S(2)}) collective-permute-start(bf16[32,32,128]{2,1,0:T(8,128)(2,1)S(1)} %get-tuple-element.54.refs_0_), channel_id=1, source_target_pairs={{0,32},{2,34},{4,36},{6,38},{8,40},{10,42},{12,44},{14,46},{16,48}... | collective-permute-start | bytes 786440 | tf_op jit(solution)/shard_map/ppermute | solution.py:330
  137.1 13.7 %collective-permute-start.21 = (bf16[32,32,128]{2,1,0:T(8,128)(2,1)S(1)}, bf16[32,32,128]{2,1,0:T(8,128)(2,1)S(1)}, u32[]{:S(2)}, u32[]{:S(2)}) collective-permute-start(bf16[32,32,128]{2,1,0:T(8,128)(2,1)S(1)} %get-tuple-element.56.refs_0_), channel_id=1, source_target_pairs={{0,64},{2,66},{4,68},{6,70},{8,72},{10,74},{12,76},{14,78},{16,80}... | collective-permute-start | bytes 786440 | tf_op jit(solution)/shard_map/ppermute | solution.py:330
  144.5 7.9 %collective-permute-start.24 = (bf16[32,32,128]{2,1,0:T(8,128)(2,1)S(1)}, bf16[32,32,128]{2,1,0:T(8,128)(2,1)S(1)}, u32[]{:S(2)}, u32[]{:S(2)}) collective-permute-start(bf16[32,32,128]{2,1,0:T(8,128)(2,1)S(1)} %get-tuple-element.59.token), channel_id=1, source_target_pairs={{0,16},{2,18},{4,20},{6,22},{8,24},{10,26},{12,28},{14,30},{16,0},... | collective-permute-start | bytes 786440 | tf_op jit(solution)/shard_map/ppermute | solution.py:330
  151.3 7.0 %collective-permute-start.23 = (bf16[32,32,128]{2,1,0:T(8,128)(2,1)S(1)}, bf16[32,32,128]{2,1,0:T(8,128)(2,1)S(1)}, u32[]{:S(2)}, u32[]{:S(2)}) collective-permute-start(bf16[32,32,128]{2,1,0:T(8,128)(2,1)S(1)} %get-tuple-element.62.refs_0_), channel_id=1, source_target_pairs={{0,32},{2,34},{4,36},{6,38},{8,40},{10,42},{12,44},{14,46},{16,48}... | collective-permute-start | bytes 786440 | tf_op jit(solution)/shard_map/ppermute | solution.py:330
  153.0 10.6 %collective-permute-start.26 = (bf16[32,32,128]{2,1,0:T(8,128)(2,1)S(1)}, bf16[32,32,128]{2,1,0:T(8,128)(2,1)S(1)}, u32[]{:S(2)}, u32[]{:S(2)}) collective-permute-start(bf16[32,32,128]{2,1,0:T(8,128)(2,1)S(1)} %get-tuple-element.64.refs_0_), channel_id=1, source_target_pairs={{0,8},{2,10},{4,12},{6,14},{8,0},{10,2},{12,4},{14,6},{16,24},{18,... | collective-permute-start | bytes 786440 | tf_op jit(solution)/shard_map/ppermute | solution.py:330
  158.8 6.8 %collective-permute-start.25 = (bf16[32,32,128]{2,1,0:T(8,128)(2,1)S(1)}, bf16[32,32,128]{2,1,0:T(8,128)(2,1)S(1)}, u32[]{:S(2)}, u32[]{:S(2)}) collective-permute-start(bf16[32,32,128]{2,1,0:T(8,128)(2,1)S(1)} %get-tuple-element.65.token), channel_id=1, source_target_pairs={{0,16},{2,18},{4,20},{6,22},{8,24},{10,26},{12,28},{14,30},{16,0},... | collective-permute-start | bytes 786440 | tf_op jit(solution)/shard_map/ppermute | solution.py:330
  164.1 8.3 %collective-permute-start.28 = (bf16[32,32,128]{2,1,0:T(8,128)(2,1)S(1)}, bf16[32,32,128]{2,1,0:T(8,128)(2,1)S(1)}, u32[]{:S(2)}, u32[]{:S(2)}) collective-permute-start(bf16[32,32,128]{2,1,0:T(8,128)(2,1)S(1)} %get-tuple-element.71.refs_0_), channel_id=1, source_target_pairs={{0,4},{2,6},{4,0},{6,2},{8,12},{10,14},{12,8},{14,10},{16,20},{18,... | collective-permute-start | bytes 786440 | tf_op jit(solution)/shard_map/ppermute | solution.py:330
  166.1 11.2 %collective-permute-start.27 = (bf16[32,32,128]{2,1,0:T(8,128)(2,1)S(1)}, bf16[32,32,128]{2,1,0:T(8,128)(2,1)S(1)}, u32[]{:S(2)}, u32[]{:S(2)}) collective-permute-start(bf16[32,32,128]{2,1,0:T(8,128)(2,1)S(1)} %get-tuple-element.73.refs_0_), channel_id=1, source_target_pairs={{0,8},{2,10},{4,12},{6,14},{8,0},{10,2},{12,4},{14,6},{16,24},{18,... | collective-permute-start | bytes 786440 | tf_op jit(solution)/shard_map/ppermute | solution.py:330
  172.9 5.7 %collective-permute-start.30 = (bf16[32,32,128]{2,1,0:T(8,128)(2,1)S(1)}, bf16[32,32,128]{2,1,0:T(8,128)(2,1)S(1)}, u32[]{:S(2)}, u32[]{:S(2)}) collective-permute-start(bf16[32,32,128]{2,1,0:T(8,128)(2,1)S(1)} %get-tuple-element.75.refs_0_), channel_id=1, source_target_pairs={{0,2},{2,0},{4,6},{6,4},{8,10},{10,8},{12,14},{14,12},{16,18},{18,... | collective-permute-start | bytes 786440 | tf_op jit(solution)/shard_map/ppermute | solution.py:330
  177.8 5.3 %collective-permute-start.29 = (bf16[32,32,128]{2,1,0:T(8,128)(2,1)S(1)}, bf16[32,32,128]{2,1,0:T(8,128)(2,1)S(1)}, u32[]{:S(2)}, u32[]{:S(2)}) collective-permute-start(bf16[32,32,128]{2,1,0:T(8,128)(2,1)S(1)} %get-tuple-element.77.token), channel_id=1, source_target_pairs={{0,4},{2,6},{4,0},{6,2},{8,12},{10,14},{12,8},{14,10},{16,20},{18,... | collective-permute-start | bytes 786440 | tf_op jit(solution)/shard_map/ppermute | solution.py:330
  183.6 5.5 %collective-permute-start.31 = (bf16[32,32,128]{2,1,0:T(8,128)(2,1)S(1)}, bf16[32,32,128]{2,1,0:T(8,128)(2,1)S(1)}, u32[]{:S(2)}, u32[]{:S(2)}) collective-permute-start(bf16[32,32,128]{2,1,0:T(8,128)(2,1)S(1)} %get-tuple-element.81.token), channel_id=1, source_target_pairs={{0,2},{2,0},{4,6},{6,4},{8,10},{10,8},{12,14},{14,12},{16,18},{18,... | collective-permute-start | bytes 786440 | tf_op jit(solution)/shard_map/ppermute | solution.py:330
  (6 other events, 99.1 us)

commit v5 on v4

--- a/solution.py
+++ b/solution.py
@@ -420,7 +420,7 @@
     first_back = top + 1 + 2 * GAP
     stages = first_back + top
     for step in range(stages + 1 + LAG * (CHUNKS - 1)):
-        for c in every:
+        for c in every if step < first_back else reversed(every):
             stage = step - LAG * c
             if 0 <= stage < top:
                 level = stage

time: 192 us -> 192 us (level)
  waiting for transfers between devices: 55.4 us -> 59.7 us
  starting transfers between devices: 94.2 us -> 90.2 us
    ppermute x28, waiting for transfers between devices: 51.9 us -> 57.9 us  [exchange(): return lax.ppermute(array, axis, [(i, i ^ 1 << bit) for i in range(count)])]
    ppermute x28, starting transfers between devices: 76.8 us -> 71.2 us  [exchange(): return lax.ppermute(array, axis, [(i, i ^ 1 << bit) for i in range(count)])]
  transfers between devices with their start and end apart: 32 -> 32, of which waited for: 16 -> 15; matrix products, arithmetic and copies ran while one was open for 1% -> 1% of each run, Pallas kernels for 14% -> 16%
where the time goes in v5:
time: 192 us
  starting transfers between devices  90.2 us (47%)
  waiting for transfers between devices  59.7 us (31%)
  Pallas kernels  35.4 us (18%)
  local copies, waits for them, and re-layouts  5.39 us (3%)
    ppermute x28, starting transfers between devices, exchange(): return lax.ppermute(array, axis, [(i, i ^ 1 << bit) for i in range(count)])  71.2 us
    ppermute x28, waiting for transfers between devices, exchange(): return lax.ppermute(array, axis, [(i, i ^ 1 << bit) for i in range(count)])  57.9 us
    ppermute x4, starting transfers between devices, reversal(): return lax.ppermute(array, ('src', 'hi'), pairs_of)  19.1 us
    pallas_call x12, Pallas kernels, adjoint_call(): call(kernel, (kept_shape, pair_shape), specs, (VMEM, VMEM), [], flops, mo...  5.96 us
    pallas_call x12, Pallas kernels, cross_call(): call(kernel, forward_shape, specs, VMEM, [], flops, moved, 4)(*operands)  5.28 us
    pallas_call x2, Pallas kernels, target_call(): call(kernel, (shape(boxes, vectors, points), pair_shape), [VMEM] * 3 + [A...  4.55 us
    pallas_call x2, Pallas kernels, local_adjoint_call(): call(kernel, (kept_shape, pair_shape), [VMEM] * 2 + [ANY], (VMEM, VMEM),...  4.3 us
    pallas_call x2, Pallas kernels, local_forward_call(): call(kernel, forward_shape, [VMEM] * 3 + [ANY], VMEM, scratch, 7 * flops,...  4.28 us
  transfers between devices with their start and end apart: 32, of which 15 were waited for; matrix products, arithmetic and copies ran while one was open for 1% of the time, Pallas kernels for 16%

profile of v5, /device:TPU:1, one launch (start us, length us, event | category | flops | bytes accessed | tf_op | source)
XLA Modules:
  0.0 192.0 jit_solution(2029701410415339997)
XLA Ops:
  7.0 2.5 %slice_bitcast_fusion = (bf16[1,64,64,128]{3,2,1,0:T(8,128)(2,1)S(1)}, bf16[1,64,64,128]{3,2,1,0:T(8,128)(2,1)S(1)}, bf16[1,64,64,128]{3,2,1,0:T(8,128)(2,1)S(1)}) fusion(bf16[13,64,1,1,64,128]{5,4,1,3,2,0:T(8,128)(2,1)} %bitcast.18), kind=kLoop, calls=%fused_computation | loop fusion | bytes 6291456 | tf_op jit(solution)/shard_map/slice | solution.py:427
  11.7 6.3 %collective-permute-done.2.other = bf16[16,64,128]{2,1,0:T(8,128)(2,1)S(1)} collective-permute-done((bf16[16,64,128]{2,1,0:T(8,128)(2,1)S(1)}, bf16[16,64,128]{2,1,0:T(8,128)(2,1)S(1)}, u32[]{:S(2)}, u32[]{:S(2)}) %collective-permute-start.2) | collective-permute-done | bytes 262176 | tf_op jit(solution)/shard_map/ppermute | solution.py:330
  18.4 2.9 %collective-permute-start.4 = (bf16[16,64,128]{2,1,0:T(8,128)(2,1)S(1)}, bf16[16,64,128]{2,1,0:T(8,128)(2,1)S(1)}, u32[]{:S(2)}, u32[]{:S(2)}) collective-permute-start(bf16[16,64,128]{2,1,0:T(8,128)(2,1)S(1)} %shard_map.70.refs_0_.own), channel_id=1, source_target_pairs={{0,8},{2,10},{4,12},{6,14},{8,0},{10,2},{12,4},{14,6},{16,24},{18,... | collective-permute-start | bytes 786440 | tf_op jit(solution)/shard_map/ppermute | solution.py:330
  22.2 4.9 %collective-permute-done.4.other = bf16[16,64,128]{2,1,0:T(8,128)(2,1)S(1)} collective-permute-done((bf16[16,64,128]{2,1,0:T(8,128)(2,1)S(1)}, bf16[16,64,128]{2,1,0:T(8,128)(2,1)S(1)}, u32[]{:S(2)}, u32[]{:S(2)}) %collective-permute-start.4) | collective-permute-done | bytes 262176 | tf_op jit(solution)/shard_map/ppermute | solution.py:330
  27.5 3.8 %collective-permute-start.6 = (bf16[16,64,128]{2,1,0:T(8,128)(2,1)S(1)}, bf16[16,64,128]{2,1,0:T(8,128)(2,1)S(1)}, u32[]{:S(2)}, u32[]{:S(2)}) collective-permute-start(bf16[16,64,128]{2,1,0:T(8,128)(2,1)S(1)} %shard_map.72.refs_0_.own), channel_id=1, source_target_pairs={{0,16},{2,18},{4,20},{6,22},{8,24},{10,26},{12,28},{14,30},{16,0},... | collective-permute-start | bytes 786440 | tf_op jit(solution)/shard_map/ppermute | solution.py:330
  36.9 4.0 %collective-permute-done.5.other = bf16[16,64,128]{2,1,0:T(8,128)(2,1)S(1)} collective-permute-done((bf16[16,64,128]{2,1,0:T(8,128)(2,1)S(1)}, bf16[16,64,128]{2,1,0:T(8,128)(2,1)S(1)}, u32[]{:S(2)}, u32[]{:S(2)}) %collective-permute-start.5) | collective-permute-done | bytes 262176 | tf_op jit(solution)/shard_map/ppermute | solution.py:330
  41.4 3.7 %collective-permute-start.7 = (bf16[16,64,128]{2,1,0:T(8,128)(2,1)S(1)}, bf16[16,64,128]{2,1,0:T(8,128)(2,1)S(1)}, u32[]{:S(2)}, u32[]{:S(2)}) collective-permute-start(bf16[16,64,128]{2,1,0:T(8,128)(2,1)S(1)} %shard_map.75.token.own), channel_id=1, source_target_pairs={{0,16},{2,18},{4,20},{6,22},{8,24},{10,26},{12,28},{14,30},{16,0},... | collective-permute-start | bytes 786440 | tf_op jit(solution)/shard_map/ppermute | solution.py:330
  47.0 3.0 %collective-permute-start.10 = (bf16[16,64,128]{2,1,0:T(8,128)(2,1)S(1)}, bf16[16,64,128]{2,1,0:T(8,128)(2,1)S(1)}, u32[]{:S(2)}, u32[]{:S(2)}) collective-permute-start(bf16[16,64,128]{2,1,0:T(8,128)(2,1)S(1)} %shard_map.77.refs_0_.own), channel_id=1, source_target_pairs={{0,64},{2,66},{4,68},{6,70},{8,72},{10,74},{12,76},{14,78},{16,80}... | collective-permute-start | bytes 786440 | tf_op jit(solution)/shard_map/ppermute | solution.py:330
  50.9 2.9 %collective-permute-done.10.other = bf16[16,64,128]{2,1,0:T(8,128)(2,1)S(1)} collective-permute-done((bf16[16,64,128]{2,1,0:T(8,128)(2,1)S(1)}, bf16[16,64,128]{2,1,0:T(8,128)(2,1)S(1)}, u32[]{:S(2)}, u32[]{:S(2)}) %collective-permute-start.10) | collective-permute-done | bytes 262176 | tf_op jit(solution)/shard_map/ppermute | solution.py:330
  55.0 4.4 %collective-permute-done.9.other = bf16[16,64,128]{2,1,0:T(8,128)(2,1)S(1)} collective-permute-done((bf16[16,64,128]{2,1,0:T(8,128)(2,1)S(1)}, bf16[16,64,128]{2,1,0:T(8,128)(2,1)S(1)}, u32[]{:S(2)}, u32[]{:S(2)}) %collective-permute-start.9) | collective-permute-done | bytes 262176 | tf_op jit(solution)/shard_map/ppermute | solution.py:330
  61.7 2.1 %shard_map.81.refs_0_ = bf16[16,64,128]{2,1,0:T(8,128)(2,1)S(1)} custom-call(bf16[16,64,128]{2,1,0:T(8,128)(2,1)S(1)} %shard_map.79.refs_0_.own, bf16[16,64,128]{2,1,0:T(8,128)(2,1)S(1)} %collective-permute-done.12.other, bf16[13,64,64,128]{3,2,1,0:T(8,128)(2,1)S(1)} %bitcast.24, bf16[16,64,128]{2,1,0:T(8,128)(2,1)S(1)} %shard_map.80.token.own), custom_call_target="tpu_custom_call" | custom-call | flops 234881024 | bytes 7340032 | tf_op jit(solution)/shard_map/pallas_call | solution.py:401
  63.8 3.0 %collective-permute-done.11.other = bf16[16,64,128]{2,1,0:T(8,128)(2,1)S(1)} collective-permute-done((bf16[16,64,128]{2,1,0:T(8,128)(2,1)S(1)}, bf16[16,64,128]{2,1,0:T(8,128)(2,1)S(1)}, u32[]{:S(2)}, u32[]{:S(2)}) %collective-permute-start.11) | collective-permute-done | bytes 262176 | tf_op jit(solution)/shard_map/ppermute | solution.py:330
  68.1 7.8 %collective-permute-start.15 = (bf16[16,64,128]{2,1,0:T(8,128)(2,1)S(1)}, bf16[16,64,128]{2,1,0:T(8,128)(2,1)S(1)}, u32[]{:S(2)}, u32[]{:S(2)}) collective-permute-start(bf16[16,64,128]{2,1,0:T(8,128)(2,1)S(1)} %shard_map.81.refs_0_), channel_id=1, source_target_pairs={{0,0},{1,2},{2,1},{3,3},{4,64},{5,66},{6,65},{7,67},{8,32},{9,34},... | collective-permute-start | bytes 786440 | tf_op jit(solution)/shard_map/ppermute | solution.py:340
  75.9 2.1 %shard_map.83.token = bf16[16,64,128]{2,1,0:T(8,128)(2,1)S(1)} custom-call(bf16[16,64,128]{2,1,0:T(8,128)(2,1)S(1)} %shard_map.82.own.token, bf16[16,64,128]{2,1,0:T(8,128)(2,1)S(1)} %collective-permute-done.13.other, bf16[13,64,64,128]{3,2,1,0:T(8,128)(2,1)S(1)} %bitcast.26, bf16[16,64,128]{2,1,0:T(8,128)(2,1)S(1)} %shard_map.82.own.token), custom_call_target="tpu_custom_call" | custom-call | flops 234881024 | bytes 7340032 | tf_op jit(solution)/shard_map/pallas_call | solution.py:401
  78.0 5.8 %collective-permute-start.14 = (bf16[16,64,128]{2,1,0:T(8,128)(2,1)S(1)}, bf16[16,64,128]{2,1,0:T(8,128)(2,1)S(1)}, u32[]{:S(2)}, u32[]{:S(2)}) collective-permute-start(bf16[16,64,128]{2,1,0:T(8,128)(2,1)S(1)} %shard_map.83.token), channel_id=1, source_target_pairs={{0,0},{1,2},{2,1},{3,3},{4,64},{5,66},{6,65},{7,67},{8,32},{9,34},... | collective-permute-start | bytes 786440 | tf_op jit(solution)/shard_map/ppermute | solution.py:340
  83.8 2.3 %shard_map.84 = (bf16[64,32,128]{2,1,0:T(8,128)(2,1)S(1)}, bf16[32,32,128]{2,1,0:T(8,128)(2,1)S(1)}) custom-call(bf16[16,64,128]{2,1,0:T(8,128)(2,1)S(1)} %collective-permute-done.15.coeffs, bf16[64,64,128]{2,1,0:T(8,128)(2,1)S(1)} %bitcast.44, bf16[64,64,128]{2,1,0:T(8,128)(2,1)S(1)} %shard_map.76.refs_0_.wanted, bf16[16,64,128]{2,1,0:T(8,128)(2,1)S(1)} %shard_map.83.token), custom_call_target="tpu_custom_call" | custom-call | flops 67108864 | bytes 4194304 | tf_op jit(solution)/shard_map/pallas_call | solution.py:364
  88.0 2.3 %shard_map.85 = (bf16[64,32,128]{2,1,0:T(8,128)(2,1)S(1)}, bf16[32,32,128]{2,1,0:T(8,128)(2,1)S(1)}) custom-call(bf16[16,64,128]{2,1,0:T(8,128)(2,1)S(1)} %collective-permute-done.14.coeffs, bf16[64,64,128]{2,1,0:T(8,128)(2,1)S(1)} %bitcast.45, bf16[64,64,128]{2,1,0:T(8,128)(2,1)S(1)} %shard_map.76.refs_0_.wanted, ...), custom_call_target="tpu_custom_call" | custom-call | flops 67108864 | bytes 4194304 | tf_op jit(solution)/shard_map/pallas_call | solution.py:364
  90.3 3.6 %collective-permute-start.16 = (bf16[32,32,128]{2,1,0:T(8,128)(2,1)S(1)}, bf16[32,32,128]{2,1,0:T(8,128)(2,1)S(1)}, u32[]{:S(2)}, u32[]{:S(2)}) collective-permute-start(bf16[32,32,128]{2,1,0:T(8,128)(2,1)S(1)} %get-tuple-element.47.token), channel_id=1, source_target_pairs={{0,0},{1,2},{2,1},{3,3},{4,64},{5,66},{6,65},{7,67},{8,32},{9,34},... | collective-permute-start | bytes 786440 | tf_op jit(solution)/shard_map/ppermute | solution.py:340
  94.0 2.2 %shard_map.86 = (f32[32,32,128]{2,1,0:T(8,128)S(1)}, bf16[32,32,128]{2,1,0:T(8,128)(2,1)S(1)}) custom-call(bf16[32,32,128]{2,1,0:T(8,128)(2,1)S(1)} %collective-permute-done.17.adjoint, bf16[13,64,64,128]{3,2,1,0:T(8,128)(2,1)S(1)} %bitcast.27, bf16[32,32,128]{2,1,0:T(8,128)(2,1)S(1)} %get-tuple-element.47.token), custom_call_target="tpu_custom_call" | custom-call | flops 234881024 | bytes 7340032 | tf_op jit(solution)/shard_map/pallas_call | solution.py:408
  98.0 2.1 %shard_map.87 = (f32[32,32,128]{2,1,0:T(8,128)S(1)}, bf16[32,32,128]{2,1,0:T(8,128)(2,1)S(1)}) custom-call(bf16[32,32,128]{2,1,0:T(8,128)(2,1)S(1)} %collective-permute-done.16.adjoint, bf16[13,64,64,128]{3,2,1,0:T(8,128)(2,1)S(1)} %bitcast.28, bf16[32,32,128]{2,1,0:T(8,128)(2,1)S(1)} %get-tuple-element.48.token), custom_call_target="tpu_custom_call" | custom-call | flops 234881024 | bytes 7340032 | tf_op jit(solution)/shard_map/pallas_call | solution.py:408
  100.3 4.0 %collective-permute-done.19.received = bf16[32,32,128]{2,1,0:T(8,128)(2,1)S(1)} collective-permute-done((bf16[32,32,128]{2,1,0:T(8,128)(2,1)S(1)}, bf16[32,32,128]{2,1,0:T(8,128)(2,1)S(1)}, u32[]{:S(2)}, u32[]{:S(2)}) %collective-permute-start.19) | collective-permute-done | bytes 262176 | tf_op jit(solution)/shard_map/ppermute | solution.py:330
  104.8 23.0 %collective-permute-start.21 = (bf16[32,32,128]{2,1,0:T(8,128)(2,1)S(1)}, bf16[32,32,128]{2,1,0:T(8,128)(2,1)S(1)}, u32[]{:S(2)}, u32[]{:S(2)}) collective-permute-start(bf16[32,32,128]{2,1,0:T(8,128)(2,1)S(1)} %get-tuple-element.52.refs_0_), channel_id=1, source_target_pairs={{0,64},{2,66},{4,68},{6,70},{8,72},{10,74},{12,76},{14,78},{16,80}... | collective-permute-start | bytes 786440 | tf_op jit(solution)/shard_map/ppermute | solution.py:330
  128.2 5.5 %collective-permute-start.20 = (bf16[32,32,128]{2,1,0:T(8,128)(2,1)S(1)}, bf16[32,32,128]{2,1,0:T(8,128)(2,1)S(1)}, u32[]{:S(2)}, u32[]{:S(2)}) collective-permute-start(bf16[32,32,128]{2,1,0:T(8,128)(2,1)S(1)} %get-tuple-element.54.refs_0_), channel_id=1, source_target_pairs={{0,64},{2,66},{4,68},{6,70},{8,72},{10,74},{12,76},{14,78},{16,80}... | collective-permute-start | bytes 786440 | tf_op jit(solution)/shard_map/ppermute | solution.py:330
  135.2 4.7 %collective-permute-done.20.received = bf16[32,32,128]{2,1,0:T(8,128)(2,1)S(1)} collective-permute-done((bf16[32,32,128]{2,1,0:T(8,128)(2,1)S(1)}, bf16[32,32,128]{2,1,0:T(8,128)(2,1)S(1)}, u32[]{:S(2)}, u32[]{:S(2)}) %collective-permute-start.20) | collective-permute-done | bytes 262176 | tf_op jit(solution)/shard_map/ppermute | solution.py:330
  142.1 4.5 %collective-permute-done.23.received = bf16[32,32,128]{2,1,0:T(8,128)(2,1)S(1)} collective-permute-done((bf16[32,32,128]{2,1,0:T(8,128)(2,1)S(1)}, bf16[32,32,128]{2,1,0:T(8,128)(2,1)S(1)}, u32[]{:S(2)}, u32[]{:S(2)}) %collective-permute-start.23) | collective-permute-done | bytes 262176 | tf_op jit(solution)/shard_map/ppermute | solution.py:330
  149.9 2.6 %collective-permute-done.22.received = bf16[32,32,128]{2,1,0:T(8,128)(2,1)S(1)} collective-permute-done((bf16[32,32,128]{2,1,0:T(8,128)(2,1)S(1)}, bf16[32,32,128]{2,1,0:T(8,128)(2,1)S(1)}, u32[]{:S(2)}, u32[]{:S(2)}) %collective-permute-start.22) | collective-permute-done | bytes 262176 | tf_op jit(solution)/shard_map/ppermute | solution.py:330
  156.4 5.3 %collective-permute-done.24.received = bf16[32,32,128]{2,1,0:T(8,128)(2,1)S(1)} collective-permute-done((bf16[32,32,128]{2,1,0:T(8,128)(2,1)S(1)}, bf16[32,32,128]{2,1,0:T(8,128)(2,1)S(1)}, u32[]{:S(2)}, u32[]{:S(2)}) %collective-permute-start.24) | collective-permute-done | bytes 262176 | tf_op jit(solution)/shard_map/ppermute | solution.py:330
  164.0 6.1 %collective-permute-done.26.received = bf16[32,32,128]{2,1,0:T(8,128)(2,1)S(1)} collective-permute-done((bf16[32,32,128]{2,1,0:T(8,128)(2,1)S(1)}, bf16[32,32,128]{2,1,0:T(8,128)(2,1)S(1)}, u32[]{:S(2)}, u32[]{:S(2)}) %collective-permute-start.26) | collective-permute-done | bytes 262176 | tf_op jit(solution)/shard_map/ppermute | solution.py:330
  170.7 3.6 %collective-permute-done.29.received = bf16[32,32,128]{2,1,0:T(8,128)(2,1)S(1)} collective-permute-done((bf16[32,32,128]{2,1,0:T(8,128)(2,1)S(1)}, bf16[32,32,128]{2,1,0:T(8,128)(2,1)S(1)}, u32[]{:S(2)}, u32[]{:S(2)}) %collective-permute-start.29) | collective-permute-done | bytes 262176 | tf_op jit(solution)/shard_map/ppermute | solution.py:330
  174.8 7.3 %collective-permute-start.31 = (bf16[32,32,128]{2,1,0:T(8,128)(2,1)S(1)}, bf16[32,32,128]{2,1,0:T(8,128)(2,1)S(1)}, u32[]{:S(2)}, u32[]{:S(2)}) collective-permute-start(bf16[32,32,128]{2,1,0:T(8,128)(2,1)S(1)} %get-tuple-element.77.refs_0_), channel_id=1, source_target_pairs={{0,2},{2,0},{4,6},{6,4},{8,10},{10,8},{12,14},{14,12},{16,18},{18,... | collective-permute-start | bytes 786440 | tf_op jit(solution)/shard_map/ppermute | solution.py:330
  182.7 5.1 %collective-permute-start.30 = (bf16[32,32,128]{2,1,0:T(8,128)(2,1)S(1)}, bf16[32,32,128]{2,1,0:T(8,128)(2,1)S(1)}, u32[]{:S(2)}, u32[]{:S(2)}) collective-permute-start(bf16[32,32,128]{2,1,0:T(8,128)(2,1)S(1)} %get-tuple-element.79.token), channel_id=1, source_target_pairs={{0,2},{2,0},{4,6},{6,4},{8,10},{10,8},{12,14},{14,12},{16,18},{18,... | collective-permute-start | bytes 786440 | tf_op jit(solution)/shard_map/ppermute | solution.py:330
  189.5 2.3 %shard_map.103 = (bf16[64,64,128]{2,1,0:T(8,128)(2,1)}, f32[8,128]{1,0:T(8,128)}) custom-call(f32[32,32,128]{2,1,0:T(8,128)S(1)} %get-tuple-element.78.held_part, bf16[32,32,128]{2,1,0:T(8,128)(2,1)S(1)} %collective-permute-done.30.received, bf16[64,64,128]{2,1,0:T(8,128)(2,1)S(1)} %bitcast.43, ...), custom_call_target="tpu_custom_call", output_to_operand_aliasing={{0}: (4, {})} | custom-call | flops 33554432 | bytes 2097152 | tf_op jit(solution)/shard_map/pallas_call | solution.py:379
  (81 shorter events, 45.0 us)
Async XLA Ops:
  5.5 4.1 %collective-permute-start.1 = (bf16[16,64,128]{2,1,0:T(8,128)(2,1)S(1)}, bf16[16,64,128]{2,1,0:T(8,128)(2,1)S(1)}, u32[]{:S(2)}, u32[]{:S(2)}) collective-permute-start(bf16[16,64,128]{2,1,0:T(8,128)(2,1)S(1)} %get-tuple-element.44.own.refs_0_), channel_id=1, source_target_pairs={{0,2},{2,0},{4,6},{6,4},{8,10},{10,8},{12,14},{14,12},{16,18},{18,... | collective-permute-start | bytes 786440 | tf_op jit(solution)/shard_map/ppermute | solution.py:330
  10.0 8.0 %collective-permute-start.2 = (bf16[16,64,128]{2,1,0:T(8,128)(2,1)S(1)}, bf16[16,64,128]{2,1,0:T(8,128)(2,1)S(1)}, u32[]{:S(2)}, u32[]{:S(2)}) collective-permute-start(bf16[16,64,128]{2,1,0:T(8,128)(2,1)S(1)} %shard_map.69.own.refs_0_), channel_id=1, source_target_pairs={{0,4},{2,6},{4,0},{6,2},{8,12},{10,14},{12,8},{14,10},{16,20},{18,... | collective-permute-start | bytes 786440 | tf_op jit(solution)/shard_map/ppermute | solution.py:330
  11.4 10.0 %collective-permute-start = (bf16[16,64,128]{2,1,0:T(8,128)(2,1)S(1)}, bf16[16,64,128]{2,1,0:T(8,128)(2,1)S(1)}, u32[]{:S(2)}, u32[]{:S(2)}) collective-permute-start(bf16[16,64,128]{2,1,0:T(8,128)(2,1)S(1)} %get-tuple-element.43.own), channel_id=1, source_target_pairs={{0,2},{2,0},{4,6},{6,4},{8,10},{10,8},{12,14},{14,12},{16,18},{18,... | collective-permute-start | bytes 786440 | tf_op jit(solution)/shard_map/ppermute | solution.py:330
  18.4 8.6 %collective-permute-start.4 = (bf16[16,64,128]{2,1,0:T(8,128)(2,1)S(1)}, bf16[16,64,128]{2,1,0:T(8,128)(2,1)S(1)}, u32[]{:S(2)}, u32[]{:S(2)}) collective-permute-start(bf16[16,64,128]{2,1,0:T(8,128)(2,1)S(1)} %shard_map.70.refs_0_.own), channel_id=1, source_target_pairs={{0,8},{2,10},{4,12},{6,14},{8,0},{10,2},{12,4},{14,6},{16,24},{18,... | collective-permute-start | bytes 786440 | tf_op jit(solution)/shard_map/ppermute | solution.py:330
  21.8 11.0 %collective-permute-start.3 = (bf16[16,64,128]{2,1,0:T(8,128)(2,1)S(1)}, bf16[16,64,128]{2,1,0:T(8,128)(2,1)S(1)}, u32[]{:S(2)}, u32[]{:S(2)}) collective-permute-start(bf16[16,64,128]{2,1,0:T(8,128)(2,1)S(1)} %shard_map.71.refs_0_.own), channel_id=1, source_target_pairs={{0,4},{2,6},{4,0},{6,2},{8,12},{10,14},{12,8},{14,10},{16,20},{18,... | collective-permute-start | bytes 786440 | tf_op jit(solution)/shard_map/ppermute | solution.py:330
  27.5 7.6 %collective-permute-start.6 = (bf16[16,64,128]{2,1,0:T(8,128)(2,1)S(1)}, bf16[16,64,128]{2,1,0:T(8,128)(2,1)S(1)}, u32[]{:S(2)}, u32[]{:S(2)}) collective-permute-start(bf16[16,64,128]{2,1,0:T(8,128)(2,1)S(1)} %shard_map.72.refs_0_.own), channel_id=1, source_target_pairs={{0,16},{2,18},{4,20},{6,22},{8,24},{10,26},{12,28},{14,30},{16,0},... | collective-permute-start | bytes 786440 | tf_op jit(solution)/shard_map/ppermute | solution.py:330
  33.3 7.7 %collective-permute-start.5 = (bf16[16,64,128]{2,1,0:T(8,128)(2,1)S(1)}, bf16[16,64,128]{2,1,0:T(8,128)(2,1)S(1)}, u32[]{:S(2)}, u32[]{:S(2)}) collective-permute-start(bf16[16,64,128]{2,1,0:T(8,128)(2,1)S(1)} %shard_map.73.refs_0_.own), channel_id=1, source_target_pairs={{0,8},{2,10},{4,12},{6,14},{8,0},{10,2},{12,4},{14,6},{16,24},{18,... | collective-permute-start | bytes 786440 | tf_op jit(solution)/shard_map/ppermute | solution.py:330
  35.5 11.0 %collective-permute-start.8 = (bf16[16,64,128]{2,1,0:T(8,128)(2,1)S(1)}, bf16[16,64,128]{2,1,0:T(8,128)(2,1)S(1)}, u32[]{:S(2)}, u32[]{:S(2)}) collective-permute-start(bf16[16,64,128]{2,1,0:T(8,128)(2,1)S(1)} %shard_map.74.refs_0_.own), channel_id=1, source_target_pairs={{0,32},{2,34},{4,36},{6,38},{8,40},{10,42},{12,44},{14,46},{16,48}... | collective-permute-start | bytes 786440 | tf_op jit(solution)/shard_map/ppermute | solution.py:330
  41.4 8.5 %collective-permute-start.7 = (bf16[16,64,128]{2,1,0:T(8,128)(2,1)S(1)}, bf16[16,64,128]{2,1,0:T(8,128)(2,1)S(1)}, u32[]{:S(2)}, u32[]{:S(2)}) collective-permute-start(bf16[16,64,128]{2,1,0:T(8,128)(2,1)S(1)} %shard_map.75.token.own), channel_id=1, source_target_pairs={{0,16},{2,18},{4,20},{6,22},{8,24},{10,26},{12,28},{14,30},{16,0},... | collective-permute-start | bytes 786440 | tf_op jit(solution)/shard_map/ppermute | solution.py:330
  47.0 6.8 %collective-permute-start.10 = (bf16[16,64,128]{2,1,0:T(8,128)(2,1)S(1)}, bf16[16,64,128]{2,1,0:T(8,128)(2,1)S(1)}, u32[]{:S(2)}, u32[]{:S(2)}) collective-permute-start(bf16[16,64,128]{2,1,0:T(8,128)(2,1)S(1)} %shard_map.77.refs_0_.own), channel_id=1, source_target_pairs={{0,64},{2,66},{4,68},{6,70},{8,72},{10,74},{12,76},{14,78},{16,80}... | collective-permute-start | bytes 786440 | tf_op jit(solution)/shard_map/ppermute | solution.py:330
  50.4 9.0 %collective-permute-start.9 = (bf16[16,64,128]{2,1,0:T(8,128)(2,1)S(1)}, bf16[16,64,128]{2,1,0:T(8,128)(2,1)S(1)}, u32[]{:S(2)}, u32[]{:S(2)}) collective-permute-start(bf16[16,64,128]{2,1,0:T(8,128)(2,1)S(1)} %shard_map.78.refs_0_.own), channel_id=1, source_target_pairs={{0,32},{2,34},{4,36},{6,38},{8,40},{10,42},{12,44},{14,46},{16,48}... | collective-permute-start | bytes 786440 | tf_op jit(solution)/shard_map/ppermute | solution.py:330
  54.2 7.5 %collective-permute-start.12 = (bf16[16,64,128]{2,1,0:T(8,128)(2,1)S(1)}, bf16[16,64,128]{2,1,0:T(8,128)(2,1)S(1)}, u32[]{:S(2)}, u32[]{:S(2)}) collective-permute-start(bf16[16,64,128]{2,1,0:T(8,128)(2,1)S(1)} %shard_map.79.refs_0_.own), channel_id=1, source_target_pairs={{0,1},{1,0},{2,3},{3,2},{4,5},{5,4},{6,7},{7,6},{8,9},{9,8},{10,11... | collective-permute-start | bytes 786440 | tf_op jit(solution)/shard_map/ppermute | solution.py:330
  59.9 7.0 %collective-permute-start.11 = (bf16[16,64,128]{2,1,0:T(8,128)(2,1)S(1)}, bf16[16,64,128]{2,1,0:T(8,128)(2,1)S(1)}, u32[]{:S(2)}, u32[]{:S(2)}) collective-permute-start(bf16[16,64,128]{2,1,0:T(8,128)(2,1)S(1)} %shard_map.80.token.own), channel_id=1, source_target_pairs={{0,64},{2,66},{4,68},{6,70},{8,72},{10,74},{12,76},{14,78},{16,80}... | collective-permute-start | bytes 786440 | tf_op jit(solution)/shard_map/ppermute | solution.py:330
  67.3 8.6 %collective-permute-start.13 = (bf16[16,64,128]{2,1,0:T(8,128)(2,1)S(1)}, bf16[16,64,128]{2,1,0:T(8,128)(2,1)S(1)}, u32[]{:S(2)}, u32[]{:S(2)}) collective-permute-start(bf16[16,64,128]{2,1,0:T(8,128)(2,1)S(1)} %shard_map.82.own.token), channel_id=1, source_target_pairs={{0,1},{1,0},{2,3},{3,2},{4,5},{5,4},{6,7},{7,6},{8,9},{9,8},{10,11... | collective-permute-start | bytes 786440 | tf_op jit(solution)/shard_map/ppermute | solution.py:330
  68.1 15.7 %collective-permute-start.15 = (bf16[16,64,128]{2,1,0:T(8,128)(2,1)S(1)}, bf16[16,64,128]{2,1,0:T(8,128)(2,1)S(1)}, u32[]{:S(2)}, u32[]{:S(2)}) collective-permute-start(bf16[16,64,128]{2,1,0:T(8,128)(2,1)S(1)} %shard_map.81.refs_0_), channel_id=1, source_target_pairs={{0,0},{1,2},{2,1},{3,3},{4,64},{5,66},{6,65},{7,67},{8,32},{9,34},... | collective-permute-start | bytes 786440 | tf_op jit(solution)/shard_map/ppermute | solution.py:340
  78.0 10.0 %collective-permute-start.14 = (bf16[16,64,128]{2,1,0:T(8,128)(2,1)S(1)}, bf16[16,64,128]{2,1,0:T(8,128)(2,1)S(1)}, u32[]{:S(2)}, u32[]{:S(2)}) collective-permute-start(bf16[16,64,128]{2,1,0:T(8,128)(2,1)S(1)} %shard_map.83.token), channel_id=1, source_target_pairs={{0,0},{1,2},{2,1},{3,3},{4,64},{5,66},{6,65},{7,67},{8,32},{9,34},... | collective-permute-start | bytes 786440 | tf_op jit(solution)/shard_map/ppermute | solution.py:340
  86.1 7.9 %collective-permute-start.17 = (bf16[32,32,128]{2,1,0:T(8,128)(2,1)S(1)}, bf16[32,32,128]{2,1,0:T(8,128)(2,1)S(1)}, u32[]{:S(2)}, u32[]{:S(2)}) collective-permute-start(bf16[32,32,128]{2,1,0:T(8,128)(2,1)S(1)} %get-tuple-element.45.token), channel_id=1, source_target_pairs={{0,0},{1,2},{2,1},{3,3},{4,64},{5,66},{6,65},{7,67},{8,32},{9,34},... | collective-permute-start | bytes 786440 | tf_op jit(solution)/shard_map/ppermute | solution.py:340
  90.3 7.7 %collective-permute-start.16 = (bf16[32,32,128]{2,1,0:T(8,128)(2,1)S(1)}, bf16[32,32,128]{2,1,0:T(8,128)(2,1)S(1)}, u32[]{:S(2)}, u32[]{:S(2)}) collective-permute-start(bf16[32,32,128]{2,1,0:T(8,128)(2,1)S(1)} %get-tuple-element.47.token), channel_id=1, source_target_pairs={{0,0},{1,2},{2,1},{3,3},{4,64},{5,66},{6,65},{7,67},{8,32},{9,34},... | collective-permute-start | bytes 786440 | tf_op jit(solution)/shard_map/ppermute | solution.py:340
  96.1 8.1 %collective-permute-start.19 = (bf16[32,32,128]{2,1,0:T(8,128)(2,1)S(1)}, bf16[32,32,128]{2,1,0:T(8,128)(2,1)S(1)}, u32[]{:S(2)}, u32[]{:S(2)}) collective-permute-start(bf16[32,32,128]{2,1,0:T(8,128)(2,1)S(1)} %get-tuple-element.48.token), channel_id=1, source_target_pairs={{0,1},{1,0},{2,3},{3,2},{4,5},{5,4},{6,7},{7,6},{8,9},{9,8},{10,11... | collective-permute-start | bytes 786440 | tf_op jit(solution)/shard_map/ppermute | solution.py:330
  100.2 27.6 %collective-permute-start.18 = (bf16[32,32,128]{2,1,0:T(8,128)(2,1)S(1)}, bf16[32,32,128]{2,1,0:T(8,128)(2,1)S(1)}, u32[]{:S(2)}, u32[]{:S(2)}) collective-permute-start(bf16[32,32,128]{2,1,0:T(8,128)(2,1)S(1)} %get-tuple-element.50.refs_0_), channel_id=1, source_target_pairs={{0,1},{1,0},{2,3},{3,2},{4,5},{5,4},{6,7},{7,6},{8,9},{9,8},{10,11... | collective-permute-start | bytes 786440 | tf_op jit(solution)/shard_map/ppermute | solution.py:330
  104.8 29.0 %collective-permute-start.21 = (bf16[32,32,128]{2,1,0:T(8,128)(2,1)S(1)}, bf16[32,32,128]{2,1,0:T(8,128)(2,1)S(1)}, u32[]{:S(2)}, u32[]{:S(2)}) collective-permute-start(bf16[32,32,128]{2,1,0:T(8,128)(2,1)S(1)} %get-tuple-element.52.refs_0_), channel_id=1, source_target_pairs={{0,64},{2,66},{4,68},{6,70},{8,72},{10,74},{12,76},{14,78},{16,80}... | collective-permute-start | bytes 786440 | tf_op jit(solution)/shard_map/ppermute | solution.py:330
  128.2 11.7 %collective-permute-start.20 = (bf16[32,32,128]{2,1,0:T(8,128)(2,1)S(1)}, bf16[32,32,128]{2,1,0:T(8,128)(2,1)S(1)}, u32[]{:S(2)}, u32[]{:S(2)}) collective-permute-start(bf16[32,32,128]{2,1,0:T(8,128)(2,1)S(1)} %get-tuple-element.54.refs_0_), channel_id=1, source_target_pairs={{0,64},{2,66},{4,68},{6,70},{8,72},{10,74},{12,76},{14,78},{16,80}... | collective-permute-start | bytes 786440 | tf_op jit(solution)/shard_map/ppermute | solution.py:330
  134.2 12.3 %collective-permute-start.23 = (bf16[32,32,128]{2,1,0:T(8,128)(2,1)S(1)}, bf16[32,32,128]{2,1,0:T(8,128)(2,1)S(1)}, u32[]{:S(2)}, u32[]{:S(2)}) collective-permute-start(bf16[32,32,128]{2,1,0:T(8,128)(2,1)S(1)} %get-tuple-element.56.refs_0_), channel_id=1, source_target_pairs={{0,32},{2,34},{4,36},{6,38},{8,40},{10,42},{12,44},{14,46},{16,48}... | collective-permute-start | bytes 786440 | tf_op jit(solution)/shard_map/ppermute | solution.py:330
  140.4 12.1 %collective-permute-start.22 = (bf16[32,32,128]{2,1,0:T(8,128)(2,1)S(1)}, bf16[32,32,128]{2,1,0:T(8,128)(2,1)S(1)}, u32[]{:S(2)}, u32[]{:S(2)}) collective-permute-start(bf16[32,32,128]{2,1,0:T(8,128)(2,1)S(1)} %get-tuple-element.58.refs_0_), channel_id=1, source_target_pairs={{0,32},{2,34},{4,36},{6,38},{8,40},{10,42},{12,44},{14,46},{16,48}... | collective-permute-start | bytes 786440 | tf_op jit(solution)/shard_map/ppermute | solution.py:330
  147.1 8.7 %collective-permute-start.25 = (bf16[32,32,128]{2,1,0:T(8,128)(2,1)S(1)}, bf16[32,32,128]{2,1,0:T(8,128)(2,1)S(1)}, u32[]{:S(2)}, u32[]{:S(2)}) collective-permute-start(bf16[32,32,128]{2,1,0:T(8,128)(2,1)S(1)} %get-tuple-element.61.token), channel_id=1, source_target_pairs={{0,16},{2,18},{4,20},{6,22},{8,24},{10,26},{12,28},{14,30},{16,0},... | collective-permute-start | bytes 786440 | tf_op jit(solution)/shard_map/ppermute | solution.py:330
  153.0 8.8 %collective-permute-start.24 = (bf16[32,32,128]{2,1,0:T(8,128)(2,1)S(1)}, bf16[32,32,128]{2,1,0:T(8,128)(2,1)S(1)}, u32[]{:S(2)}, u32[]{:S(2)}) collective-permute-start(bf16[32,32,128]{2,1,0:T(8,128)(2,1)S(1)} %get-tuple-element.63.token), channel_id=1, source_target_pairs={{0,16},{2,18},{4,20},{6,22},{8,24},{10,26},{12,28},{14,30},{16,0},... | collective-permute-start | bytes 786440 | tf_op jit(solution)/shard_map/ppermute | solution.py:330
  156.3 7.1 %collective-permute-start.27 = (bf16[32,32,128]{2,1,0:T(8,128)(2,1)S(1)}, bf16[32,32,128]{2,1,0:T(8,128)(2,1)S(1)}, u32[]{:S(2)}, u32[]{:S(2)}) collective-permute-start(bf16[32,32,128]{2,1,0:T(8,128)(2,1)S(1)} %get-tuple-element.69.refs_0_), channel_id=1, source_target_pairs={{0,8},{2,10},{4,12},{6,14},{8,0},{10,2},{12,4},{14,6},{16,24},{18,... | collective-permute-start | bytes 786440 | tf_op jit(solution)/shard_map/ppermute | solution.py:330
  162.3 7.9 %collective-permute-start.26 = (bf16[32,32,128]{2,1,0:T(8,128)(2,1)S(1)}, bf16[32,32,128]{2,1,0:T(8,128)(2,1)S(1)}, u32[]{:S(2)}, u32[]{:S(2)}) collective-permute-start(bf16[32,32,128]{2,1,0:T(8,128)(2,1)S(1)} %get-tuple-element.71.refs_0_), channel_id=1, source_target_pairs={{0,8},{2,10},{4,12},{6,14},{8,0},{10,2},{12,4},{14,6},{16,24},{18,... | collective-permute-start | bytes 786440 | tf_op jit(solution)/shard_map/ppermute | solution.py:330
  163.9 10.4 %collective-permute-start.29 = (bf16[32,32,128]{2,1,0:T(8,128)(2,1)S(1)}, bf16[32,32,128]{2,1,0:T(8,128)(2,1)S(1)}, u32[]{:S(2)}, u32[]{:S(2)}) collective-permute-start(bf16[32,32,128]{2,1,0:T(8,128)(2,1)S(1)} %get-tuple-element.73.refs_0_), channel_id=1, source_target_pairs={{0,4},{2,6},{4,0},{6,2},{8,12},{10,14},{12,8},{14,10},{16,20},{18,... | collective-permute-start | bytes 786440 | tf_op jit(solution)/shard_map/ppermute | solution.py:330
  170.6 11.5 %collective-permute-start.28 = (bf16[32,32,128]{2,1,0:T(8,128)(2,1)S(1)}, bf16[32,32,128]{2,1,0:T(8,128)(2,1)S(1)}, u32[]{:S(2)}, u32[]{:S(2)}) collective-permute-start(bf16[32,32,128]{2,1,0:T(8,128)(2,1)S(1)} %get-tuple-element.75.refs_0_), channel_id=1, source_target_pairs={{0,4},{2,6},{4,0},{6,2},{8,12},{10,14},{12,8},{14,10},{16,20},{18,... | collective-permute-start | bytes 786440 | tf_op jit(solution)/shard_map/ppermute | solution.py:330
  174.8 13.0 %collective-permute-start.31 = (bf16[32,32,128]{2,1,0:T(8,128)(2,1)S(1)}, bf16[32,32,128]{2,1,0:T(8,128)(2,1)S(1)}, u32[]{:S(2)}, u32[]{:S(2)}) collective-permute-start(bf16[32,32,128]{2,1,0:T(8,128)(2,1)S(1)} %get-tuple-element.77.refs_0_), channel_id=1, source_target_pairs={{0,2},{2,0},{4,6},{6,4},{8,10},{10,8},{12,14},{14,12},{16,18},{18,... | collective-permute-start | bytes 786440 | tf_op jit(solution)/shard_map/ppermute | solution.py:330
  182.7 6.8 %collective-permute-start.30 = (bf16[32,32,128]{2,1,0:T(8,128)(2,1)S(1)}, bf16[32,32,128]{2,1,0:T(8,128)(2,1)S(1)}, u32[]{:S(2)}, u32[]{:S(2)}) collective-permute-start(bf16[32,32,128]{2,1,0:T(8,128)(2,1)S(1)} %get-tuple-element.79.token), channel_id=1, source_target_pairs={{0,2},{2,0},{4,6},{6,4},{8,10},{10,8},{12,14},{14,12},{16,18},{18,... | collective-permute-start | bytes 786440 | tf_op jit(solution)/shard_map/ppermute | solution.py:330
  (6 other events, 106.3 us)

commit v6 on v5

--- a/solution.py
+++ b/solution.py
@@ -420,7 +420,7 @@
     first_back = top + 1 + 2 * GAP
     stages = first_back + top
     for step in range(stages + 1 + LAG * (CHUNKS - 1)):
-        for c in every if step < first_back else reversed(every):
+        for c in reversed(every) if step == first_back else every:
             stage = step - LAG * c
             if 0 <= stage < top:
                 level = stage
@@ -450,8 +450,9 @@
                 )
             if (stage, c) == (2, CHUNKS - 1):
                 wanted = token = order_call(wanted, token)
-            if stage == first_back + 2:
-                *residual, token = residual_call(c, by_box[c], token, *residual)
+            if (stage, c) in ((top + GAP, CHUNKS - 1), (top + 2 * GAP, 0)):
+                part = 0 if c else 1
+                *residual, token = residual_call(part, by_box[part], token, *residual)
     residual, gradient = residual[0], gradient[0]
     return (
         residual.reshape(total, 1, 1, boxes, points),

time: 192 us -> 189 us (0.984)
  waiting for transfers between devices: 59.7 us -> 48.4 us
  starting transfers between devices: 90.2 us -> 98.4 us
    ppermute x28, waiting for transfers between devices: 57.9 us -> 48.4 us  [exchange(): return lax.ppermute(array, axis, [(i, i ^ 1 << bit) for i in range(count)])]
    ppermute x28, starting transfers between devices: 71.2 us -> 79.3 us  [exchange(): return lax.ppermute(array, axis, [(i, i ^ 1 << bit) for i in range(count)])]
  transfers between devices with their start and end apart: 32 -> 32, of which waited for: 15 -> 16; matrix products, arithmetic and copies ran while one was open for 1% -> 1% of each run, Pallas kernels for 16% -> 15%
where the time goes in v6:
time: 189 us
  starting transfers between devices  98.4 us (52%)
  waiting for transfers between devices  48.4 us (26%)
  Pallas kernels  35.4 us (19%)
  local copies, waits for them, and re-layouts  5.39 us (3%)
    ppermute x28, starting transfers between devices, exchange(): return lax.ppermute(array, axis, [(i, i ^ 1 << bit) for i in range(count)])  79.3 us
    ppermute x28, waiting for transfers between devices, exchange(): return lax.ppermute(array, axis, [(i, i ^ 1 << bit) for i in range(count)])  48.4 us
    ppermute x4, starting transfers between devices, reversal(): return lax.ppermute(array, ('src', 'hi'), pairs_of)  19.1 us
    pallas_call x12, Pallas kernels, adjoint_call(): call(kernel, (kept_shape, pair_shape), specs, (VMEM, VMEM), [], flops, mo...  5.95 us
    pallas_call x12, Pallas kernels, cross_call(): call(kernel, forward_shape, specs, VMEM, [], flops, moved, 4)(*operands)  5.28 us
    pallas_call x2, Pallas kernels, target_call(): call(kernel, (shape(boxes, vectors, points), pair_shape), [VMEM] * 3 + [A...  4.55 us
    pallas_call x2, Pallas kernels, local_adjoint_call(): call(kernel, (kept_shape, pair_shape), [VMEM] * 2 + [ANY], (VMEM, VMEM),...  4.3 us
    pallas_call x2, Pallas kernels, local_forward_call(): call(kernel, forward_shape, [VMEM] * 3 + [ANY], VMEM, scratch, 7 * flops,...  4.28 us
  transfers between devices with their start and end apart: 32, of which 16 were waited for; matrix products, arithmetic and copies ran while one was open for 1% of the time, Pallas kernels for 15%

profile of v6, /device:TPU:1, one launch (start us, length us, event | category | flops | bytes accessed | tf_op | source)
XLA Modules:
  0.0 188.9 jit_solution(4418229770055658961)
XLA Ops:
  7.0 2.5 %slice_bitcast_fusion = (bf16[1,64,64,128]{3,2,1,0:T(8,128)(2,1)S(1)}, bf16[1,64,64,128]{3,2,1,0:T(8,128)(2,1)S(1)}, bf16[1,64,64,128]{3,2,1,0:T(8,128)(2,1)S(1)}) fusion(bf16[13,64,1,1,64,128]{5,4,1,3,2,0:T(8,128)(2,1)} %bitcast.18), kind=kLoop, calls=%fused_computation | loop fusion | bytes 6291456 | tf_op jit(solution)/shard_map/slice | solution.py:427
  11.7 6.3 %collective-permute-done.2.other = bf16[16,64,128]{2,1,0:T(8,128)(2,1)S(1)} collective-permute-done((bf16[16,64,128]{2,1,0:T(8,128)(2,1)S(1)}, bf16[16,64,128]{2,1,0:T(8,128)(2,1)S(1)}, u32[]{:S(2)}, u32[]{:S(2)}) %collective-permute-start.2) | collective-permute-done | bytes 262176 | tf_op jit(solution)/shard_map/ppermute | solution.py:330
  18.4 2.9 %collective-permute-start.4 = (bf16[16,64,128]{2,1,0:T(8,128)(2,1)S(1)}, bf16[16,64,128]{2,1,0:T(8,128)(2,1)S(1)}, u32[]{:S(2)}, u32[]{:S(2)}) collective-permute-start(bf16[16,64,128]{2,1,0:T(8,128)(2,1)S(1)} %shard_map.70.refs_0_.own), channel_id=1, source_target_pairs={{0,8},{2,10},{4,12},{6,14},{8,0},{10,2},{12,4},{14,6},{16,24},{18,... | collective-permute-start | bytes 786440 | tf_op jit(solution)/shard_map/ppermute | solution.py:330
  22.2 4.9 %collective-permute-done.4.other = bf16[16,64,128]{2,1,0:T(8,128)(2,1)S(1)} collective-permute-done((bf16[16,64,128]{2,1,0:T(8,128)(2,1)S(1)}, bf16[16,64,128]{2,1,0:T(8,128)(2,1)S(1)}, u32[]{:S(2)}, u32[]{:S(2)}) %collective-permute-start.4) | collective-permute-done | bytes 262176 | tf_op jit(solution)/shard_map/ppermute | solution.py:330
  27.5 3.8 %collective-permute-start.6 = (bf16[16,64,128]{2,1,0:T(8,128)(2,1)S(1)}, bf16[16,64,128]{2,1,0:T(8,128)(2,1)S(1)}, u32[]{:S(2)}, u32[]{:S(2)}) collective-permute-start(bf16[16,64,128]{2,1,0:T(8,128)(2,1)S(1)} %shard_map.72.refs_0_.own), channel_id=1, source_target_pairs={{0,16},{2,18},{4,20},{6,22},{8,24},{10,26},{12,28},{14,30},{16,0},... | collective-permute-start | bytes 786440 | tf_op jit(solution)/shard_map/ppermute | solution.py:330
  36.9 4.0 %collective-permute-done.5.other = bf16[16,64,128]{2,1,0:T(8,128)(2,1)S(1)} collective-permute-done((bf16[16,64,128]{2,1,0:T(8,128)(2,1)S(1)}, bf16[16,64,128]{2,1,0:T(8,128)(2,1)S(1)}, u32[]{:S(2)}, u32[]{:S(2)}) %collective-permute-start.5) | collective-permute-done | bytes 262176 | tf_op jit(solution)/shard_map/ppermute | solution.py:330
  41.4 3.7 %collective-permute-start.7 = (bf16[16,64,128]{2,1,0:T(8,128)(2,1)S(1)}, bf16[16,64,128]{2,1,0:T(8,128)(2,1)S(1)}, u32[]{:S(2)}, u32[]{:S(2)}) collective-permute-start(bf16[16,64,128]{2,1,0:T(8,128)(2,1)S(1)} %shard_map.75.token.own), channel_id=1, source_target_pairs={{0,16},{2,18},{4,20},{6,22},{8,24},{10,26},{12,28},{14,30},{16,0},... | collective-permute-start | bytes 786440 | tf_op jit(solution)/shard_map/ppermute | solution.py:330
  47.0 3.0 %collective-permute-start.10 = (bf16[16,64,128]{2,1,0:T(8,128)(2,1)S(1)}, bf16[16,64,128]{2,1,0:T(8,128)(2,1)S(1)}, u32[]{:S(2)}, u32[]{:S(2)}) collective-permute-start(bf16[16,64,128]{2,1,0:T(8,128)(2,1)S(1)} %shard_map.77.refs_0_.own), channel_id=1, source_target_pairs={{0,64},{2,66},{4,68},{6,70},{8,72},{10,74},{12,76},{14,78},{16,80}... | collective-permute-start | bytes 786440 | tf_op jit(solution)/shard_map/ppermute | solution.py:330
  50.9 2.9 %collective-permute-done.10.other = bf16[16,64,128]{2,1,0:T(8,128)(2,1)S(1)} collective-permute-done((bf16[16,64,128]{2,1,0:T(8,128)(2,1)S(1)}, bf16[16,64,128]{2,1,0:T(8,128)(2,1)S(1)}, u32[]{:S(2)}, u32[]{:S(2)}) %collective-permute-start.10) | collective-permute-done | bytes 262176 | tf_op jit(solution)/shard_map/ppermute | solution.py:330
  55.0 4.4 %collective-permute-done.9.other = bf16[16,64,128]{2,1,0:T(8,128)(2,1)S(1)} collective-permute-done((bf16[16,64,128]{2,1,0:T(8,128)(2,1)S(1)}, bf16[16,64,128]{2,1,0:T(8,128)(2,1)S(1)}, u32[]{:S(2)}, u32[]{:S(2)}) %collective-permute-start.9) | collective-permute-done | bytes 262176 | tf_op jit(solution)/shard_map/ppermute | solution.py:330
  61.7 2.1 %shard_map.81.refs_0_ = bf16[16,64,128]{2,1,0:T(8,128)(2,1)S(1)} custom-call(bf16[16,64,128]{2,1,0:T(8,128)(2,1)S(1)} %shard_map.79.refs_0_.own, bf16[16,64,128]{2,1,0:T(8,128)(2,1)S(1)} %collective-permute-done.12.other, bf16[13,64,64,128]{3,2,1,0:T(8,128)(2,1)S(1)} %bitcast.24, bf16[16,64,128]{2,1,0:T(8,128)(2,1)S(1)} %shard_map.80.token.own), custom_call_target="tpu_custom_call" | custom-call | flops 234881024 | bytes 7340032 | tf_op jit(solution)/shard_map/pallas_call | solution.py:401
  63.8 3.0 %collective-permute-done.11.other = bf16[16,64,128]{2,1,0:T(8,128)(2,1)S(1)} collective-permute-done((bf16[16,64,128]{2,1,0:T(8,128)(2,1)S(1)}, bf16[16,64,128]{2,1,0:T(8,128)(2,1)S(1)}, u32[]{:S(2)}, u32[]{:S(2)}) %collective-permute-start.11) | collective-permute-done | bytes 262176 | tf_op jit(solution)/shard_map/ppermute | solution.py:330
  68.1 7.8 %collective-permute-start.15 = (bf16[16,64,128]{2,1,0:T(8,128)(2,1)S(1)}, bf16[16,64,128]{2,1,0:T(8,128)(2,1)S(1)}, u32[]{:S(2)}, u32[]{:S(2)}) collective-permute-start(bf16[16,64,128]{2,1,0:T(8,128)(2,1)S(1)} %shard_map.81.refs_0_), channel_id=1, source_target_pairs={{0,0},{1,2},{2,1},{3,3},{4,64},{5,66},{6,65},{7,67},{8,32},{9,34},... | collective-permute-start | bytes 786440 | tf_op jit(solution)/shard_map/ppermute | solution.py:340
  78.0 5.8 %collective-permute-start.14 = (bf16[16,64,128]{2,1,0:T(8,128)(2,1)S(1)}, bf16[16,64,128]{2,1,0:T(8,128)(2,1)S(1)}, u32[]{:S(2)}, u32[]{:S(2)}) collective-permute-start(bf16[16,64,128]{2,1,0:T(8,128)(2,1)S(1)} %shard_map.83.token), channel_id=1, source_target_pairs={{0,0},{1,2},{2,1},{3,3},{4,64},{5,66},{6,65},{7,67},{8,32},{9,34},... | collective-permute-start | bytes 786440 | tf_op jit(solution)/shard_map/ppermute | solution.py:340
  83.8 2.3 %shard_map.84 = (bf16[64,32,128]{2,1,0:T(8,128)(2,1)S(1)}, bf16[32,32,128]{2,1,0:T(8,128)(2,1)S(1)}) custom-call(bf16[16,64,128]{2,1,0:T(8,128)(2,1)S(1)} %collective-permute-done.15.coeffs, bf16[64,64,128]{2,1,0:T(8,128)(2,1)S(1)} %bitcast.44, bf16[64,64,128]{2,1,0:T(8,128)(2,1)S(1)} %shard_map.76.refs_0_.wanted, bf16[16,64,128]{2,1,0:T(8,128)(2,1)S(1)} %shard_map.83.token), custom_call_target="tpu_custom_call" | custom-call | flops 67108864 | bytes 4194304 | tf_op jit(solution)/shard_map/pallas_call | solution.py:364
  88.0 2.3 %shard_map.85 = (bf16[64,32,128]{2,1,0:T(8,128)(2,1)S(1)}, bf16[32,32,128]{2,1,0:T(8,128)(2,1)S(1)}) custom-call(bf16[16,64,128]{2,1,0:T(8,128)(2,1)S(1)} %collective-permute-done.14.coeffs, bf16[64,64,128]{2,1,0:T(8,128)(2,1)S(1)} %bitcast.45, bf16[64,64,128]{2,1,0:T(8,128)(2,1)S(1)} %shard_map.76.refs_0_.wanted, ...), custom_call_target="tpu_custom_call" | custom-call | flops 67108864 | bytes 4194304 | tf_op jit(solution)/shard_map/pallas_call | solution.py:364
  90.3 3.6 %collective-permute-start.17 = (bf16[32,32,128]{2,1,0:T(8,128)(2,1)S(1)}, bf16[32,32,128]{2,1,0:T(8,128)(2,1)S(1)}, u32[]{:S(2)}, u32[]{:S(2)}) collective-permute-start(bf16[32,32,128]{2,1,0:T(8,128)(2,1)S(1)} %get-tuple-element.48.token), channel_id=1, source_target_pairs={{0,0},{1,2},{2,1},{3,3},{4,64},{5,66},{6,65},{7,67},{8,32},{9,34},... | collective-permute-start | bytes 786440 | tf_op jit(solution)/shard_map/ppermute | solution.py:340
  95.8 2.1 %shard_map.87 = (f32[32,32,128]{2,1,0:T(8,128)S(1)}, bf16[32,32,128]{2,1,0:T(8,128)(2,1)S(1)}) custom-call(bf16[32,32,128]{2,1,0:T(8,128)(2,1)S(1)} %collective-permute-done.16.adjoint, bf16[13,64,64,128]{3,2,1,0:T(8,128)(2,1)S(1)} %bitcast.27, f32[8,128]{1,0:T(8,128)S(1)} %get-tuple-element.49.token), custom_call_target="tpu_custom_call" | custom-call | flops 234881024 | bytes 7340032 | tf_op jit(solution)/shard_map/pallas_call | solution.py:408
  100.2 2.1 %shard_map.89 = (f32[32,32,128]{2,1,0:T(8,128)S(1)}, bf16[32,32,128]{2,1,0:T(8,128)(2,1)S(1)}) custom-call(bf16[32,32,128]{2,1,0:T(8,128)(2,1)S(1)} %collective-permute-done.17.adjoint, bf16[13,64,64,128]{3,2,1,0:T(8,128)(2,1)S(1)} %bitcast.28, f32[8,128]{1,0:T(8,128)S(1)} %get-tuple-element.53.token), custom_call_target="tpu_custom_call" | custom-call | flops 234881024 | bytes 7340032 | tf_op jit(solution)/shard_map/pallas_call | solution.py:408
  102.3 2.9 %collective-permute-done.19.received = bf16[32,32,128]{2,1,0:T(8,128)(2,1)S(1)} collective-permute-done((bf16[32,32,128]{2,1,0:T(8,128)(2,1)S(1)}, bf16[32,32,128]{2,1,0:T(8,128)(2,1)S(1)}, u32[]{:S(2)}, u32[]{:S(2)}) %collective-permute-start.19) | collective-permute-done | bytes 262176 | tf_op jit(solution)/shard_map/ppermute | solution.py:330
  105.7 21.7 %collective-permute-start.20 = (bf16[32,32,128]{2,1,0:T(8,128)(2,1)S(1)}, bf16[32,32,128]{2,1,0:T(8,128)(2,1)S(1)}, u32[]{:S(2)}, u32[]{:S(2)}) collective-permute-start(bf16[32,32,128]{2,1,0:T(8,128)(2,1)S(1)} %get-tuple-element.58.refs_0_), channel_id=1, source_target_pairs={{0,64},{2,66},{4,68},{6,70},{8,72},{10,74},{12,76},{14,78},{16,80}... | collective-permute-start | bytes 786440 | tf_op jit(solution)/shard_map/ppermute | solution.py:330
  128.8 2.4 %collective-permute-done.20.received = bf16[32,32,128]{2,1,0:T(8,128)(2,1)S(1)} collective-permute-done((bf16[32,32,128]{2,1,0:T(8,128)(2,1)S(1)}, bf16[32,32,128]{2,1,0:T(8,128)(2,1)S(1)}, u32[]{:S(2)}, u32[]{:S(2)}) %collective-permute-start.20) | collective-permute-done | bytes 262176 | tf_op jit(solution)/shard_map/ppermute | solution.py:330
  134.0 3.6 %collective-permute-start.21 = (bf16[32,32,128]{2,1,0:T(8,128)(2,1)S(1)}, bf16[32,32,128]{2,1,0:T(8,128)(2,1)S(1)}, u32[]{:S(2)}, u32[]{:S(2)}) collective-permute-start(bf16[32,32,128]{2,1,0:T(8,128)(2,1)S(1)} %get-tuple-element.61.refs_0_), channel_id=1, source_target_pairs={{0,64},{2,66},{4,68},{6,70},{8,72},{10,74},{12,76},{14,78},{16,80}... | collective-permute-start | bytes 786440 | tf_op jit(solution)/shard_map/ppermute | solution.py:330
  140.7 2.9 %collective-permute-done.21.received = bf16[32,32,128]{2,1,0:T(8,128)(2,1)S(1)} collective-permute-done((bf16[32,32,128]{2,1,0:T(8,128)(2,1)S(1)}, bf16[32,32,128]{2,1,0:T(8,128)(2,1)S(1)}, u32[]{:S(2)}, u32[]{:S(2)}) %collective-permute-start.21) | collective-permute-done | bytes 262176 | tf_op jit(solution)/shard_map/ppermute | solution.py:330
  144.2 2.6 %collective-permute-done.24.received = bf16[32,32,128]{2,1,0:T(8,128)(2,1)S(1)} collective-permute-done((bf16[32,32,128]{2,1,0:T(8,128)(2,1)S(1)}, bf16[32,32,128]{2,1,0:T(8,128)(2,1)S(1)}, u32[]{:S(2)}, u32[]{:S(2)}) %collective-permute-start.24) | collective-permute-done | bytes 262176 | tf_op jit(solution)/shard_map/ppermute | solution.py:330
  147.3 4.3 %collective-permute-start.26 = (bf16[32,32,128]{2,1,0:T(8,128)(2,1)S(1)}, bf16[32,32,128]{2,1,0:T(8,128)(2,1)S(1)}, u32[]{:S(2)}, u32[]{:S(2)}) collective-permute-start(bf16[32,32,128]{2,1,0:T(8,128)(2,1)S(1)} %get-tuple-element.67.refs_0_), channel_id=1, source_target_pairs={{0,8},{2,10},{4,12},{6,14},{8,0},{10,2},{12,4},{14,6},{16,24},{18,... | collective-permute-start | bytes 786440 | tf_op jit(solution)/shard_map/ppermute | solution.py:330
  152.6 2.6 %collective-permute-done.26.received = bf16[32,32,128]{2,1,0:T(8,128)(2,1)S(1)} collective-permute-done((bf16[32,32,128]{2,1,0:T(8,128)(2,1)S(1)}, bf16[32,32,128]{2,1,0:T(8,128)(2,1)S(1)}, u32[]{:S(2)}, u32[]{:S(2)}) %collective-permute-start.26) | collective-permute-done | bytes 262176 | tf_op jit(solution)/shard_map/ppermute | solution.py:330
  156.0 2.8 %collective-permute-done.25.received = bf16[32,32,128]{2,1,0:T(8,128)(2,1)S(1)} collective-permute-done((bf16[32,32,128]{2,1,0:T(8,128)(2,1)S(1)}, bf16[32,32,128]{2,1,0:T(8,128)(2,1)S(1)}, u32[]{:S(2)}, u32[]{:S(2)}) %collective-permute-start.25) | collective-permute-done | bytes 262176 | tf_op jit(solution)/shard_map/ppermute | solution.py:330
  159.4 3.7 %collective-permute-start.27 = (bf16[32,32,128]{2,1,0:T(8,128)(2,1)S(1)}, bf16[32,32,128]{2,1,0:T(8,128)(2,1)S(1)}, u32[]{:S(2)}, u32[]{:S(2)}) collective-permute-start(bf16[32,32,128]{2,1,0:T(8,128)(2,1)S(1)} %get-tuple-element.73.refs_0_), channel_id=1, source_target_pairs={{0,8},{2,10},{4,12},{6,14},{8,0},{10,2},{12,4},{14,6},{16,24},{18,... | collective-permute-start | bytes 786440 | tf_op jit(solution)/shard_map/ppermute | solution.py:330
  163.6 8.5 %collective-permute-start.30 = (bf16[32,32,128]{2,1,0:T(8,128)(2,1)S(1)}, bf16[32,32,128]{2,1,0:T(8,128)(2,1)S(1)}, u32[]{:S(2)}, u32[]{:S(2)}) collective-permute-start(bf16[32,32,128]{2,1,0:T(8,128)(2,1)S(1)} %get-tuple-element.75.refs_0_), channel_id=1, source_target_pairs={{0,2},{2,0},{4,6},{6,4},{8,10},{10,8},{12,14},{14,12},{16,18},{18,... | collective-permute-start | bytes 786440 | tf_op jit(solution)/shard_map/ppermute | solution.py:330
  178.9 6.2 %collective-permute-start.31 = (bf16[32,32,128]{2,1,0:T(8,128)(2,1)S(1)}, bf16[32,32,128]{2,1,0:T(8,128)(2,1)S(1)}, u32[]{:S(2)}, u32[]{:S(2)}) collective-permute-start(bf16[32,32,128]{2,1,0:T(8,128)(2,1)S(1)} %get-tuple-element.81.token), channel_id=1, source_target_pairs={{0,2},{2,0},{4,6},{6,4},{8,10},{10,8},{12,14},{14,12},{16,18},{18,... | collective-permute-start | bytes 786440 | tf_op jit(solution)/shard_map/ppermute | solution.py:330
  186.3 2.3 %shard_map.103 = (bf16[64,64,128]{2,1,0:T(8,128)(2,1)}, f32[8,128]{1,0:T(8,128)}) custom-call(f32[32,32,128]{2,1,0:T(8,128)S(1)} %get-tuple-element.80.held_part, bf16[32,32,128]{2,1,0:T(8,128)(2,1)S(1)} %collective-permute-done.31.received, bf16[64,64,128]{2,1,0:T(8,128)(2,1)S(1)} %bitcast.43, ...), custom_call_target="tpu_custom_call", output_to_operand_aliasing={{0}: (4, {})} | custom-call | flops 33554432 | bytes 2097152 | tf_op jit(solution)/shard_map/pallas_call | solution.py:379
  (81 shorter events, 51.4 us)
Async XLA Ops:
  5.5 4.1 %collective-permute-start.1 = (bf16[16,64,128]{2,1,0:T(8,128)(2,1)S(1)}, bf16[16,64,128]{2,1,0:T(8,128)(2,1)S(1)}, u32[]{:S(2)}, u32[]{:S(2)}) collective-permute-start(bf16[16,64,128]{2,1,0:T(8,128)(2,1)S(1)} %get-tuple-element.44.own.refs_0_), channel_id=1, source_target_pairs={{0,2},{2,0},{4,6},{6,4},{8,10},{10,8},{12,14},{14,12},{16,18},{18,... | collective-permute-start | bytes 786440 | tf_op jit(solution)/shard_map/ppermute | solution.py:330
  10.0 8.0 %collective-permute-start.2 = (bf16[16,64,128]{2,1,0:T(8,128)(2,1)S(1)}, bf16[16,64,128]{2,1,0:T(8,128)(2,1)S(1)}, u32[]{:S(2)}, u32[]{:S(2)}) collective-permute-start(bf16[16,64,128]{2,1,0:T(8,128)(2,1)S(1)} %shard_map.69.own.refs_0_), channel_id=1, source_target_pairs={{0,4},{2,6},{4,0},{6,2},{8,12},{10,14},{12,8},{14,10},{16,20},{18,... | collective-permute-start | bytes 786440 | tf_op jit(solution)/shard_map/ppermute | solution.py:330
  11.4 10.0 %collective-permute-start = (bf16[16,64,128]{2,1,0:T(8,128)(2,1)S(1)}, bf16[16,64,128]{2,1,0:T(8,128)(2,1)S(1)}, u32[]{:S(2)}, u32[]{:S(2)}) collective-permute-start(bf16[16,64,128]{2,1,0:T(8,128)(2,1)S(1)} %get-tuple-element.43.own), channel_id=1, source_target_pairs={{0,2},{2,0},{4,6},{6,4},{8,10},{10,8},{12,14},{14,12},{16,18},{18,... | collective-permute-start | bytes 786440 | tf_op jit(solution)/shard_map/ppermute | solution.py:330
  18.4 8.6 %collective-permute-start.4 = (bf16[16,64,128]{2,1,0:T(8,128)(2,1)S(1)}, bf16[16,64,128]{2,1,0:T(8,128)(2,1)S(1)}, u32[]{:S(2)}, u32[]{:S(2)}) collective-permute-start(bf16[16,64,128]{2,1,0:T(8,128)(2,1)S(1)} %shard_map.70.refs_0_.own), channel_id=1, source_target_pairs={{0,8},{2,10},{4,12},{6,14},{8,0},{10,2},{12,4},{14,6},{16,24},{18,... | collective-permute-start | bytes 786440 | tf_op jit(solution)/shard_map/ppermute | solution.py:330
  21.8 11.0 %collective-permute-start.3 = (bf16[16,64,128]{2,1,0:T(8,128)(2,1)S(1)}, bf16[16,64,128]{2,1,0:T(8,128)(2,1)S(1)}, u32[]{:S(2)}, u32[]{:S(2)}) collective-permute-start(bf16[16,64,128]{2,1,0:T(8,128)(2,1)S(1)} %shard_map.71.refs_0_.own), channel_id=1, source_target_pairs={{0,4},{2,6},{4,0},{6,2},{8,12},{10,14},{12,8},{14,10},{16,20},{18,... | collective-permute-start | bytes 786440 | tf_op jit(solution)/shard_map/ppermute | solution.py:330
  27.5 7.6 %collective-permute-start.6 = (bf16[16,64,128]{2,1,0:T(8,128)(2,1)S(1)}, bf16[16,64,128]{2,1,0:T(8,128)(2,1)S(1)}, u32[]{:S(2)}, u32[]{:S(2)}) collective-permute-start(bf16[16,64,128]{2,1,0:T(8,128)(2,1)S(1)} %shard_map.72.refs_0_.own), channel_id=1, source_target_pairs={{0,16},{2,18},{4,20},{6,22},{8,24},{10,26},{12,28},{14,30},{16,0},... | collective-permute-start | bytes 786440 | tf_op jit(solution)/shard_map/ppermute | solution.py:330
  33.3 7.7 %collective-permute-start.5 = (bf16[16,64,128]{2,1,0:T(8,128)(2,1)S(1)}, bf16[16,64,128]{2,1,0:T(8,128)(2,1)S(1)}, u32[]{:S(2)}, u32[]{:S(2)}) collective-permute-start(bf16[16,64,128]{2,1,0:T(8,128)(2,1)S(1)} %shard_map.73.refs_0_.own), channel_id=1, source_target_pairs={{0,8},{2,10},{4,12},{6,14},{8,0},{10,2},{12,4},{14,6},{16,24},{18,... | collective-permute-start | bytes 786440 | tf_op jit(solution)/shard_map/ppermute | solution.py:330
  35.5 11.0 %collective-permute-start.8 = (bf16[16,64,128]{2,1,0:T(8,128)(2,1)S(1)}, bf16[16,64,128]{2,1,0:T(8,128)(2,1)S(1)}, u32[]{:S(2)}, u32[]{:S(2)}) collective-permute-start(bf16[16,64,128]{2,1,0:T(8,128)(2,1)S(1)} %shard_map.74.refs_0_.own), channel_id=1, source_target_pairs={{0,32},{2,34},{4,36},{6,38},{8,40},{10,42},{12,44},{14,46},{16,48}... | collective-permute-start | bytes 786440 | tf_op jit(solution)/shard_map/ppermute | solution.py:330
  41.4 8.5 %collective-permute-start.7 = (bf16[16,64,128]{2,1,0:T(8,128)(2,1)S(1)}, bf16[16,64,128]{2,1,0:T(8,128)(2,1)S(1)}, u32[]{:S(2)}, u32[]{:S(2)}) collective-permute-start(bf16[16,64,128]{2,1,0:T(8,128)(2,1)S(1)} %shard_map.75.token.own), channel_id=1, source_target_pairs={{0,16},{2,18},{4,20},{6,22},{8,24},{10,26},{12,28},{14,30},{16,0},... | collective-permute-start | bytes 786440 | tf_op jit(solution)/shard_map/ppermute | solution.py:330
  47.0 6.8 %collective-permute-start.10 = (bf16[16,64,128]{2,1,0:T(8,128)(2,1)S(1)}, bf16[16,64,128]{2,1,0:T(8,128)(2,1)S(1)}, u32[]{:S(2)}, u32[]{:S(2)}) collective-permute-start(bf16[16,64,128]{2,1,0:T(8,128)(2,1)S(1)} %shard_map.77.refs_0_.own), channel_id=1, source_target_pairs={{0,64},{2,66},{4,68},{6,70},{8,72},{10,74},{12,76},{14,78},{16,80}... | collective-permute-start | bytes 786440 | tf_op jit(solution)/shard_map/ppermute | solution.py:330
  50.4 9.0 %collective-permute-start.9 = (bf16[16,64,128]{2,1,0:T(8,128)(2,1)S(1)}, bf16[16,64,128]{2,1,0:T(8,128)(2,1)S(1)}, u32[]{:S(2)}, u32[]{:S(2)}) collective-permute-start(bf16[16,64,128]{2,1,0:T(8,128)(2,1)S(1)} %shard_map.78.refs_0_.own), channel_id=1, source_target_pairs={{0,32},{2,34},{4,36},{6,38},{8,40},{10,42},{12,44},{14,46},{16,48}... | collective-permute-start | bytes 786440 | tf_op jit(solution)/shard_map/ppermute | solution.py:330
  54.2 7.5 %collective-permute-start.12 = (bf16[16,64,128]{2,1,0:T(8,128)(2,1)S(1)}, bf16[16,64,128]{2,1,0:T(8,128)(2,1)S(1)}, u32[]{:S(2)}, u32[]{:S(2)}) collective-permute-start(bf16[16,64,128]{2,1,0:T(8,128)(2,1)S(1)} %shard_map.79.refs_0_.own), channel_id=1, source_target_pairs={{0,1},{1,0},{2,3},{3,2},{4,5},{5,4},{6,7},{7,6},{8,9},{9,8},{10,11... | collective-permute-start | bytes 786440 | tf_op jit(solution)/shard_map/ppermute | solution.py:330
  59.9 7.0 %collective-permute-start.11 = (bf16[16,64,128]{2,1,0:T(8,128)(2,1)S(1)}, bf16[16,64,128]{2,1,0:T(8,128)(2,1)S(1)}, u32[]{:S(2)}, u32[]{:S(2)}) collective-permute-start(bf16[16,64,128]{2,1,0:T(8,128)(2,1)S(1)} %shard_map.80.token.own), channel_id=1, source_target_pairs={{0,64},{2,66},{4,68},{6,70},{8,72},{10,74},{12,76},{14,78},{16,80}... | collective-permute-start | bytes 786440 | tf_op jit(solution)/shard_map/ppermute | solution.py:330
  67.3 8.6 %collective-permute-start.13 = (bf16[16,64,128]{2,1,0:T(8,128)(2,1)S(1)}, bf16[16,64,128]{2,1,0:T(8,128)(2,1)S(1)}, u32[]{:S(2)}, u32[]{:S(2)}) collective-permute-start(bf16[16,64,128]{2,1,0:T(8,128)(2,1)S(1)} %shard_map.82.own.token), channel_id=1, source_target_pairs={{0,1},{1,0},{2,3},{3,2},{4,5},{5,4},{6,7},{7,6},{8,9},{9,8},{10,11... | collective-permute-start | bytes 786440 | tf_op jit(solution)/shard_map/ppermute | solution.py:330
  68.1 15.7 %collective-permute-start.15 = (bf16[16,64,128]{2,1,0:T(8,128)(2,1)S(1)}, bf16[16,64,128]{2,1,0:T(8,128)(2,1)S(1)}, u32[]{:S(2)}, u32[]{:S(2)}) collective-permute-start(bf16[16,64,128]{2,1,0:T(8,128)(2,1)S(1)} %shard_map.81.refs_0_), channel_id=1, source_target_pairs={{0,0},{1,2},{2,1},{3,3},{4,64},{5,66},{6,65},{7,67},{8,32},{9,34},... | collective-permute-start | bytes 786440 | tf_op jit(solution)/shard_map/ppermute | solution.py:340
  78.0 10.0 %collective-permute-start.14 = (bf16[16,64,128]{2,1,0:T(8,128)(2,1)S(1)}, bf16[16,64,128]{2,1,0:T(8,128)(2,1)S(1)}, u32[]{:S(2)}, u32[]{:S(2)}) collective-permute-start(bf16[16,64,128]{2,1,0:T(8,128)(2,1)S(1)} %shard_map.83.token), channel_id=1, source_target_pairs={{0,0},{1,2},{2,1},{3,3},{4,64},{5,66},{6,65},{7,67},{8,32},{9,34},... | collective-permute-start | bytes 786440 | tf_op jit(solution)/shard_map/ppermute | solution.py:340
  86.1 9.7 %collective-permute-start.16 = (bf16[32,32,128]{2,1,0:T(8,128)(2,1)S(1)}, bf16[32,32,128]{2,1,0:T(8,128)(2,1)S(1)}, u32[]{:S(2)}, u32[]{:S(2)}) collective-permute-start(bf16[32,32,128]{2,1,0:T(8,128)(2,1)S(1)} %get-tuple-element.45.token), channel_id=1, source_target_pairs={{0,0},{1,2},{2,1},{3,3},{4,64},{5,66},{6,65},{7,67},{8,32},{9,34},... | collective-permute-start | bytes 786440 | tf_op jit(solution)/shard_map/ppermute | solution.py:340
  90.3 9.8 %collective-permute-start.17 = (bf16[32,32,128]{2,1,0:T(8,128)(2,1)S(1)}, bf16[32,32,128]{2,1,0:T(8,128)(2,1)S(1)}, u32[]{:S(2)}, u32[]{:S(2)}) collective-permute-start(bf16[32,32,128]{2,1,0:T(8,128)(2,1)S(1)} %get-tuple-element.48.token), channel_id=1, source_target_pairs={{0,0},{1,2},{2,1},{3,3},{4,64},{5,66},{6,65},{7,67},{8,32},{9,34},... | collective-permute-start | bytes 786440 | tf_op jit(solution)/shard_map/ppermute | solution.py:340
  98.0 7.2 %collective-permute-start.19 = (bf16[32,32,128]{2,1,0:T(8,128)(2,1)S(1)}, bf16[32,32,128]{2,1,0:T(8,128)(2,1)S(1)}, u32[]{:S(2)}, u32[]{:S(2)}) collective-permute-start(bf16[32,32,128]{2,1,0:T(8,128)(2,1)S(1)} %get-tuple-element.50.token), channel_id=1, source_target_pairs={{0,1},{1,0},{2,3},{3,2},{4,5},{5,4},{6,7},{7,6},{8,9},{9,8},{10,11... | collective-permute-start | bytes 786440 | tf_op jit(solution)/shard_map/ppermute | solution.py:330
  105.7 25.5 %collective-permute-start.20 = (bf16[32,32,128]{2,1,0:T(8,128)(2,1)S(1)}, bf16[32,32,128]{2,1,0:T(8,128)(2,1)S(1)}, u32[]{:S(2)}, u32[]{:S(2)}) collective-permute-start(bf16[32,32,128]{2,1,0:T(8,128)(2,1)S(1)} %get-tuple-element.58.refs_0_), channel_id=1, source_target_pairs={{0,64},{2,66},{4,68},{6,70},{8,72},{10,74},{12,76},{14,78},{16,80}... | collective-permute-start | bytes 786440 | tf_op jit(solution)/shard_map/ppermute | solution.py:330
  127.4 6.1 %collective-permute-start.18 = (bf16[32,32,128]{2,1,0:T(8,128)(2,1)S(1)}, bf16[32,32,128]{2,1,0:T(8,128)(2,1)S(1)}, u32[]{:S(2)}, u32[]{:S(2)}) collective-permute-start(bf16[32,32,128]{2,1,0:T(8,128)(2,1)S(1)} %get-tuple-element.55.refs_0_), channel_id=1, source_target_pairs={{0,1},{1,0},{2,3},{3,2},{4,5},{5,4},{6,7},{7,6},{8,9},{9,8},{10,11... | collective-permute-start | bytes 786440 | tf_op jit(solution)/shard_map/ppermute | solution.py:330
  131.7 7.8 %collective-permute-start.22 = (bf16[32,32,128]{2,1,0:T(8,128)(2,1)S(1)}, bf16[32,32,128]{2,1,0:T(8,128)(2,1)S(1)}, u32[]{:S(2)}, u32[]{:S(2)}) collective-permute-start(bf16[32,32,128]{2,1,0:T(8,128)(2,1)S(1)} %get-tuple-element.59.refs_0_), channel_id=1, source_target_pairs={{0,32},{2,34},{4,36},{6,38},{8,40},{10,42},{12,44},{14,46},{16,48}... | collective-permute-start | bytes 786440 | tf_op jit(solution)/shard_map/ppermute | solution.py:330
  134.0 9.6 %collective-permute-start.21 = (bf16[32,32,128]{2,1,0:T(8,128)(2,1)S(1)}, bf16[32,32,128]{2,1,0:T(8,128)(2,1)S(1)}, u32[]{:S(2)}, u32[]{:S(2)}) collective-permute-start(bf16[32,32,128]{2,1,0:T(8,128)(2,1)S(1)} %get-tuple-element.61.refs_0_), channel_id=1, source_target_pairs={{0,64},{2,66},{4,68},{6,70},{8,72},{10,74},{12,76},{14,78},{16,80}... | collective-permute-start | bytes 786440 | tf_op jit(solution)/shard_map/ppermute | solution.py:330
  140.0 6.8 %collective-permute-start.24 = (bf16[32,32,128]{2,1,0:T(8,128)(2,1)S(1)}, bf16[32,32,128]{2,1,0:T(8,128)(2,1)S(1)}, u32[]{:S(2)}, u32[]{:S(2)}) collective-permute-start(bf16[32,32,128]{2,1,0:T(8,128)(2,1)S(1)} %get-tuple-element.63.refs_0_), channel_id=1, source_target_pairs={{0,16},{2,18},{4,20},{6,22},{8,24},{10,26},{12,28},{14,30},{16,0},... | collective-permute-start | bytes 786440 | tf_op jit(solution)/shard_map/ppermute | solution.py:330
  144.1 7.4 %collective-permute-start.23 = (bf16[32,32,128]{2,1,0:T(8,128)(2,1)S(1)}, bf16[32,32,128]{2,1,0:T(8,128)(2,1)S(1)}, u32[]{:S(2)}, u32[]{:S(2)}) collective-permute-start(bf16[32,32,128]{2,1,0:T(8,128)(2,1)S(1)} %get-tuple-element.65.refs_0_), channel_id=1, source_target_pairs={{0,32},{2,34},{4,36},{6,38},{8,40},{10,42},{12,44},{14,46},{16,48}... | collective-permute-start | bytes 786440 | tf_op jit(solution)/shard_map/ppermute | solution.py:330
  147.3 8.0 %collective-permute-start.26 = (bf16[32,32,128]{2,1,0:T(8,128)(2,1)S(1)}, bf16[32,32,128]{2,1,0:T(8,128)(2,1)S(1)}, u32[]{:S(2)}, u32[]{:S(2)}) collective-permute-start(bf16[32,32,128]{2,1,0:T(8,128)(2,1)S(1)} %get-tuple-element.67.refs_0_), channel_id=1, source_target_pairs={{0,8},{2,10},{4,12},{6,14},{8,0},{10,2},{12,4},{14,6},{16,24},{18,... | collective-permute-start | bytes 786440 | tf_op jit(solution)/shard_map/ppermute | solution.py:330
  152.0 6.8 %collective-permute-start.25 = (bf16[32,32,128]{2,1,0:T(8,128)(2,1)S(1)}, bf16[32,32,128]{2,1,0:T(8,128)(2,1)S(1)}, u32[]{:S(2)}, u32[]{:S(2)}) collective-permute-start(bf16[32,32,128]{2,1,0:T(8,128)(2,1)S(1)} %get-tuple-element.69.refs_0_), channel_id=1, source_target_pairs={{0,16},{2,18},{4,20},{6,22},{8,24},{10,26},{12,28},{14,30},{16,0},... | collective-permute-start | bytes 786440 | tf_op jit(solution)/shard_map/ppermute | solution.py:330
  155.8 7.3 %collective-permute-start.28 = (bf16[32,32,128]{2,1,0:T(8,128)(2,1)S(1)}, bf16[32,32,128]{2,1,0:T(8,128)(2,1)S(1)}, u32[]{:S(2)}, u32[]{:S(2)}) collective-permute-start(bf16[32,32,128]{2,1,0:T(8,128)(2,1)S(1)} %get-tuple-element.71.refs_0_), channel_id=1, source_target_pairs={{0,4},{2,6},{4,0},{6,2},{8,12},{10,14},{12,8},{14,10},{16,20},{18,... | collective-permute-start | bytes 786440 | tf_op jit(solution)/shard_map/ppermute | solution.py:330
  159.4 12.7 %collective-permute-start.27 = (bf16[32,32,128]{2,1,0:T(8,128)(2,1)S(1)}, bf16[32,32,128]{2,1,0:T(8,128)(2,1)S(1)}, u32[]{:S(2)}, u32[]{:S(2)}) collective-permute-start(bf16[32,32,128]{2,1,0:T(8,128)(2,1)S(1)} %get-tuple-element.73.refs_0_), channel_id=1, source_target_pairs={{0,8},{2,10},{4,12},{6,14},{8,0},{10,2},{12,4},{14,6},{16,24},{18,... | collective-permute-start | bytes 786440 | tf_op jit(solution)/shard_map/ppermute | solution.py:330
  163.6 11.1 %collective-permute-start.30 = (bf16[32,32,128]{2,1,0:T(8,128)(2,1)S(1)}, bf16[32,32,128]{2,1,0:T(8,128)(2,1)S(1)}, u32[]{:S(2)}, u32[]{:S(2)}) collective-permute-start(bf16[32,32,128]{2,1,0:T(8,128)(2,1)S(1)} %get-tuple-element.75.refs_0_), channel_id=1, source_target_pairs={{0,2},{2,0},{4,6},{6,4},{8,10},{10,8},{12,14},{14,12},{16,18},{18,... | collective-permute-start | bytes 786440 | tf_op jit(solution)/shard_map/ppermute | solution.py:330
  172.6 5.8 %collective-permute-start.29 = (bf16[32,32,128]{2,1,0:T(8,128)(2,1)S(1)}, bf16[32,32,128]{2,1,0:T(8,128)(2,1)S(1)}, u32[]{:S(2)}, u32[]{:S(2)}) collective-permute-start(bf16[32,32,128]{2,1,0:T(8,128)(2,1)S(1)} %get-tuple-element.77.token), channel_id=1, source_target_pairs={{0,4},{2,6},{4,0},{6,2},{8,12},{10,14},{12,8},{14,10},{16,20},{18,... | collective-permute-start | bytes 786440 | tf_op jit(solution)/shard_map/ppermute | solution.py:330
  178.9 7.4 %collective-permute-start.31 = (bf16[32,32,128]{2,1,0:T(8,128)(2,1)S(1)}, bf16[32,32,128]{2,1,0:T(8,128)(2,1)S(1)}, u32[]{:S(2)}, u32[]{:S(2)}) collective-permute-start(bf16[32,32,128]{2,1,0:T(8,128)(2,1)S(1)} %get-tuple-element.81.token), channel_id=1, source_target_pairs={{0,2},{2,0},{4,6},{6,4},{8,10},{10,8},{12,14},{14,12},{16,18},{18,... | collective-permute-start | bytes 786440 | tf_op jit(solution)/shard_map/ppermute | solution.py:330
  (6 other events, 104.5 us)

commit v7 on v6

--- a/solution.py
+++ b/solution.py
@@ -420,7 +420,7 @@
     first_back = top + 1 + 2 * GAP
     stages = first_back + top
     for step in range(stages + 1 + LAG * (CHUNKS - 1)):
-        for c in reversed(every) if step == first_back else every:
+        for c in reversed(every) if step in (first_back, first_back + 1) else every:
             stage = step - LAG * c
             if 0 <= stage < top:
                 level = stage

time: 189 us -> 193 us (1.021)
  starting transfers between devices: 98.4 us -> 102 us
    ppermute x28, starting transfers between devices: 79.3 us -> 83.3 us  [exchange(): return lax.ppermute(array, axis, [(i, i ^ 1 << bit) for i in range(count)])]
  transfers between devices with their start and end apart: 32 -> 32, of which waited for: 16 -> 17; matrix products, arithmetic and copies ran while one was open for 1% -> 1% of each run, Pallas kernels for 15% -> 15%
where the time goes in v7:
time: 193 us; the launch traced here: 192 us
  starting transfers between devices  102 us (53%)
  waiting for transfers between devices  47.7 us (25%)
  Pallas kernels  35.4 us (18%)
  local copies, waits for them, and re-layouts  5.39 us (3%)
    ppermute x28, starting transfers between devices, exchange(): return lax.ppermute(array, axis, [(i, i ^ 1 << bit) for i in range(count)])  83.3 us
    ppermute x28, waiting for transfers between devices, exchange(): return lax.ppermute(array, axis, [(i, i ^ 1 << bit) for i in range(count)])  47.7 us
    ppermute x4, starting transfers between devices, reversal(): return lax.ppermute(array, ('src', 'hi'), pairs_of)  19.1 us
    pallas_call x12, Pallas kernels, adjoint_call(): call(kernel, (kept_shape, pair_shape), specs, (VMEM, VMEM), [], flops, mo...  5.96 us
    pallas_call x12, Pallas kernels, cross_call(): call(kernel, forward_shape, specs, VMEM, [], flops, moved, 4)(*operands)  5.28 us
    pallas_call x2, Pallas kernels, target_call(): call(kernel, (shape(boxes, vectors, points), pair_shape), [VMEM] * 3 + [A...  4.55 us
    pallas_call x2, Pallas kernels, local_adjoint_call(): call(kernel, (kept_shape, pair_shape), [VMEM] * 2 + [ANY], (VMEM, VMEM),...  4.3 us
    pallas_call x2, Pallas kernels, local_forward_call(): call(kernel, forward_shape, [VMEM] * 3 + [ANY], VMEM, scratch, 7 * flops,...  4.28 us
  transfers between devices with their start and end apart: 32, of which 17 were waited for; matrix products, arithmetic and copies ran while one was open for 1% of the time, Pallas kernels for 15%

profile of v7, /device:TPU:1, one launch (start us, length us, event | category | flops | bytes accessed | tf_op | source)
XLA Modules:
  0.0 192.3 jit_solution(15412454724245359569)
XLA Ops:
  7.0 2.5 %slice_bitcast_fusion = (bf16[1,64,64,128]{3,2,1,0:T(8,128)(2,1)S(1)}, bf16[1,64,64,128]{3,2,1,0:T(8,128)(2,1)S(1)}, bf16[1,64,64,128]{3,2,1,0:T(8,128)(2,1)S(1)}) fusion(bf16[13,64,1,1,64,128]{5,4,1,3,2,0:T(8,128)(2,1)} %bitcast.18), kind=kLoop, calls=%fused_computation | loop fusion | bytes 6291456 | tf_op jit(solution)/shard_map/slice | solution.py:427
  11.7 6.3 %collective-permute-done.2.other = bf16[16,64,128]{2,1,0:T(8,128)(2,1)S(1)} collective-permute-done((bf16[16,64,128]{2,1,0:T(8,128)(2,1)S(1)}, bf16[16,64,128]{2,1,0:T(8,128)(2,1)S(1)}, u32[]{:S(2)}, u32[]{:S(2)}) %collective-permute-start.2) | collective-permute-done | bytes 262176 | tf_op jit(solution)/shard_map/ppermute | solution.py:330
  18.4 2.9 %collective-permute-start.4 = (bf16[16,64,128]{2,1,0:T(8,128)(2,1)S(1)}, bf16[16,64,128]{2,1,0:T(8,128)(2,1)S(1)}, u32[]{:S(2)}, u32[]{:S(2)}) collective-permute-start(bf16[16,64,128]{2,1,0:T(8,128)(2,1)S(1)} %shard_map.70.refs_0_.own), channel_id=1, source_target_pairs={{0,8},{2,10},{4,12},{6,14},{8,0},{10,2},{12,4},{14,6},{16,24},{18,... | collective-permute-start | bytes 786440 | tf_op jit(solution)/shard_map/ppermute | solution.py:330
  22.2 4.9 %collective-permute-done.4.other = bf16[16,64,128]{2,1,0:T(8,128)(2,1)S(1)} collective-permute-done((bf16[16,64,128]{2,1,0:T(8,128)(2,1)S(1)}, bf16[16,64,128]{2,1,0:T(8,128)(2,1)S(1)}, u32[]{:S(2)}, u32[]{:S(2)}) %collective-permute-start.4) | collective-permute-done | bytes 262176 | tf_op jit(solution)/shard_map/ppermute | solution.py:330
  27.5 3.8 %collective-permute-start.6 = (bf16[16,64,128]{2,1,0:T(8,128)(2,1)S(1)}, bf16[16,64,128]{2,1,0:T(8,128)(2,1)S(1)}, u32[]{:S(2)}, u32[]{:S(2)}) collective-permute-start(bf16[16,64,128]{2,1,0:T(8,128)(2,1)S(1)} %shard_map.72.refs_0_.own), channel_id=1, source_target_pairs={{0,16},{2,18},{4,20},{6,22},{8,24},{10,26},{12,28},{14,30},{16,0},... | collective-permute-start | bytes 786440 | tf_op jit(solution)/shard_map/ppermute | solution.py:330
  36.9 4.0 %collective-permute-done.5.other = bf16[16,64,128]{2,1,0:T(8,128)(2,1)S(1)} collective-permute-done((bf16[16,64,128]{2,1,0:T(8,128)(2,1)S(1)}, bf16[16,64,128]{2,1,0:T(8,128)(2,1)S(1)}, u32[]{:S(2)}, u32[]{:S(2)}) %collective-permute-start.5) | collective-permute-done | bytes 262176 | tf_op jit(solution)/shard_map/ppermute | solution.py:330
  41.4 3.7 %collective-permute-start.7 = (bf16[16,64,128]{2,1,0:T(8,128)(2,1)S(1)}, bf16[16,64,128]{2,1,0:T(8,128)(2,1)S(1)}, u32[]{:S(2)}, u32[]{:S(2)}) collective-permute-start(bf16[16,64,128]{2,1,0:T(8,128)(2,1)S(1)} %shard_map.75.token.own), channel_id=1, source_target_pairs={{0,16},{2,18},{4,20},{6,22},{8,24},{10,26},{12,28},{14,30},{16,0},... | collective-permute-start | bytes 786440 | tf_op jit(solution)/shard_map/ppermute | solution.py:330
  47.0 3.0 %collective-permute-start.10 = (bf16[16,64,128]{2,1,0:T(8,128)(2,1)S(1)}, bf16[16,64,128]{2,1,0:T(8,128)(2,1)S(1)}, u32[]{:S(2)}, u32[]{:S(2)}) collective-permute-start(bf16[16,64,128]{2,1,0:T(8,128)(2,1)S(1)} %shard_map.77.refs_0_.own), channel_id=1, source_target_pairs={{0,64},{2,66},{4,68},{6,70},{8,72},{10,74},{12,76},{14,78},{16,80}... | collective-permute-start | bytes 786440 | tf_op jit(solution)/shard_map/ppermute | solution.py:330
  50.9 2.9 %collective-permute-done.10.other = bf16[16,64,128]{2,1,0:T(8,128)(2,1)S(1)} collective-permute-done((bf16[16,64,128]{2,1,0:T(8,128)(2,1)S(1)}, bf16[16,64,128]{2,1,0:T(8,128)(2,1)S(1)}, u32[]{:S(2)}, u32[]{:S(2)}) %collective-permute-start.10) | collective-permute-done | bytes 262176 | tf_op jit(solution)/shard_map/ppermute | solution.py:330
  55.0 4.4 %collective-permute-done.9.other = bf16[16,64,128]{2,1,0:T(8,128)(2,1)S(1)} collective-permute-done((bf16[16,64,128]{2,1,0:T(8,128)(2,1)S(1)}, bf16[16,64,128]{2,1,0:T(8,128)(2,1)S(1)}, u32[]{:S(2)}, u32[]{:S(2)}) %collective-permute-start.9) | collective-permute-done | bytes 262176 | tf_op jit(solution)/shard_map/ppermute | solution.py:330
  61.7 2.1 %shard_map.81.refs_0_ = bf16[16,64,128]{2,1,0:T(8,128)(2,1)S(1)} custom-call(bf16[16,64,128]{2,1,0:T(8,128)(2,1)S(1)} %shard_map.79.refs_0_.own, bf16[16,64,128]{2,1,0:T(8,128)(2,1)S(1)} %collective-permute-done.12.other, bf16[13,64,64,128]{3,2,1,0:T(8,128)(2,1)S(1)} %bitcast.24, bf16[16,64,128]{2,1,0:T(8,128)(2,1)S(1)} %shard_map.80.token.own), custom_call_target="tpu_custom_call" | custom-call | flops 234881024 | bytes 7340032 | tf_op jit(solution)/shard_map/pallas_call | solution.py:401
  63.8 3.0 %collective-permute-done.11.other = bf16[16,64,128]{2,1,0:T(8,128)(2,1)S(1)} collective-permute-done((bf16[16,64,128]{2,1,0:T(8,128)(2,1)S(1)}, bf16[16,64,128]{2,1,0:T(8,128)(2,1)S(1)}, u32[]{:S(2)}, u32[]{:S(2)}) %collective-permute-start.11) | collective-permute-done | bytes 262176 | tf_op jit(solution)/shard_map/ppermute | solution.py:330
  68.1 7.8 %collective-permute-start.15 = (bf16[16,64,128]{2,1,0:T(8,128)(2,1)S(1)}, bf16[16,64,128]{2,1,0:T(8,128)(2,1)S(1)}, u32[]{:S(2)}, u32[]{:S(2)}) collective-permute-start(bf16[16,64,128]{2,1,0:T(8,128)(2,1)S(1)} %shard_map.81.refs_0_), channel_id=1, source_target_pairs={{0,0},{1,2},{2,1},{3,3},{4,64},{5,66},{6,65},{7,67},{8,32},{9,34},... | collective-permute-start | bytes 786440 | tf_op jit(solution)/shard_map/ppermute | solution.py:340
  75.9 2.1 %shard_map.83.token = bf16[16,64,128]{2,1,0:T(8,128)(2,1)S(1)} custom-call(bf16[16,64,128]{2,1,0:T(8,128)(2,1)S(1)} %shard_map.82.own.token, bf16[16,64,128]{2,1,0:T(8,128)(2,1)S(1)} %collective-permute-done.13.other, bf16[13,64,64,128]{3,2,1,0:T(8,128)(2,1)S(1)} %bitcast.26, bf16[16,64,128]{2,1,0:T(8,128)(2,1)S(1)} %shard_map.82.own.token), custom_call_target="tpu_custom_call" | custom-call | flops 234881024 | bytes 7340032 | tf_op jit(solution)/shard_map/pallas_call | solution.py:401
  78.0 5.8 %collective-permute-start.14 = (bf16[16,64,128]{2,1,0:T(8,128)(2,1)S(1)}, bf16[16,64,128]{2,1,0:T(8,128)(2,1)S(1)}, u32[]{:S(2)}, u32[]{:S(2)}) collective-permute-start(bf16[16,64,128]{2,1,0:T(8,128)(2,1)S(1)} %shard_map.83.token), channel_id=1, source_target_pairs={{0,0},{1,2},{2,1},{3,3},{4,64},{5,66},{6,65},{7,67},{8,32},{9,34},... | collective-permute-start | bytes 786440 | tf_op jit(solution)/shard_map/ppermute | solution.py:340
  83.8 2.3 %shard_map.84 = (bf16[64,32,128]{2,1,0:T(8,128)(2,1)S(1)}, bf16[32,32,128]{2,1,0:T(8,128)(2,1)S(1)}) custom-call(bf16[16,64,128]{2,1,0:T(8,128)(2,1)S(1)} %collective-permute-done.15.coeffs, bf16[64,64,128]{2,1,0:T(8,128)(2,1)S(1)} %bitcast.44, bf16[64,64,128]{2,1,0:T(8,128)(2,1)S(1)} %shard_map.76.refs_0_.wanted, bf16[16,64,128]{2,1,0:T(8,128)(2,1)S(1)} %shard_map.83.token), custom_call_target="tpu_custom_call" | custom-call | flops 67108864 | bytes 4194304 | tf_op jit(solution)/shard_map/pallas_call | solution.py:364
  88.0 2.3 %shard_map.85 = (bf16[64,32,128]{2,1,0:T(8,128)(2,1)S(1)}, bf16[32,32,128]{2,1,0:T(8,128)(2,1)S(1)}) custom-call(bf16[16,64,128]{2,1,0:T(8,128)(2,1)S(1)} %collective-permute-done.14.coeffs, bf16[64,64,128]{2,1,0:T(8,128)(2,1)S(1)} %bitcast.45, bf16[64,64,128]{2,1,0:T(8,128)(2,1)S(1)} %shard_map.76.refs_0_.wanted, ...), custom_call_target="tpu_custom_call" | custom-call | flops 67108864 | bytes 4194304 | tf_op jit(solution)/shard_map/pallas_call | solution.py:364
  90.3 3.6 %collective-permute-start.17 = (bf16[32,32,128]{2,1,0:T(8,128)(2,1)S(1)}, bf16[32,32,128]{2,1,0:T(8,128)(2,1)S(1)}, u32[]{:S(2)}, u32[]{:S(2)}) collective-permute-start(bf16[32,32,128]{2,1,0:T(8,128)(2,1)S(1)} %get-tuple-element.48.token), channel_id=1, source_target_pairs={{0,0},{1,2},{2,1},{3,3},{4,64},{5,66},{6,65},{7,67},{8,32},{9,34},... | collective-permute-start | bytes 786440 | tf_op jit(solution)/shard_map/ppermute | solution.py:340
  95.8 2.1 %shard_map.87 = (f32[32,32,128]{2,1,0:T(8,128)S(1)}, bf16[32,32,128]{2,1,0:T(8,128)(2,1)S(1)}) custom-call(bf16[32,32,128]{2,1,0:T(8,128)(2,1)S(1)} %collective-permute-done.16.adjoint, bf16[13,64,64,128]{3,2,1,0:T(8,128)(2,1)S(1)} %bitcast.27, f32[8,128]{1,0:T(8,128)S(1)} %get-tuple-element.49.token), custom_call_target="tpu_custom_call" | custom-call | flops 234881024 | bytes 7340032 | tf_op jit(solution)/shard_map/pallas_call | solution.py:408
  100.2 2.2 %shard_map.89 = (f32[32,32,128]{2,1,0:T(8,128)S(1)}, bf16[32,32,128]{2,1,0:T(8,128)(2,1)S(1)}) custom-call(bf16[32,32,128]{2,1,0:T(8,128)(2,1)S(1)} %collective-permute-done.17.adjoint, bf16[13,64,64,128]{3,2,1,0:T(8,128)(2,1)S(1)} %bitcast.28, f32[8,128]{1,0:T(8,128)S(1)} %get-tuple-element.53.token), custom_call_target="tpu_custom_call" | custom-call | flops 234881024 | bytes 7340032 | tf_op jit(solution)/shard_map/pallas_call | solution.py:408
  105.7 21.8 %collective-permute-start.21 = (bf16[32,32,128]{2,1,0:T(8,128)(2,1)S(1)}, bf16[32,32,128]{2,1,0:T(8,128)(2,1)S(1)}, u32[]{:S(2)}, u32[]{:S(2)}) collective-permute-start(bf16[32,32,128]{2,1,0:T(8,128)(2,1)S(1)} %get-tuple-element.57.refs_0_), channel_id=1, source_target_pairs={{0,64},{2,66},{4,68},{6,70},{8,72},{10,74},{12,76},{14,78},{16,80}... | collective-permute-start | bytes 786440 | tf_op jit(solution)/shard_map/ppermute | solution.py:330
  128.0 3.3 %collective-permute-done.21.received = bf16[32,32,128]{2,1,0:T(8,128)(2,1)S(1)} collective-permute-done((bf16[32,32,128]{2,1,0:T(8,128)(2,1)S(1)}, bf16[32,32,128]{2,1,0:T(8,128)(2,1)S(1)}, u32[]{:S(2)}, u32[]{:S(2)}) %collective-permute-start.21) | collective-permute-done | bytes 262176 | tf_op jit(solution)/shard_map/ppermute | solution.py:330
  133.5 3.6 %collective-permute-start.20 = (bf16[32,32,128]{2,1,0:T(8,128)(2,1)S(1)}, bf16[32,32,128]{2,1,0:T(8,128)(2,1)S(1)}, u32[]{:S(2)}, u32[]{:S(2)}) collective-permute-start(bf16[32,32,128]{2,1,0:T(8,128)(2,1)S(1)} %get-tuple-element.59.refs_0_), channel_id=1, source_target_pairs={{0,64},{2,66},{4,68},{6,70},{8,72},{10,74},{12,76},{14,78},{16,80}... | collective-permute-start | bytes 786440 | tf_op jit(solution)/shard_map/ppermute | solution.py:330
  139.5 4.1 %collective-permute-done.20.received = bf16[32,32,128]{2,1,0:T(8,128)(2,1)S(1)} collective-permute-done((bf16[32,32,128]{2,1,0:T(8,128)(2,1)S(1)}, bf16[32,32,128]{2,1,0:T(8,128)(2,1)S(1)}, u32[]{:S(2)}, u32[]{:S(2)}) %collective-permute-start.20) | collective-permute-done | bytes 262176 | tf_op jit(solution)/shard_map/ppermute | solution.py:330
  146.7 3.0 %collective-permute-start.26 = (bf16[32,32,128]{2,1,0:T(8,128)(2,1)S(1)}, bf16[32,32,128]{2,1,0:T(8,128)(2,1)S(1)}, u32[]{:S(2)}, u32[]{:S(2)}) collective-permute-start(bf16[32,32,128]{2,1,0:T(8,128)(2,1)S(1)} %get-tuple-element.67.refs_0_), channel_id=1, source_target_pairs={{0,8},{2,10},{4,12},{6,14},{8,0},{10,2},{12,4},{14,6},{16,24},{18,... | collective-permute-start | bytes 786440 | tf_op jit(solution)/shard_map/ppermute | solution.py:330
  155.9 3.0 %collective-permute-done.25.received = bf16[32,32,128]{2,1,0:T(8,128)(2,1)S(1)} collective-permute-done((bf16[32,32,128]{2,1,0:T(8,128)(2,1)S(1)}, bf16[32,32,128]{2,1,0:T(8,128)(2,1)S(1)}, u32[]{:S(2)}, u32[]{:S(2)}) %collective-permute-start.25) | collective-permute-done | bytes 262176 | tf_op jit(solution)/shard_map/ppermute | solution.py:330
  159.4 3.1 %collective-permute-start.27 = (bf16[32,32,128]{2,1,0:T(8,128)(2,1)S(1)}, bf16[32,32,128]{2,1,0:T(8,128)(2,1)S(1)}, u32[]{:S(2)}, u32[]{:S(2)}) collective-permute-start(bf16[32,32,128]{2,1,0:T(8,128)(2,1)S(1)} %get-tuple-element.73.refs_0_), channel_id=1, source_target_pairs={{0,8},{2,10},{4,12},{6,14},{8,0},{10,2},{12,4},{14,6},{16,24},{18,... | collective-permute-start | bytes 786440 | tf_op jit(solution)/shard_map/ppermute | solution.py:330
  163.1 13.9 %collective-permute-start.30 = (bf16[32,32,128]{2,1,0:T(8,128)(2,1)S(1)}, bf16[32,32,128]{2,1,0:T(8,128)(2,1)S(1)}, u32[]{:S(2)}, u32[]{:S(2)}) collective-permute-start(bf16[32,32,128]{2,1,0:T(8,128)(2,1)S(1)} %get-tuple-element.75.refs_0_), channel_id=1, source_target_pairs={{0,2},{2,0},{4,6},{6,4},{8,10},{10,8},{12,14},{14,12},{16,18},{18,... | collective-permute-start | bytes 786440 | tf_op jit(solution)/shard_map/ppermute | solution.py:330
  177.5 2.1 %collective-permute-start.29 = (bf16[32,32,128]{2,1,0:T(8,128)(2,1)S(1)}, bf16[32,32,128]{2,1,0:T(8,128)(2,1)S(1)}, u32[]{:S(2)}, u32[]{:S(2)}) collective-permute-start(bf16[32,32,128]{2,1,0:T(8,128)(2,1)S(1)} %get-tuple-element.77.token), channel_id=1, source_target_pairs={{0,4},{2,6},{4,0},{6,2},{8,12},{10,14},{12,8},{14,10},{16,20},{18,... | collective-permute-start | bytes 786440 | tf_op jit(solution)/shard_map/ppermute | solution.py:330
  181.3 2.2 %collective-permute-done.29.received = bf16[32,32,128]{2,1,0:T(8,128)(2,1)S(1)} collective-permute-done((bf16[32,32,128]{2,1,0:T(8,128)(2,1)S(1)}, bf16[32,32,128]{2,1,0:T(8,128)(2,1)S(1)}, u32[]{:S(2)}, u32[]{:S(2)}) %collective-permute-start.29) | collective-permute-done | bytes 262176 | tf_op jit(solution)/shard_map/ppermute | solution.py:330
  183.9 4.6 %collective-permute-start.31 = (bf16[32,32,128]{2,1,0:T(8,128)(2,1)S(1)}, bf16[32,32,128]{2,1,0:T(8,128)(2,1)S(1)}, u32[]{:S(2)}, u32[]{:S(2)}) collective-permute-start(bf16[32,32,128]{2,1,0:T(8,128)(2,1)S(1)} %get-tuple-element.81.token), channel_id=1, source_target_pairs={{0,2},{2,0},{4,6},{6,4},{8,10},{10,8},{12,14},{14,12},{16,18},{18,... | collective-permute-start | bytes 786440 | tf_op jit(solution)/shard_map/ppermute | solution.py:330
  189.7 2.4 %shard_map.103 = (bf16[64,64,128]{2,1,0:T(8,128)(2,1)}, f32[8,128]{1,0:T(8,128)}) custom-call(f32[32,32,128]{2,1,0:T(8,128)S(1)} %get-tuple-element.80.held_part, bf16[32,32,128]{2,1,0:T(8,128)(2,1)S(1)} %collective-permute-done.31.received, bf16[64,64,128]{2,1,0:T(8,128)(2,1)S(1)} %bitcast.43, ...), custom_call_target="tpu_custom_call", output_to_operand_aliasing={{0}: (4, {})} | custom-call | flops 33554432 | bytes 2097152 | tf_op jit(solution)/shard_map/pallas_call | solution.py:379
  (81 shorter events, 52.3 us)
Async XLA Ops:
  5.5 4.1 %collective-permute-start.1 = (bf16[16,64,128]{2,1,0:T(8,128)(2,1)S(1)}, bf16[16,64,128]{2,1,0:T(8,128)(2,1)S(1)}, u32[]{:S(2)}, u32[]{:S(2)}) collective-permute-start(bf16[16,64,128]{2,1,0:T(8,128)(2,1)S(1)} %get-tuple-element.44.own.refs_0_), channel_id=1, source_target_pairs={{0,2},{2,0},{4,6},{6,4},{8,10},{10,8},{12,14},{14,12},{16,18},{18,... | collective-permute-start | bytes 786440 | tf_op jit(solution)/shard_map/ppermute | solution.py:330
  10.0 8.0 %collective-permute-start.2 = (bf16[16,64,128]{2,1,0:T(8,128)(2,1)S(1)}, bf16[16,64,128]{2,1,0:T(8,128)(2,1)S(1)}, u32[]{:S(2)}, u32[]{:S(2)}) collective-permute-start(bf16[16,64,128]{2,1,0:T(8,128)(2,1)S(1)} %shard_map.69.own.refs_0_), channel_id=1, source_target_pairs={{0,4},{2,6},{4,0},{6,2},{8,12},{10,14},{12,8},{14,10},{16,20},{18,... | collective-permute-start | bytes 786440 | tf_op jit(solution)/shard_map/ppermute | solution.py:330
  11.4 10.0 %collective-permute-start = (bf16[16,64,128]{2,1,0:T(8,128)(2,1)S(1)}, bf16[16,64,128]{2,1,0:T(8,128)(2,1)S(1)}, u32[]{:S(2)}, u32[]{:S(2)}) collective-permute-start(bf16[16,64,128]{2,1,0:T(8,128)(2,1)S(1)} %get-tuple-element.43.own), channel_id=1, source_target_pairs={{0,2},{2,0},{4,6},{6,4},{8,10},{10,8},{12,14},{14,12},{16,18},{18,... | collective-permute-start | bytes 786440 | tf_op jit(solution)/shard_map/ppermute | solution.py:330
  18.4 8.6 %collective-permute-start.4 = (bf16[16,64,128]{2,1,0:T(8,128)(2,1)S(1)}, bf16[16,64,128]{2,1,0:T(8,128)(2,1)S(1)}, u32[]{:S(2)}, u32[]{:S(2)}) collective-permute-start(bf16[16,64,128]{2,1,0:T(8,128)(2,1)S(1)} %shard_map.70.refs_0_.own), channel_id=1, source_target_pairs={{0,8},{2,10},{4,12},{6,14},{8,0},{10,2},{12,4},{14,6},{16,24},{18,... | collective-permute-start | bytes 786440 | tf_op jit(solution)/shard_map/ppermute | solution.py:330
  21.8 11.0 %collective-permute-start.3 = (bf16[16,64,128]{2,1,0:T(8,128)(2,1)S(1)}, bf16[16,64,128]{2,1,0:T(8,128)(2,1)S(1)}, u32[]{:S(2)}, u32[]{:S(2)}) collective-permute-start(bf16[16,64,128]{2,1,0:T(8,128)(2,1)S(1)} %shard_map.71.refs_0_.own), channel_id=1, source_target_pairs={{0,4},{2,6},{4,0},{6,2},{8,12},{10,14},{12,8},{14,10},{16,20},{18,... | collective-permute-start | bytes 786440 | tf_op jit(solution)/shard_map/ppermute | solution.py:330
  27.5 7.6 %collective-permute-start.6 = (bf16[16,64,128]{2,1,0:T(8,128)(2,1)S(1)}, bf16[16,64,128]{2,1,0:T(8,128)(2,1)S(1)}, u32[]{:S(2)}, u32[]{:S(2)}) collective-permute-start(bf16[16,64,128]{2,1,0:T(8,128)(2,1)S(1)} %shard_map.72.refs_0_.own), channel_id=1, source_target_pairs={{0,16},{2,18},{4,20},{6,22},{8,24},{10,26},{12,28},{14,30},{16,0},... | collective-permute-start | bytes 786440 | tf_op jit(solution)/shard_map/ppermute | solution.py:330
  33.3 7.7 %collective-permute-start.5 = (bf16[16,64,128]{2,1,0:T(8,128)(2,1)S(1)}, bf16[16,64,128]{2,1,0:T(8,128)(2,1)S(1)}, u32[]{:S(2)}, u32[]{:S(2)}) collective-permute-start(bf16[16,64,128]{2,1,0:T(8,128)(2,1)S(1)} %shard_map.73.refs_0_.own), channel_id=1, source_target_pairs={{0,8},{2,10},{4,12},{6,14},{8,0},{10,2},{12,4},{14,6},{16,24},{18,... | collective-permute-start | bytes 786440 | tf_op jit(solution)/shard_map/ppermute | solution.py:330
  35.5 11.0 %collective-permute-start.8 = (bf16[16,64,128]{2,1,0:T(8,128)(2,1)S(1)}, bf16[16,64,128]{2,1,0:T(8,128)(2,1)S(1)}, u32[]{:S(2)}, u32[]{:S(2)}) collective-permute-start(bf16[16,64,128]{2,1,0:T(8,128)(2,1)S(1)} %shard_map.74.refs_0_.own), channel_id=1, source_target_pairs={{0,32},{2,34},{4,36},{6,38},{8,40},{10,42},{12,44},{14,46},{16,48}... | collective-permute-start | bytes 786440 | tf_op jit(solution)/shard_map/ppermute | solution.py:330
  41.4 8.5 %collective-permute-start.7 = (bf16[16,64,128]{2,1,0:T(8,128)(2,1)S(1)}, bf16[16,64,128]{2,1,0:T(8,128)(2,1)S(1)}, u32[]{:S(2)}, u32[]{:S(2)}) collective-permute-start(bf16[16,64,128]{2,1,0:T(8,128)(2,1)S(1)} %shard_map.75.token.own), channel_id=1, source_target_pairs={{0,16},{2,18},{4,20},{6,22},{8,24},{10,26},{12,28},{14,30},{16,0},... | collective-permute-start | bytes 786440 | tf_op jit(solution)/shard_map/ppermute | solution.py:330
  47.0 6.8 %collective-permute-start.10 = (bf16[16,64,128]{2,1,0:T(8,128)(2,1)S(1)}, bf16[16,64,128]{2,1,0:T(8,128)(2,1)S(1)}, u32[]{:S(2)}, u32[]{:S(2)}) collective-permute-start(bf16[16,64,128]{2,1,0:T(8,128)(2,1)S(1)} %shard_map.77.refs_0_.own), channel_id=1, source_target_pairs={{0,64},{2,66},{4,68},{6,70},{8,72},{10,74},{12,76},{14,78},{16,80}... | collective-permute-start | bytes 786440 | tf_op jit(solution)/shard_map/ppermute | solution.py:330
  50.4 9.0 %collective-permute-start.9 = (bf16[16,64,128]{2,1,0:T(8,128)(2,1)S(1)}, bf16[16,64,128]{2,1,0:T(8,128)(2,1)S(1)}, u32[]{:S(2)}, u32[]{:S(2)}) collective-permute-start(bf16[16,64,128]{2,1,0:T(8,128)(2,1)S(1)} %shard_map.78.refs_0_.own), channel_id=1, source_target_pairs={{0,32},{2,34},{4,36},{6,38},{8,40},{10,42},{12,44},{14,46},{16,48}... | collective-permute-start | bytes 786440 | tf_op jit(solution)/shard_map/ppermute | solution.py:330
  54.2 7.5 %collective-permute-start.12 = (bf16[16,64,128]{2,1,0:T(8,128)(2,1)S(1)}, bf16[16,64,128]{2,1,0:T(8,128)(2,1)S(1)}, u32[]{:S(2)}, u32[]{:S(2)}) collective-permute-start(bf16[16,64,128]{2,1,0:T(8,128)(2,1)S(1)} %shard_map.79.refs_0_.own), channel_id=1, source_target_pairs={{0,1},{1,0},{2,3},{3,2},{4,5},{5,4},{6,7},{7,6},{8,9},{9,8},{10,11... | collective-permute-start | bytes 786440 | tf_op jit(solution)/shard_map/ppermute | solution.py:330
  59.9 7.0 %collective-permute-start.11 = (bf16[16,64,128]{2,1,0:T(8,128)(2,1)S(1)}, bf16[16,64,128]{2,1,0:T(8,128)(2,1)S(1)}, u32[]{:S(2)}, u32[]{:S(2)}) collective-permute-start(bf16[16,64,128]{2,1,0:T(8,128)(2,1)S(1)} %shard_map.80.token.own), channel_id=1, source_target_pairs={{0,64},{2,66},{4,68},{6,70},{8,72},{10,74},{12,76},{14,78},{16,80}... | collective-permute-start | bytes 786440 | tf_op jit(solution)/shard_map/ppermute | solution.py:330
  67.3 8.6 %collective-permute-start.13 = (bf16[16,64,128]{2,1,0:T(8,128)(2,1)S(1)}, bf16[16,64,128]{2,1,0:T(8,128)(2,1)S(1)}, u32[]{:S(2)}, u32[]{:S(2)}) collective-permute-start(bf16[16,64,128]{2,1,0:T(8,128)(2,1)S(1)} %shard_map.82.own.token), channel_id=1, source_target_pairs={{0,1},{1,0},{2,3},{3,2},{4,5},{5,4},{6,7},{7,6},{8,9},{9,8},{10,11... | collective-permute-start | bytes 786440 | tf_op jit(solution)/shard_map/ppermute | solution.py:330
  68.1 15.7 %collective-permute-start.15 = (bf16[16,64,128]{2,1,0:T(8,128)(2,1)S(1)}, bf16[16,64,128]{2,1,0:T(8,128)(2,1)S(1)}, u32[]{:S(2)}, u32[]{:S(2)}) collective-permute-start(bf16[16,64,128]{2,1,0:T(8,128)(2,1)S(1)} %shard_map.81.refs_0_), channel_id=1, source_target_pairs={{0,0},{1,2},{2,1},{3,3},{4,64},{5,66},{6,65},{7,67},{8,32},{9,34},... | collective-permute-start | bytes 786440 | tf_op jit(solution)/shard_map/ppermute | solution.py:340
  78.0 10.0 %collective-permute-start.14 = (bf16[16,64,128]{2,1,0:T(8,128)(2,1)S(1)}, bf16[16,64,128]{2,1,0:T(8,128)(2,1)S(1)}, u32[]{:S(2)}, u32[]{:S(2)}) collective-permute-start(bf16[16,64,128]{2,1,0:T(8,128)(2,1)S(1)} %shard_map.83.token), channel_id=1, source_target_pairs={{0,0},{1,2},{2,1},{3,3},{4,64},{5,66},{6,65},{7,67},{8,32},{9,34},... | collective-permute-start | bytes 786440 | tf_op jit(solution)/shard_map/ppermute | solution.py:340
  86.1 9.7 %collective-permute-start.16 = (bf16[32,32,128]{2,1,0:T(8,128)(2,1)S(1)}, bf16[32,32,128]{2,1,0:T(8,128)(2,1)S(1)}, u32[]{:S(2)}, u32[]{:S(2)}) collective-permute-start(bf16[32,32,128]{2,1,0:T(8,128)(2,1)S(1)} %get-tuple-element.45.token), channel_id=1, source_target_pairs={{0,0},{1,2},{2,1},{3,3},{4,64},{5,66},{6,65},{7,67},{8,32},{9,34},... | collective-permute-start | bytes 786440 | tf_op jit(solution)/shard_map/ppermute | solution.py:340
  90.3 9.8 %collective-permute-start.17 = (bf16[32,32,128]{2,1,0:T(8,128)(2,1)S(1)}, bf16[32,32,128]{2,1,0:T(8,128)(2,1)S(1)}, u32[]{:S(2)}, u32[]{:S(2)}) collective-permute-start(bf16[32,32,128]{2,1,0:T(8,128)(2,1)S(1)} %get-tuple-element.48.token), channel_id=1, source_target_pairs={{0,0},{1,2},{2,1},{3,3},{4,64},{5,66},{6,65},{7,67},{8,32},{9,34},... | collective-permute-start | bytes 786440 | tf_op jit(solution)/shard_map/ppermute | solution.py:340
  98.0 7.2 %collective-permute-start.19 = (bf16[32,32,128]{2,1,0:T(8,128)(2,1)S(1)}, bf16[32,32,128]{2,1,0:T(8,128)(2,1)S(1)}, u32[]{:S(2)}, u32[]{:S(2)}) collective-permute-start(bf16[32,32,128]{2,1,0:T(8,128)(2,1)S(1)} %get-tuple-element.50.token), channel_id=1, source_target_pairs={{0,1},{1,0},{2,3},{3,2},{4,5},{5,4},{6,7},{7,6},{8,9},{9,8},{10,11... | collective-permute-start | bytes 786440 | tf_op jit(solution)/shard_map/ppermute | solution.py:330
  102.3 25.2 %collective-permute-start.18 = (bf16[32,32,128]{2,1,0:T(8,128)(2,1)S(1)}, bf16[32,32,128]{2,1,0:T(8,128)(2,1)S(1)}, u32[]{:S(2)}, u32[]{:S(2)}) collective-permute-start(bf16[32,32,128]{2,1,0:T(8,128)(2,1)S(1)} %get-tuple-element.55.refs_0_), channel_id=1, source_target_pairs={{0,1},{1,0},{2,3},{3,2},{4,5},{5,4},{6,7},{7,6},{8,9},{9,8},{10,11... | collective-permute-start | bytes 786440 | tf_op jit(solution)/shard_map/ppermute | solution.py:330
  105.7 25.6 %collective-permute-start.21 = (bf16[32,32,128]{2,1,0:T(8,128)(2,1)S(1)}, bf16[32,32,128]{2,1,0:T(8,128)(2,1)S(1)}, u32[]{:S(2)}, u32[]{:S(2)}) collective-permute-start(bf16[32,32,128]{2,1,0:T(8,128)(2,1)S(1)} %get-tuple-element.57.refs_0_), channel_id=1, source_target_pairs={{0,64},{2,66},{4,68},{6,70},{8,72},{10,74},{12,76},{14,78},{16,80}... | collective-permute-start | bytes 786440 | tf_op jit(solution)/shard_map/ppermute | solution.py:330
  131.8 7.1 %collective-permute-start.22 = (bf16[32,32,128]{2,1,0:T(8,128)(2,1)S(1)}, bf16[32,32,128]{2,1,0:T(8,128)(2,1)S(1)}, u32[]{:S(2)}, u32[]{:S(2)}) collective-permute-start(bf16[32,32,128]{2,1,0:T(8,128)(2,1)S(1)} %get-tuple-element.62.refs_0_), channel_id=1, source_target_pairs={{0,32},{2,34},{4,36},{6,38},{8,40},{10,42},{12,44},{14,46},{16,48}... | collective-permute-start | bytes 786440 | tf_op jit(solution)/shard_map/ppermute | solution.py:330
  133.5 10.1 %collective-permute-start.20 = (bf16[32,32,128]{2,1,0:T(8,128)(2,1)S(1)}, bf16[32,32,128]{2,1,0:T(8,128)(2,1)S(1)}, u32[]{:S(2)}, u32[]{:S(2)}) collective-permute-start(bf16[32,32,128]{2,1,0:T(8,128)(2,1)S(1)} %get-tuple-element.59.refs_0_), channel_id=1, source_target_pairs={{0,64},{2,66},{4,68},{6,70},{8,72},{10,74},{12,76},{14,78},{16,80}... | collective-permute-start | bytes 786440 | tf_op jit(solution)/shard_map/ppermute | solution.py:330
  139.4 6.8 %collective-permute-start.24 = (bf16[32,32,128]{2,1,0:T(8,128)(2,1)S(1)}, bf16[32,32,128]{2,1,0:T(8,128)(2,1)S(1)}, u32[]{:S(2)}, u32[]{:S(2)}) collective-permute-start(bf16[32,32,128]{2,1,0:T(8,128)(2,1)S(1)} %get-tuple-element.63.refs_0_), channel_id=1, source_target_pairs={{0,16},{2,18},{4,20},{6,22},{8,24},{10,26},{12,28},{14,30},{16,0},... | collective-permute-start | bytes 786440 | tf_op jit(solution)/shard_map/ppermute | solution.py:330
  144.1 7.5 %collective-permute-start.23 = (bf16[32,32,128]{2,1,0:T(8,128)(2,1)S(1)}, bf16[32,32,128]{2,1,0:T(8,128)(2,1)S(1)}, u32[]{:S(2)}, u32[]{:S(2)}) collective-permute-start(bf16[32,32,128]{2,1,0:T(8,128)(2,1)S(1)} %get-tuple-element.65.refs_0_), channel_id=1, source_target_pairs={{0,32},{2,34},{4,36},{6,38},{8,40},{10,42},{12,44},{14,46},{16,48}... | collective-permute-start | bytes 786440 | tf_op jit(solution)/shard_map/ppermute | solution.py:330
  146.7 7.1 %collective-permute-start.26 = (bf16[32,32,128]{2,1,0:T(8,128)(2,1)S(1)}, bf16[32,32,128]{2,1,0:T(8,128)(2,1)S(1)}, u32[]{:S(2)}, u32[]{:S(2)}) collective-permute-start(bf16[32,32,128]{2,1,0:T(8,128)(2,1)S(1)} %get-tuple-element.67.refs_0_), channel_id=1, source_target_pairs={{0,8},{2,10},{4,12},{6,14},{8,0},{10,2},{12,4},{14,6},{16,24},{18,... | collective-permute-start | bytes 786440 | tf_op jit(solution)/shard_map/ppermute | solution.py:330
  152.1 6.8 %collective-permute-start.25 = (bf16[32,32,128]{2,1,0:T(8,128)(2,1)S(1)}, bf16[32,32,128]{2,1,0:T(8,128)(2,1)S(1)}, u32[]{:S(2)}, u32[]{:S(2)}) collective-permute-start(bf16[32,32,128]{2,1,0:T(8,128)(2,1)S(1)} %get-tuple-element.69.refs_0_), channel_id=1, source_target_pairs={{0,16},{2,18},{4,20},{6,22},{8,24},{10,26},{12,28},{14,30},{16,0},... | collective-permute-start | bytes 786440 | tf_op jit(solution)/shard_map/ppermute | solution.py:330
  154.3 8.2 %collective-permute-start.28 = (bf16[32,32,128]{2,1,0:T(8,128)(2,1)S(1)}, bf16[32,32,128]{2,1,0:T(8,128)(2,1)S(1)}, u32[]{:S(2)}, u32[]{:S(2)}) collective-permute-start(bf16[32,32,128]{2,1,0:T(8,128)(2,1)S(1)} %get-tuple-element.71.refs_0_), channel_id=1, source_target_pairs={{0,4},{2,6},{4,0},{6,2},{8,12},{10,14},{12,8},{14,10},{16,20},{18,... | collective-permute-start | bytes 786440 | tf_op jit(solution)/shard_map/ppermute | solution.py:330
  159.4 17.6 %collective-permute-start.27 = (bf16[32,32,128]{2,1,0:T(8,128)(2,1)S(1)}, bf16[32,32,128]{2,1,0:T(8,128)(2,1)S(1)}, u32[]{:S(2)}, u32[]{:S(2)}) collective-permute-start(bf16[32,32,128]{2,1,0:T(8,128)(2,1)S(1)} %get-tuple-element.73.refs_0_), channel_id=1, source_target_pairs={{0,8},{2,10},{4,12},{6,14},{8,0},{10,2},{12,4},{14,6},{16,24},{18,... | collective-permute-start | bytes 786440 | tf_op jit(solution)/shard_map/ppermute | solution.py:330
  163.1 16.5 %collective-permute-start.30 = (bf16[32,32,128]{2,1,0:T(8,128)(2,1)S(1)}, bf16[32,32,128]{2,1,0:T(8,128)(2,1)S(1)}, u32[]{:S(2)}, u32[]{:S(2)}) collective-permute-start(bf16[32,32,128]{2,1,0:T(8,128)(2,1)S(1)} %get-tuple-element.75.refs_0_), channel_id=1, source_target_pairs={{0,2},{2,0},{4,6},{6,4},{8,10},{10,8},{12,14},{14,12},{16,18},{18,... | collective-permute-start | bytes 786440 | tf_op jit(solution)/shard_map/ppermute | solution.py:330
  177.5 5.9 %collective-permute-start.29 = (bf16[32,32,128]{2,1,0:T(8,128)(2,1)S(1)}, bf16[32,32,128]{2,1,0:T(8,128)(2,1)S(1)}, u32[]{:S(2)}, u32[]{:S(2)}) collective-permute-start(bf16[32,32,128]{2,1,0:T(8,128)(2,1)S(1)} %get-tuple-element.77.token), channel_id=1, source_target_pairs={{0,4},{2,6},{4,0},{6,2},{8,12},{10,14},{12,8},{14,10},{16,20},{18,... | collective-permute-start | bytes 786440 | tf_op jit(solution)/shard_map/ppermute | solution.py:330
  183.9 5.8 %collective-permute-start.31 = (bf16[32,32,128]{2,1,0:T(8,128)(2,1)S(1)}, bf16[32,32,128]{2,1,0:T(8,128)(2,1)S(1)}, u32[]{:S(2)}, u32[]{:S(2)}) collective-permute-start(bf16[32,32,128]{2,1,0:T(8,128)(2,1)S(1)} %get-tuple-element.81.token), channel_id=1, source_target_pairs={{0,2},{2,0},{4,6},{6,4},{8,10},{10,8},{12,14},{14,12},{16,18},{18,... | collective-permute-start | bytes 786440 | tf_op jit(solution)/shard_map/ppermute | solution.py:330
  (6 other events, 109.9 us)
